TPU v7x, 32 devices: a whole 2x2x4 slice. The times are simulated.
32 devices in a mesh: fsdp: 2 (over y), ctx: 4 (over z), tp: 4 (over x, core).
Axes of the slice: x: 2, y: 2, z: 4, core: 2. Of those that a mesh axis runs over, the one named last changes fastest.
Arguments:
- tokens: bfloat16 [4096, 1024], P(('fsdp', 'ctx')), may hold values from -6 to 6
- cotangent: bfloat16 [4096, 1024], P(('fsdp', 'ctx')), may hold values from -6 to 6
- block_place: int32 [2, 16], P('fsdp'), may hold values from 0 to 15, each once within a row
- segment_ids: int32 [2, 2048], P('fsdp'), may hold values from -1 to 3, as said below
- qkv_weight: bfloat16 [2, 1024, 3, 1024], P(None, ('fsdp', 'ctx'), None, 'tp'), may hold values from -0.1875 to 0.1875
- out_weight: bfloat16 [2, 1024, 1024], P(None, ('fsdp', 'ctx'), 'tp'), may hold values from -0.5 to 0.5
- up_weight: bfloat16 [2, 1024, 4096], P(None, ('fsdp', 'ctx'), 'tp'), may hold values from -0.1875 to 0.1875
- down_weight: bfloat16 [2, 1024, 4096], P(None, ('fsdp', 'ctx'), 'tp'), may hold values from -0.09375 to 0.09375
- query_value_bias: bfloat16 [2, 2, 1024], P(None, None, 'tp'), may hold values from -3 to 3
- up_bias: bfloat16 [2, 4096], P(None, 'tp'), may hold values from -3 to 3
- norm_gains: bfloat16 [2, 1024, 2], P(None, ('fsdp', 'ctx')), may hold values from 0.099609375 to 1.8984375
- row_biases: bfloat16 [2, 1024, 4], P(None, ('fsdp', 'ctx')), may hold values from -3 to 3
Outputs:
- block_output: bfloat16 [4096, 1024], P(('fsdp', 'ctx'))
- grad_tokens: float32 [4096, 1024], P(('fsdp', 'ctx'))
- grad_qkv_weight: float32 [2, 1024, 3, 1024], P(None, ('fsdp', 'ctx'), None, 'tp')
- grad_out_weight: float32 [2, 1024, 1024], P(None, ('fsdp', 'ctx'), 'tp')
- grad_up_weight: float32 [2, 1024, 4096], P(None, ('fsdp', 'ctx'), 'tp')
- grad_down_weight: float32 [2, 1024, 4096], P(None, ('fsdp', 'ctx'), 'tp')
- grad_query_value_bias: float32 [2, 2, 1024], P(None, None, 'tp')
- grad_up_bias: float32 [2, 4096], P(None, 'tp')
- grad_norm_gains: float32 [2, 1024, 2], P(None, ('fsdp', 'ctx'))
- grad_row_biases: float32 [2, 1024, 4], P(None, ('fsdp', 'ctx'))
Inputs may be any that keep to these rules, and one draw needn't show every extreme that they name: `block_place`: each row is a permutation of 0 to 15. `segment_ids`: in stream order each sequence is a run of one id that begins at the start of a block and lies within one aligned group of 8 blocks; the rows after a sequence up to the end of its last block carry -1; ids of different sequences of one batch differ; every batch has a sequence of 1024 rows and three sequences in all.
All inputs are finite; a program needn't handle non-finite values.
Results may differ from a plain program's by a relative error of at most 0.013.
Values may be sent and summed in bfloat16 or wider, within the bound.
No kernel may reach another device: no remote copies, remote signals or barrier semaphores. Data moves between devices by JAX's collectives and lax.ppermute only.
A program may use at most 192 MiB of HBM per device.

v0:
```python
from functools import partial

import jax
import jax.numpy as jnp
from jax import lax
from jax.sharding import PartitionSpec as P

HEADS = 16
HD = 64
BLK = 128
LAYERS = 2


norm_eps = 1e-05
masked_score = -1000000000.0


def shortened(value):
    return jax.tree.map(lambda a: a.astype(jnp.bfloat16) if a.dtype == jnp.float32 else a, value)


def layer_norm(values, gain_vec, shift_vec):
    average = jnp.mean(values, axis=-1, keepdims=True)
    centred = values - average
    variance = jnp.mean(centred * centred, axis=-1, keepdims=True)
    return centred * lax.rsqrt(variance + norm_eps) * gain_vec + shift_vec


def score_block(queries, key_heads, query_rows, key_rows, query_segs, key_segs, slopes):
    score_scale = queries.shape[-1] ** (-0.5)
    scores = (
        jnp.einsum("qhd,khd->hqk", queries, key_heads, preferred_element_type=jnp.float32)
        * score_scale
    )
    distance = query_rows[:, None] - key_rows[None, :]
    allowed = (query_segs[:, None] == key_segs[None, :]) & (query_segs[:, None] >= 0) & (
        distance >= 0
    ) | (distance == 0)
    scores = scores - slopes[:, None, None] * distance.astype(jnp.float32)[None]
    return jnp.where(allowed[None], scores, masked_score)


def attend_forward(
    queries, key_heads, value_heads, query_rows, key_rows, query_segs, key_segs, slopes
):
    scores = score_block(queries, key_heads, query_rows, key_rows, query_segs, key_segs, slopes)
    largest = jnp.max(scores, axis=-1, keepdims=True)
    exponent = jnp.exp(scores - largest)
    softmax_total = jnp.sum(exponent, axis=-1, keepdims=True)
    softmax_low = (exponent / softmax_total).astype(jnp.bfloat16)
    output = jnp.einsum(
        "hqk,khd->qhd", softmax_low, value_heads, preferred_element_type=jnp.float32
    )
    return (output, (largest + jnp.log(softmax_total))[..., 0])


def attend_backward(
    queries,
    key_heads,
    value_heads,
    grad_heads,
    log_total,
    query_rows,
    key_rows,
    query_segs,
    key_segs,
    slopes,
):
    score_scale = queries.shape[-1] ** (-0.5)
    scores = score_block(queries, key_heads, query_rows, key_rows, query_segs, key_segs, slopes)
    softmax_out = jnp.exp(scores - log_total[..., None])
    softmax_low = softmax_out.astype(jnp.bfloat16)
    grad_soft = jnp.einsum(
        "qhd,khd->hqk", grad_heads, value_heads, preferred_element_type=jnp.float32
    )
    inner_sum = jnp.sum(softmax_out * grad_soft, axis=-1, keepdims=True)
    grad_scores = (softmax_out * (grad_soft - inner_sum)).astype(jnp.bfloat16)
    grad_query = (
        jnp.einsum("hqk,khd->qhd", grad_scores, key_heads, preferred_element_type=jnp.float32)
        * score_scale
    )
    grad_keys = (
        jnp.einsum("hqk,qhd->khd", grad_scores, queries, preferred_element_type=jnp.float32)
        * score_scale
    )
    grad_values = jnp.einsum(
        "hqk,qhd->khd", softmax_low, grad_heads, preferred_element_type=jnp.float32
    )
    return (grad_query, grad_keys, grad_values)


def on_device(
    tokens,
    cotangent,
    block_place,
    segment_ids,
    qkv_weight,
    out_weight,
    up_weight,
    down_weight,
    query_value_bias,
    up_bias,
    norm_gains,
    row_biases,
):
    row_count = tokens.shape[0]
    local_width = qkv_weight.shape[3]
    local_heads = local_width // HD
    ctx_index = lax.axis_index("ctx")
    tp_index = lax.axis_index("tp")
    block_order = block_place[0]
    stream_segs = segment_ids[0]
    offsets = jnp.arange(BLK, dtype=jnp.int32)
    key_rows = (block_order[:, None] * BLK + offsets[None, :]).reshape(-1)
    key_segs = jnp.take(stream_segs, key_rows)
    own_rows = lax.dynamic_slice_in_dim(key_rows, ctx_index * row_count, row_count)
    own_segs = lax.dynamic_slice_in_dim(key_segs, ctx_index * row_count, row_count)
    head_slopes = jnp.exp2(-8.0 * (jnp.arange(HEADS, dtype=jnp.float32) + 1.0) / HEADS)
    slopes = lax.dynamic_slice_in_dim(head_slopes, tp_index * local_heads, local_heads)
    block_size = min(row_count, 512)
    block_count = row_count // block_size

    def split_heads(source):
        return source.reshape(source.shape[0], local_heads, HD)

    def tensor_sum(partial_sum):
        return lax.psum(partial_sum, "tp")

    def input_sum(partial_sum):
        return lax.psum(partial_sum, "tp")

    def layer_pieces(layer_number):
        return (
            qkv_weight[layer_number],
            out_weight[layer_number],
            up_weight[layer_number],
            down_weight[layer_number],
            norm_gains[layer_number],
            row_biases[layer_number],
        )

    residual = tokens.astype(jnp.float32)
    records = []
    for layer_number in range(LAYERS):
        gathered = lax.all_gather(
            shortened(layer_pieces(layer_number)), ("fsdp", "ctx"), axis=0, tiled=True
        )
        qkv_full, out_full, up_full, down_full, gain_full, shift_full = gathered
        gain_values = gain_full.astype(jnp.float32)
        shift_values = shift_full.astype(jnp.float32)
        layer_input = residual
        normed = layer_norm(residual, gain_values[:, 0], shift_values[:, 0]).astype(jnp.bfloat16)
        projected = jnp.einsum("rd,dcn->rcn", normed, qkv_full, preferred_element_type=jnp.float32)
        bias_values = query_value_bias[layer_number].astype(jnp.float32)
        query_low = (projected[:, 0] + bias_values[0]).astype(jnp.bfloat16)
        key_low = projected[:, 1].astype(jnp.bfloat16)
        value_low = (projected[:, 2] + bias_values[1]).astype(jnp.bfloat16)
        keys_values = lax.all_gather(
            jnp.stack([key_low, value_low], axis=1), "ctx", axis=0, tiled=True
        )
        attention_queries = split_heads(query_low)
        attention_key_heads = split_heads(keys_values[:, 0])
        attention_value_heads = split_heads(keys_values[:, 1])

        def one_block(member):
            return attend_forward(
                member[0],
                attention_key_heads,
                attention_value_heads,
                member[1],
                key_rows,
                member[2],
                key_segs,
                slopes,
            )

        output, attention_log_total = lax.map(
            one_block,
            (
                attention_queries.reshape(block_count, block_size, local_heads, HD),
                own_rows.reshape(block_count, block_size),
                own_segs.reshape(block_count, block_size),
            ),
        )
        attended = output.reshape(row_count, local_width)
        log_total = attention_log_total
        heads_low = attended.astype(jnp.bfloat16)
        partial_branch = jnp.einsum(
            "rk,dk->rd", heads_low, out_full, preferred_element_type=jnp.float32
        )
        branch = tensor_sum(partial_branch)
        middle = residual + (branch + shift_values[:, 1])
        second_normed = layer_norm(middle, gain_values[:, 1], shift_values[:, 2]).astype(
            jnp.bfloat16
        )
        hidden = jnp.dot(second_normed, up_full, preferred_element_type=jnp.float32) + up_bias[
            layer_number
        ].astype(jnp.float32)
        activated = jax.nn.gelu(hidden, approximate=True).astype(jnp.bfloat16)
        partial_second = jnp.einsum(
            "rf,df->rd", activated, down_full, preferred_element_type=jnp.float32
        )
        second_branch = tensor_sum(partial_second)
        residual = middle + (second_branch + shift_values[:, 3])
        records.append(
            (
                gathered,
                layer_input,
                normed,
                query_low,
                keys_values,
                log_total,
                heads_low,
                middle,
                second_normed,
                hidden,
                activated,
            )
        )
    grad_state = cotangent.astype(jnp.float32)
    grad_layers = [None] * LAYERS
    bias_grads = [None] * LAYERS
    for layer_number in reversed(range(LAYERS)):
        (
            gathered,
            layer_input,
            normed,
            query_low,
            keys_values,
            log_total,
            heads_low,
            middle,
            second_normed,
            hidden,
            activated,
        ) = records[layer_number]
        gathered = lax.all_gather(
            shortened(layer_pieces(layer_number)), ("fsdp", "ctx"), axis=0, tiled=True
        )
        qkv_full, out_full, up_full, down_full, gain_full, shift_full = gathered
        gain_values = gain_full.astype(jnp.float32)
        shift_values = shift_full.astype(jnp.float32)
        down_low = grad_state.astype(jnp.bfloat16)
        grad_down = jnp.einsum("rd,rf->df", down_low, activated, preferred_element_type=jnp.float32)
        grad_act = jnp.dot(down_low, down_full, preferred_element_type=jnp.float32)
        gelu_back = jax.vjp(partial(jax.nn.gelu, approximate=True), hidden)[1]
        up_low = gelu_back(grad_act)[0].astype(jnp.bfloat16)
        grad_up = jnp.einsum("rd,rf->df", second_normed, up_low, preferred_element_type=jnp.float32)
        partial_second = jnp.einsum(
            "rf,df->rd", up_low, up_full, preferred_element_type=jnp.float32
        )
        grad_second = input_sum(partial_second)
        second_back = jax.vjp(layer_norm, middle, gain_values[:, 1], shift_values[:, 2])[1]
        grad_middle_norm, grad_gain_two, grad_shift_two = second_back(grad_second)
        grad_middle = grad_state + grad_middle_norm
        branch_low = grad_middle.astype(jnp.bfloat16)
        grad_out = jnp.einsum(
            "rd,rk->dk", branch_low, heads_low, preferred_element_type=jnp.float32
        )
        grad_heads = jnp.dot(branch_low, out_full, preferred_element_type=jnp.float32).astype(
            jnp.bfloat16
        )
        queries = split_heads(query_low)
        key_heads = split_heads(keys_values[:, 0])
        value_heads = split_heads(keys_values[:, 1])
        attention_grad_heads = split_heads(grad_heads)

        def one_step(carry, member):
            piece_query, piece_keys, piece_values = attend_backward(
                member[0],
                key_heads,
                value_heads,
                member[1],
                member[2],
                member[3],
                key_rows,
                member[4],
                key_segs,
                slopes,
            )
            return ((carry[0] + piece_keys, carry[1] + piece_values), piece_query)

        zero_grads = jnp.zeros(key_heads.shape, jnp.float32)
        (grad_keys, grad_values), grad_query = lax.scan(
            one_step,
            (zero_grads, zero_grads),
            (
                queries.reshape(block_count, block_size, local_heads, HD),
                attention_grad_heads.reshape(block_count, block_size, local_heads, HD),
                log_total,
                own_rows.reshape(block_count, block_size),
                own_segs.reshape(block_count, block_size),
            ),
        )
        grad_kv = jnp.stack(
            [grad_keys.reshape(-1, local_width), grad_values.reshape(-1, local_width)], axis=1
        )
        grad_query, grad_kv = (grad_query.reshape(row_count, local_width), grad_kv)
        own_kv = lax.psum_scatter(grad_kv, "ctx", scatter_dimension=0, tiled=True)
        grad_proj = jnp.stack([grad_query, own_kv[:, 0], own_kv[:, 1]], axis=1).astype(jnp.bfloat16)
        grad_qkv = jnp.einsum("rd,rcn->dcn", normed, grad_proj, preferred_element_type=jnp.float32)
        partial_normed = jnp.einsum(
            "rcn,dcn->rd", grad_proj, qkv_full, preferred_element_type=jnp.float32
        )
        grad_normed = input_sum(partial_normed)
        first_back = jax.vjp(layer_norm, layer_input, gain_values[:, 0], shift_values[:, 0])[1]
        grad_input_norm, grad_gain_one, grad_shift_one = first_back(grad_normed)
        grad_state = grad_middle + grad_input_norm
        column_sums = jnp.sum(grad_proj.astype(jnp.float32), axis=0)
        bias_grads[layer_number] = (
            jnp.stack([column_sums[0], column_sums[2]]),
            jnp.sum(up_low.astype(jnp.float32), axis=0),
        )
        norm_terms = (
            jnp.stack([grad_gain_one, grad_gain_two], axis=1),
            jnp.stack([grad_shift_one, grad_shift_two], axis=1),
        )
        grad_gains = norm_terms[0]
        grad_shifts = jnp.stack(
            [
                norm_terms[1][:, 0],
                jnp.sum(branch_low.astype(jnp.float32), axis=0),
                norm_terms[1][:, 1],
                jnp.sum(down_low.astype(jnp.float32), axis=0),
            ],
            axis=1,
        )
        grad_layers[layer_number] = (
            lax.psum_scatter(grad_qkv, ("fsdp", "ctx"), scatter_dimension=0, tiled=True),
            lax.psum_scatter(grad_out, ("fsdp", "ctx"), scatter_dimension=0, tiled=True),
            lax.psum_scatter(grad_up, ("fsdp", "ctx"), scatter_dimension=0, tiled=True),
            lax.psum_scatter(grad_down, ("fsdp", "ctx"), scatter_dimension=0, tiled=True),
            lax.psum_scatter(grad_gains, ("fsdp", "ctx"), scatter_dimension=0, tiled=True),
            lax.psum_scatter(grad_shifts, ("fsdp", "ctx"), scatter_dimension=0, tiled=True),
        )
    block_output = residual.astype(jnp.bfloat16)
    column_grads = jnp.stack([member[0] for member in bias_grads])
    hidden_grads = jnp.stack([member[1] for member in bias_grads])
    column_total, hidden_total = lax.psum((column_grads, hidden_grads), ("fsdp", "ctx"))
    stacked = [
        jnp.stack([grad_layers[number][position] for number in range(LAYERS)])
        for position in range(6)
    ]
    return (
        block_output,
        grad_state,
        stacked[0],
        stacked[1],
        stacked[2],
        stacked[3],
        column_total,
        hidden_total,
        stacked[4],
        stacked[5],
    )


def solution(mesh):
    placed = (
        P(("fsdp", "ctx"), None),
        P(("fsdp", "ctx"), None),
        P("fsdp", None),
        P("fsdp", None),
        P(None, ("fsdp", "ctx"), None, "tp"),
        P(None, ("fsdp", "ctx"), "tp"),
        P(None, ("fsdp", "ctx"), "tp"),
        P(None, ("fsdp", "ctx"), "tp"),
        P(None, None, "tp"),
        P(None, "tp"),
        P(None, ("fsdp", "ctx"), None),
        P(None, ("fsdp", "ctx"), None),
    )
    return jax.shard_map(
        on_device,
        mesh=mesh,
        in_specs=placed,
        out_specs=(
            P(("fsdp", "ctx"), None),
            P(("fsdp", "ctx"), None),
            P(None, ("fsdp", "ctx"), None, "tp"),
            P(None, ("fsdp", "ctx"), "tp"),
            P(None, ("fsdp", "ctx"), "tp"),
            P(None, ("fsdp", "ctx"), "tp"),
            P(None, None, "tp"),
            P(None, "tp"),
            P(None, ("fsdp", "ctx"), None),
            P(None, ("fsdp", "ctx"), None),
        ),
        check_vma=False,
    )
```

profile of v0, /device:TPU:0, one launch (start us, length us, event | category | flops | bytes accessed | tf_op | source)
XLA Modules:
  0.0 2095.8 jit_solution(17326076167432683379)
XLA Ops:
  149.4 48.1 %all-reduce.10.cloned.1.call-done = f32[512,1024]{1,0:T(8,128)} async-done(((f32[512,1024]{1,0:T(8,128)}), f32[512,1024]{1,0:T(8,128)}) %all-reduce.10.cloned.1.call-update) | async-done | bytes 2097168 | tf_op jit(solution)/shard_map/psum | solution.py:127
  199.8 49.8 %all-gather.27.cloned.1.call-done = bf16[1,1024,1024]{2,1,0:T(8,128)(2,1)} async-done(((bf16[1,128,1024]{2,1,0:T(8,128)(2,1)}), bf16[1,1024,1024]{2,1,0:T(8,128)(2,1)}) %all-gather.27.cloned.1.call-update) | async-done | bytes 2097168 | tf_op jit(solution)/shard_map/all_gather | solution.py:145
  253.9 46.3 %all-gather.29.cloned.1.call-done = bf16[1,1024,1024]{2,1,0:T(8,128)(2,1)} async-done(((bf16[1,128,1024]{2,1,0:T(8,128)(2,1)}), bf16[1,1024,1024]{2,1,0:T(8,128)(2,1)}) %all-gather.29.cloned.1.call-update) | async-done | bytes 2097168 | tf_op jit(solution)/shard_map/all_gather | solution.py:145
  358.2 45.1 %all-gather.31.cloned.1.call-done = bf16[1,1024,3,256]{1,3,2,0:T(8,128)(2,1)} async-done(((bf16[1,128,3,256]{1,3,2,0:T(8,128)(2,1)}), bf16[1,1024,3,256]{1,3,2,0:T(8,128)(2,1)}) %all-gather.31.cloned.1.call-update) | async-done | bytes 1572880 | tf_op jit(solution)/shard_map/all_gather | solution.py:145
  490.3 48.7 %all-reduce.14.cloned.1.call-done = f32[512,1024]{1,0:T(8,128)} async-done(((f32[512,1024]{1,0:T(8,128)}), f32[512,1024]{1,0:T(8,128)}) %all-reduce.14.cloned.1.call-update) | async-done | bytes 2097168 | tf_op jit(solution)/shard_map/psum | solution.py:127
  541.9 48.7 %all-gather.33.cloned.1.call-done = bf16[1,1024,1024]{2,1,0:T(8,128)(2,1)} async-done(((bf16[1,128,1024]{2,1,0:T(8,128)(2,1)}), bf16[1,1024,1024]{2,1,0:T(8,128)(2,1)}) %all-gather.33.cloned.1.call-update) | async-done | bytes 2097168 | tf_op jit(solution)/shard_map/all_gather | solution.py:145
  594.9 46.4 %all-gather.35.cloned.1.call-done = bf16[1,1024,1024]{2,1,0:T(8,128)(2,1)} async-done(((bf16[1,128,1024]{2,1,0:T(8,128)(2,1)}), bf16[1,1024,1024]{2,1,0:T(8,128)(2,1)}) %all-gather.35.cloned.1.call-update) | async-done | bytes 2097168 | tf_op jit(solution)/shard_map/all_gather | solution.py:145
  650.6 49.8 %all-reduce.16.cloned.1.call-done = f32[512,1024]{1,0:T(8,128)} async-done(((f32[512,1024]{1,0:T(8,128)}), f32[512,1024]{1,0:T(8,128)}) %all-reduce.16.cloned.1.call-update) | async-done | bytes 2097168 | tf_op jit(solution)/shard_map/psum | solution.py:130
  758.8 68.8 %reduce-scatter.23.cloned.1.call-done = f32[512,2,256]{2,0,1:T(8,128)} async-done(((f32[2048,2,256]{2,0,1:T(8,128)}), f32[512,2,256]{2,0,1:T(8,128)}) %reduce-scatter.23.cloned.1.call-update) | async-done | bytes 1048592 | tf_op jit(solution)/shard_map/reduce_scatter | solution.py:299
  833.8 51.6 %all-reduce.18.cloned.1.call-done = f32[512,1024]{1,0:T(8,128)} async-done(((f32[512,1024]{1,0:T(8,128)}), f32[512,1024]{1,0:T(8,128)}) %all-reduce.18.cloned.1.call-update) | async-done | bytes 2097168 | tf_op jit(solution)/shard_map/psum | solution.py:130
  899.9 51.6 %all-reduce.20.cloned.1.call-done = f32[512,1024]{1,0:T(8,128)} async-done(((f32[512,1024]{1,0:T(8,128)}), f32[512,1024]{1,0:T(8,128)}) %all-reduce.20.cloned.1.call-update) | async-done | bytes 2097168 | tf_op jit(solution)/shard_map/psum | solution.py:130
  1018.1 62.3 %reduce-scatter.25.cloned.1.call-done = f32[512,2,256]{2,0,1:T(8,128)} async-done(((f32[2048,2,256]{2,0,1:T(8,128)}), f32[512,2,256]{2,0,1:T(8,128)}) %reduce-scatter.25.cloned.1.call-update) | async-done | bytes 1048592 | tf_op jit(solution)/shard_map/reduce_scatter | solution.py:299
  1116.4 56.3 %all-reduce.22.cloned.1.call-done = (f32[512,1024]{1,0:T(8,128)}, f32[512,1024]{1,0:T(8,128)}) async-done(((f32[512,1024]{1,0:T(8,128)}, f32[512,1024]{1,0:T(8,128)}), (f32[512,1024]{1,0:T(8,128)}, f32[512,1024]{1,0:T(8,128)})) %all-reduce.22.cloned.1.call-update) | async-done | bytes 4194320 | tf_op jit(solution)/shard_map/psum | solution.py:127
  1188.8 49.4 %reduce-scatter.45.cloned.1.call-done = f32[128,2]{1,0:T(8,128)} async-done(((f32[1024,2]{1,0:T(8,128)}), f32[128,2]{1,0:T(8,128)}) %reduce-scatter.45.cloned.1.call-update) | async-done | bytes 1040
  1239.2 63.4 %reduce-scatter.49.cloned.1.call-done = f32[128,4]{1,0:T(8,128)} async-done(((f32[1024,4]{1,0:T(8,128)}), f32[128,4]{1,0:T(8,128)}) %reduce-scatter.49.cloned.1.call-update) | async-done | bytes 2064
  1303.5 65.8 %reduce-scatter.33.cloned.1.call-done = f32[128,256]{1,0:T(8,128)} async-done(((f32[1024,256]{1,0:T(8,128)}), f32[128,256]{1,0:T(8,128)}) %reduce-scatter.33.cloned.1.call-update) | async-done | bytes 131088 | tf_op jit(solution)/shard_map/reduce_scatter | solution.py:330
  1369.3 66.5 %reduce-scatter.31.cloned.1.call-done = f32[128,256]{1,0:T(8,128)} async-done(((f32[1024,256]{1,0:T(8,128)}), f32[128,256]{1,0:T(8,128)}) %reduce-scatter.31.cloned.1.call-update) | async-done | bytes 131088 | tf_op jit(solution)/shard_map/reduce_scatter | solution.py:330
  1437.5 89.3 %reduce-scatter.37.cloned.1.call-done = f32[128,1024]{1,0:T(8,128)} async-done(((f32[1024,1024]{1,0:T(8,128)}), f32[128,1024]{1,0:T(8,128)}) %reduce-scatter.37.cloned.1.call-update) | async-done | bytes 524304 | tf_op jit(solution)/shard_map/reduce_scatter | solution.py:331
  1526.8 91.3 %reduce-scatter.35.cloned.1.call-done = f32[128,1024]{1,0:T(8,128)} async-done(((f32[1024,1024]{1,0:T(8,128)}), f32[128,1024]{1,0:T(8,128)}) %reduce-scatter.35.cloned.1.call-update) | async-done | bytes 524304 | tf_op jit(solution)/shard_map/reduce_scatter | solution.py:331
  1620.5 89.3 %reduce-scatter.41.cloned.1.call-done = f32[128,1024]{1,0:T(8,128)} async-done(((f32[1024,1024]{1,0:T(8,128)}), f32[128,1024]{1,0:T(8,128)}) %reduce-scatter.41.cloned.1.call-update) | async-done | bytes 524304 | tf_op jit(solution)/shard_map/reduce_scatter | solution.py:332
  1709.8 91.3 %reduce-scatter.39.cloned.1.call-done = f32[128,1024]{1,0:T(8,128)} async-done(((f32[1024,1024]{1,0:T(8,128)}), f32[128,1024]{1,0:T(8,128)}) %reduce-scatter.39.cloned.1.call-update) | async-done | bytes 524304 | tf_op jit(solution)/shard_map/reduce_scatter | solution.py:332
  1867.9 62.6 %reduce-scatter.47.cloned.1.call-done = f32[128,4]{1,0:T(8,128)} async-done(((f32[1024,4]{1,0:T(8,128)}), f32[128,4]{1,0:T(8,128)}) %reduce-scatter.47.cloned.1.call-update) | async-done | bytes 2064
  1932.0 76.6 %reduce-scatter.29.cloned.1.call-done = f32[128,3,256]{2,0,1:T(8,128)} async-done(((f32[1024,3,256]{2,0,1:T(8,128)}), f32[128,3,256]{2,0,1:T(8,128)}) %reduce-scatter.29.cloned.1.call-update) | async-done | bytes 393232 | tf_op jit(solution)/shard_map/reduce_scatter | solution.py:329
  2008.6 78.3 %reduce-scatter.27.cloned.1.call-done = f32[128,3,256]{2,0,1:T(8,128)} async-done(((f32[1024,3,256]{2,0,1:T(8,128)}), f32[128,3,256]{2,0,1:T(8,128)}) %reduce-scatter.27.cloned.1.call-update) | async-done | bytes 393232 | tf_op jit(solution)/shard_map/reduce_scatter | solution.py:329
  (404 shorter events, 583.1 us)
Async XLA Ops:
  62.5 134.9 %all-reduce.10.cloned.1.call-start = ((), (), s32[]{:S(2)}) async-start(), calls=%async_computation.15 | async-start | bytes 4194304 | tf_op jit(solution)/shard_map/psum | solution.py:127
  148.0 152.2 %all-gather.29.cloned.1.call-start = ((), (), s32[]{:S(2)}) async-start(), calls=%async_computation.34 | async-start | bytes 2359296 | tf_op jit(solution)/shard_map/all_gather | solution.py:145
  148.9 206.4 %all-reduce.12.cloned.1.call-start = ((), (), s32[]{:S(2)}) async-start(), calls=%async_computation.16 | async-start | bytes 4194304 | tf_op jit(solution)/shard_map/psum | solution.py:127
  306.2 152.5 %all-gather.23.cloned.1.call-start = ((), (), s32[]{:S(2)}) async-start(), calls=%async_computation.17 | async-start | bytes 2621440 | tf_op jit(solution)/shard_map/all_gather | solution.py:158
  407.0 132.0 %all-reduce.14.cloned.1.call-start = ((), (), s32[]{:S(2)}) async-start(), calls=%async_computation.18 | async-start | bytes 4194304 | tf_op jit(solution)/shard_map/psum | solution.py:127
  489.5 151.8 %all-gather.35.cloned.1.call-start = ((), (), s32[]{:S(2)}) async-start(), calls=%async_computation.37 | async-start | bytes 2359296 | tf_op jit(solution)/shard_map/all_gather | solution.py:145
  490.2 210.2 %all-reduce.16.cloned.1.call-start = ((), (), s32[]{:S(2)}) async-start(), calls=%async_computation.19 | async-start | bytes 4194304 | tf_op jit(solution)/shard_map/psum | solution.py:130
  650.4 177.2 %reduce-scatter.23.cloned.1.call-start = ((), (), s32[]{:S(2)}) async-start(), calls=%async_computation.20 | async-start | bytes 5242880 | tf_op jit(solution)/shard_map/reduce_scatter | solution.py:299
  750.5 134.9 %all-reduce.18.cloned.1.call-start = ((), (), s32[]{:S(2)}) async-start(), calls=%async_computation.21 | async-start | bytes 4194304 | tf_op jit(solution)/shard_map/psum | solution.py:130
  833.4 118.0 %all-reduce.20.cloned.1.call-start = ((), (), s32[]{:S(2)}) async-start(), calls=%async_computation.22 | async-start | bytes 4194304 | tf_op jit(solution)/shard_map/psum | solution.py:130
  899.8 180.6 %reduce-scatter.25.cloned.1.call-start = ((), (), s32[]{:S(2)}) async-start(), calls=%async_computation.23 | async-start | bytes 5242880 | tf_op jit(solution)/shard_map/reduce_scatter | solution.py:299
  1003.4 169.3 %all-reduce.22.cloned.1.call-start = ((), (), s32[]{:S(2)}) async-start(), calls=%async_computation.42 | async-start | bytes 8388608 | tf_op jit(solution)/shard_map/psum | solution.py:127
  1086.4 151.9 %reduce-scatter.45.cloned.1.call-start = ((), (), s32[]{:S(2)}) async-start(), calls=%async_computation.39 | async-start | bytes 589824
  1087.5 215.1 %reduce-scatter.49.cloned.1.call-start = ((), (), s32[]{:S(2)}) async-start(), calls=%async_computation.41 | async-start | bytes 589824
  1088.6 280.6 %reduce-scatter.33.cloned.1.call-start = ((), (), s32[]{:S(2)}) async-start(), calls=%async_computation.27 | async-start | bytes 1179648 | tf_op jit(solution)/shard_map/reduce_scatter | solution.py:330
  1091.1 344.7 %reduce-scatter.31.cloned.1.call-start = ((), (), s32[]{:S(2)}) async-start(), calls=%async_computation.26 | async-start | bytes 1179648 | tf_op jit(solution)/shard_map/reduce_scatter | solution.py:330
  1094.2 432.6 %reduce-scatter.37.cloned.1.call-start = ((), (), s32[]{:S(2)}) async-start(), calls=%async_computation.29 | async-start | bytes 4718592 | tf_op jit(solution)/shard_map/reduce_scatter | solution.py:331
  1097.8 520.4 %reduce-scatter.35.cloned.1.call-start = ((), (), s32[]{:S(2)}) async-start(), calls=%async_computation.28 | async-start | bytes 4718592 | tf_op jit(solution)/shard_map/reduce_scatter | solution.py:331
  1104.1 605.7 %reduce-scatter.41.cloned.1.call-start = ((), (), s32[]{:S(2)}) async-start(), calls=%async_computation.31 | async-start | bytes 4718592 | tf_op jit(solution)/shard_map/reduce_scatter | solution.py:332
  1110.5 690.6 %reduce-scatter.39.cloned.1.call-start = ((), (), s32[]{:S(2)}) async-start(), calls=%async_computation.30 | async-start | bytes 4718592 | tf_op jit(solution)/shard_map/reduce_scatter | solution.py:332
  1116.2 750.3 %reduce-scatter.43.cloned.1.call-start = ((), (), s32[]{:S(2)}) async-start(), calls=%async_computation.38 | async-start | bytes 589824
  1177.1 753.4 %reduce-scatter.47.cloned.1.call-start = ((), (), s32[]{:S(2)}) async-start(), calls=%async_computation.40 | async-start | bytes 589824
  1178.3 830.4 %reduce-scatter.29.cloned.1.call-start = ((), (), s32[]{:S(2)}) async-start(), calls=%async_computation.25 | async-start | bytes 3538944 | tf_op jit(solution)/shard_map/reduce_scatter | solution.py:329
  1182.9 904.1 %reduce-scatter.27.cloned.1.call-start = ((), (), s32[]{:S(2)}) async-start(), calls=%async_computation.24 | async-start | bytes 3538944 | tf_op jit(solution)/shard_map/reduce_scatter | solution.py:329
  (93 other events, 2610.3 us)
Sparse Core Ops, SparseCore 0:
  62.6 53.7 all-gather.20
  147.2 50.1 all-reduce.9
  200.2 49.3 all-gather.26
  305.4 49.8 all-reduce.11
  407.1 51.4 all-gather.22
  489.0 49.9 all-reduce.13
  650.5 49.8 all-reduce.15
  750.6 76.8 reduce-scatter.22
  833.5 51.8 all-reduce.17
  899.9 51.4 all-reduce.19
  1003.5 76.8 reduce-scatter.24
  1086.5 86.1 all-reduce.21
  1176.2 61.9 reduce-scatter.44
  1241.6 60.8 reduce-scatter.48
  1306.8 62.4 reduce-scatter.32
  1373.2 62.5 reduce-scatter.30
  1439.9 86.9 reduce-scatter.36
  1530.4 87.6 reduce-scatter.34
  1622.1 87.6 reduce-scatter.40
  1713.4 87.6 reduce-scatter.38
  1804.6 61.7 reduce-scatter.42
  1869.6 60.8 reduce-scatter.46
  1934.6 74.0 reduce-scatter.28
  2012.7 74.2 reduce-scatter.26
  (5 shorter events, 238.0 us)
where the time goes:
time: 2110 us; the launch traced here: 2100 us
  waiting for transfers between devices  1560 us (74%)
  blocking collectives  179 us (8%)
  matrix products  175 us (8%)
  other arithmetic  101 us (5%)
  local copies, waits for them, and re-layouts  63.4 us (3%)
    all_gather x6, waiting for transfers between devices, on_device(): lax.all_gather(shortened(layer_pieces(layer_number)), ('fsdp', 'ctx'), ax...  245 us
    unnamed x33, waiting for transfers between devices  197 us
    reduce_scatter x2, waiting for transfers between devices, on_device(): lax.psum_scatter(grad_up, ('fsdp', 'ctx'), scatter_dimension=0, tiled=True)  181 us
    reduce_scatter x2, waiting for transfers between devices, on_device(): lax.psum_scatter(grad_down, ('fsdp', 'ctx'), scatter_dimension=0, tiled=T...  181 us
    psum x4, waiting for transfers between devices, tensor_sum(): return lax.psum(partial_sum, 'tp')  167 us
    reduce_scatter x2, waiting for transfers between devices, on_device(): lax.psum_scatter(grad_qkv, ('fsdp', 'ctx'), scatter_dimension=0, tiled=True)  155 us
    psum x3, waiting for transfers between devices, input_sum(): return lax.psum(partial_sum, 'tp')  153 us
    all_gather x6, blocking collectives, on_device(): lax.all_gather(shortened(layer_pieces(layer_number)), ('fsdp', 'ctx'), ax...  143 us
  transfers between devices with their start and end apart: 29, of which 29 were waited for; matrix products, arithmetic and copies ran while one was open for 6% of the time, Pallas kernels for 0%

commit v1 on v0

v1 whole, which is shorter than its diff:
```python
from functools import partial

import jax
import jax.numpy as jnp
from jax import lax
from jax.experimental import pallas as pl
from jax.experimental.pallas import tpu as pltpu
from jax.sharding import PartitionSpec as P

HEADS = 16
HD = 64
BLK = 128
RUN_BLOCKS = 8
LAYERS = 2
NORM_ROWS = 8
NORM_EPS = 1e-05
MASKED = -1000000000.0
QB = 256
GELU_A = 0.7978845608028654
GELU_B = 0.044715
BF = jnp.bfloat16
F32 = jnp.float32
NN = ((1,), (0,))
NT = ((1,), (1,))
VMEM_LIMIT = 40 * 1024 * 1024


def dot(left, right, dims=NN):
    return lax.dot_general(left, right, (dims, ((), ())), preferred_element_type=F32)


def shaped(shape, dtype):
    return jax.ShapeDtypeStruct(shape, dtype)


def whole():
    return pl.BlockSpec(memory_space=pltpu.VMEM)


def fixed(shape):
    return pl.BlockSpec(shape, lambda *ids: (0,) * len(shape))


def params(flops, bytes_accessed, transcendentals=0):
    return dict(
        compiler_params=pltpu.CompilerParams(vmem_limit_bytes=VMEM_LIMIT),
        cost_estimate=pl.CostEstimate(
            flops=int(flops), bytes_accessed=int(bytes_accessed), transcendentals=int(transcendentals)
        ),
    )


def rows_of(w_ref, depth):
    return jnp.concatenate([w_ref[z, :depth, :] for z in range(w_ref.shape[0])], axis=0)


def norm_stats(values):
    average = jnp.mean(values, axis=-1, keepdims=True)
    centred = values - average
    variance = jnp.mean(centred * centred, axis=-1, keepdims=True)
    scale = lax.rsqrt(variance + NORM_EPS)
    return centred * scale, scale


def gelu_parts(u):
    inner = GELU_A * (u + GELU_B * u * u * u)
    t = jnp.tanh(inner)
    return t


def norm_kernel(row, x_ref, table_ref, h_ref):
    n, _ = norm_stats(x_ref[...].astype(F32))
    h_ref[...] = (n * table_ref[row : row + 1, :] + table_ref[row + 2 : row + 3, :]).astype(BF)


def first_norm(x, table, row):
    rows, width = x.shape
    step = min(rows, 256)
    return pl.pallas_call(
        partial(norm_kernel, row),
        grid=(rows // step,),
        in_specs=[pl.BlockSpec((step, width), lambda i: (i, 0)), fixed(table.shape)],
        out_specs=pl.BlockSpec((step, width), lambda i: (i, 0)),
        out_shape=shaped((rows, width), BF),
        **params(rows * width * 10, rows * width * 4),
    )(x, table)


def add_norm_kernel(bias_row, gain_row, shift_row, x_ref, a_ref, b_ref, table_ref, y_ref, h_ref):
    branch = a_ref[...].astype(F32) + b_ref[...].astype(F32) + table_ref[bias_row : bias_row + 1, :]
    y = x_ref[...].astype(F32) + branch
    y_ref[...] = y
    n, _ = norm_stats(y)
    h_ref[...] = (
        n * table_ref[gain_row : gain_row + 1, :] + table_ref[shift_row : shift_row + 1, :]
    ).astype(BF)


def add_norm(x, a, b, table, bias_row, gain_row, shift_row):
    rows, width = x.shape
    step = min(rows, 128)
    spec = pl.BlockSpec((step, width), lambda i: (i, 0))
    return pl.pallas_call(
        partial(add_norm_kernel, bias_row, gain_row, shift_row),
        grid=(rows // step,),
        in_specs=[spec, spec, spec, fixed(table.shape)],
        out_specs=[spec, spec],
        out_shape=[shaped((rows, width), F32), shaped((rows, width), BF)],
        **params(rows * width * 12, rows * width * 14),
    )(x, a, b, table)


def qkv_kernel(nf, depth, *refs):
    h_refs, bias_ref, w_refs, out_ref = refs[:2], refs[2], refs[3 : 3 + nf], refs[3 + nf]
    weights = [rows_of(w, depth) for w in w_refs]
    span = weights[0].shape[0]
    heads = out_ref.shape[0]
    half = h_refs[0].shape[0]
    for number, h_ref in enumerate(h_refs):
        total = bias_ref[0]
        for y in range(nf):
            total = total + dot(h_ref[:, y * span : (y + 1) * span], weights[y])
        turned = total.astype(BF).T
        for j in range(heads):
            out_ref[j, :, number * half : (number + 1) * half] = turned[j * HD : (j + 1) * HD, :]


def qkv_project(h_own, h_oth, bias, packs, depth):
    half, width = h_own.shape
    nc, pad_depth, cols = packs[0].shape
    nf = len(packs)
    local = cols // 3
    heads = local // HD
    return pl.pallas_call(
        partial(qkv_kernel, nf, depth),
        grid=(3,),
        in_specs=[fixed((half, width))] * 2
        + [pl.BlockSpec((1, 1, local), lambda i: (i, 0, 0))]
        + [pl.BlockSpec((nc, pad_depth, local), lambda i: (0, 0, i))] * nf,
        out_specs=pl.BlockSpec((heads, HD, 2 * half), lambda i: (0, i, 0)),
        out_shape=shaped((heads, 3 * HD, 2 * half), BF),
        **params(2 * 2 * half * width * cols, width * cols * 2 + 2 * half * (width + cols) * 2),
    )(h_own, h_oth, bias, *packs)


def out_kernel(nf, depth, col, start, o_ref, *refs):
    w_refs, out_ref = refs[:nf], refs[nf]
    half = out_ref.shape[0]
    heads = o_ref.shape[0]
    o = jnp.concatenate([o_ref[j, :, start : start + half] for j in range(heads)], axis=0).T
    span = w_refs[0].shape[0] * depth
    for y in range(nf):
        out_ref[:, y * span : (y + 1) * span] = dot(o, rows_of(w_refs[y], depth), NT).astype(out_ref.dtype)


def out_project(o_rows, packs, depth, col, start, dtype):
    heads, _, rows = o_rows.shape
    half = rows // 2
    local = heads * HD
    nc = packs[0].shape[0]
    nf = len(packs)
    width = nf * nc * depth
    return pl.pallas_call(
        partial(out_kernel, nf, depth, col, start),
        grid=(1,),
        in_specs=[fixed(o_rows.shape)]
        + [pl.BlockSpec((nc, depth, local), lambda i: (0, 0, col // local))] * nf,
        out_specs=fixed((half, width)),
        out_shape=shaped((half, width), dtype),
        **params(2 * half * width * local, width * local * 2 + half * width * 4),
    )(o_rows, *packs)


def mlp_kernel(nf, depth, *refs):
    h_refs, bias_ref = refs[:2], refs[2]
    up_refs, down_refs = refs[3 : 3 + nf], refs[3 + nf : 3 + 2 * nf]
    u_ref, oth_ref, own_ref, acc_ref = refs[3 + 2 * nf :]
    step = pl.program_id(0)
    half = h_refs[0].shape[0]
    ups = [rows_of(w, depth) for w in up_refs]
    downs = [rows_of(w, depth) for w in down_refs]
    span = ups[0].shape[0]
    for number in range(2):
        rows = slice(number * half, (number + 1) * half)
        u = bias_ref[...]
        for y in range(nf):
            u = u + dot(h_refs[number][:, y * span : (y + 1) * span], ups[y])
        u_ref[rows, :] = u
        act = (0.5 * u * (1.0 + gelu_parts(u))).astype(BF)
        for y in range(nf):
            piece = dot(act, downs[y], NT)
            cols = slice(y * span, (y + 1) * span)

            @pl.when(step == 0)
            def _():
                acc_ref[rows, cols] = piece

            @pl.when(step > 0)
            def _():
                acc_ref[rows, cols] += piece

    @pl.when(step == pl.num_programs(0) - 1)
    def _():
        own_ref[...] = acc_ref[:half, :]
        oth_ref[...] = acc_ref[half:, :].astype(BF)


def mlp_forward(h_own, h_oth, bias, ups, up_col, downs, down_col, depth, hidden):
    half, width = h_own.shape
    nc = ups[0].shape[0]
    nf = len(ups)
    tile = min(hidden, 256)

    def weight_spec(w, col):
        return pl.BlockSpec((nc, w.shape[1], tile), lambda i: (0, 0, col // tile + i))

    return pl.pallas_call(
        partial(mlp_kernel, nf, depth),
        grid=(hidden // tile,),
        in_specs=[fixed((half, width))] * 2
        + [pl.BlockSpec((1, tile), lambda i: (0, i))]
        + [weight_spec(w, up_col) for w in ups]
        + [weight_spec(w, down_col) for w in downs],
        out_specs=[
            pl.BlockSpec((2 * half, tile), lambda i: (0, i)),
            fixed((half, width)),
            fixed((half, width)),
        ],
        out_shape=[
            shaped((2 * half, hidden), F32),
            shaped((half, width), BF),
            shaped((half, width), F32),
        ],
        scratch_shapes=[pltpu.VMEM((2 * half, width), F32)],
        **params(8 * half * width * hidden, 4 * width * hidden + 8 * half * hidden, 2 * half * hidden),
    )(h_own, h_oth, bias, *ups, *downs)


def mlp_back_kernel(nf, depth, *refs):
    g_refs, u_ref = refs[:2], refs[2]
    up_refs, down_refs = refs[3 : 3 + nf], refs[3 + nf : 3 + 2 * nf]
    act_ref, gu_ref, sum_ref, oth_ref, own_ref, acc_ref = refs[3 + 2 * nf :]
    step = pl.program_id(0)
    half = g_refs[0].shape[0]
    ups = [rows_of(w, depth) for w in up_refs]
    downs = [rows_of(w, depth) for w in down_refs]
    span = ups[0].shape[0]
    column = 0.0
    for number in range(2):
        rows = slice(number * half, (number + 1) * half)
        grad = 0.0
        for y in range(nf):
            grad = grad + dot(g_refs[number][:, y * span : (y + 1) * span], downs[y])
        u = u_ref[rows, :]
        t = gelu_parts(u)
        act_ref[rows, :] = (0.5 * u * (1.0 + t)).astype(BF)
        slope = 0.5 * (1.0 + t) + 0.5 * u * (1.0 - t * t) * (GELU_A * (1.0 + 3.0 * GELU_B * u * u))
        gu = (grad * slope).astype(BF)
        gu_ref[rows, :] = gu
        column = column + jnp.sum(gu.astype(F32), axis=0, keepdims=True)
        for y in range(nf):
            piece = dot(gu, ups[y], NT)
            cols = slice(y * span, (y + 1) * span)

            @pl.when(step == 0)
            def _():
                acc_ref[rows, cols] = piece

            @pl.when(step > 0)
            def _():
                acc_ref[rows, cols] += piece

    sum_ref[...] = column

    @pl.when(step == pl.num_programs(0) - 1)
    def _():
        own_ref[...] = acc_ref[:half, :]
        oth_ref[...] = acc_ref[half:, :].astype(BF)


def mlp_backward(g_own, g_oth, u, ups, up_col, downs, down_col, depth):
    half, width = g_own.shape
    hidden = u.shape[1]
    nc = ups[0].shape[0]
    nf = len(ups)
    tile = min(hidden, 256)

    def weight_spec(w, col):
        return pl.BlockSpec((nc, w.shape[1], tile), lambda i: (0, 0, col // tile + i))

    rows_spec = pl.BlockSpec((2 * half, tile), lambda i: (0, i))
    return pl.pallas_call(
        partial(mlp_back_kernel, nf, depth),
        grid=(hidden // tile,),
        in_specs=[fixed((half, width))] * 2
        + [rows_spec]
        + [weight_spec(w, up_col) for w in ups]
        + [weight_spec(w, down_col) for w in downs],
        out_specs=[
            rows_spec,
            rows_spec,
            pl.BlockSpec((1, tile), lambda i: (0, i)),
            fixed((half, width)),
            fixed((half, width)),
        ],
        out_shape=[
            shaped((2 * half, hidden), BF),
            shaped((2 * half, hidden), BF),
            shaped((1, hidden), F32),
            shaped((half, width), BF),
            shaped((half, width), F32),
        ],
        scratch_shapes=[pltpu.VMEM((2 * half, width), F32)],
        **params(8 * half * width * hidden, 4 * width * hidden + 16 * half * hidden, 2 * half * hidden),
    )(g_own, g_oth, u, *ups, *downs)


def weight_grad_kernel(nf, *refs):
    l_own, l_oth, r_ref = refs[:3]
    out_refs, turned_ref = refs[3 : 3 + nf], refs[3 + nf]
    half = l_own.shape[0]

    @pl.when(pl.program_id(0) == 0)
    def _():
        turned_ref[:, :half] = l_own[...].T
        turned_ref[:, half:] = l_oth[...].T

    right = r_ref[...]
    span = out_refs[0].shape[0]
    for y in range(nf):
        out_refs[y][...] = dot(turned_ref[y * span : (y + 1) * span, :], right).astype(BF)


def weight_grad(l_own, l_oth, right, nf):
    half, width = l_own.shape
    cols = right.shape[1]
    tile = min(cols, 256)
    return pl.pallas_call(
        partial(weight_grad_kernel, nf),
        grid=(cols // tile,),
        in_specs=[fixed((half, width))] * 2 + [pl.BlockSpec((2 * half, tile), lambda i: (0, i))],
        out_specs=[pl.BlockSpec((width // nf, tile), lambda i: (0, i))] * nf,
        out_shape=[shaped((width // nf, cols), BF)] * nf,
        scratch_shapes=[pltpu.VMEM((width, 2 * half), BF)],
        **params(4 * half * width * cols, 2 * width * cols + 4 * half * (width + cols)),
    )(l_own, l_oth, right)


def out_grad_kernel(nf, *refs):
    l_own, l_oth, o_ref = refs[:3]
    out_refs = refs[3:]
    half = l_own.shape[0]
    heads = o_ref.shape[0]
    turned = jnp.concatenate([o_ref[j] for j in range(heads)], axis=0)
    span = out_refs[0].shape[0]
    for y in range(nf):
        cols = slice(y * span, (y + 1) * span)
        total = dot(turned[:, :half], l_own[:, cols]) + dot(turned[:, half:], l_oth[:, cols])
        out_refs[y][...] = total.astype(BF).T


def out_grad(l_own, l_oth, o_rows, nf):
    half, width = l_own.shape
    local = o_rows.shape[0] * HD
    return pl.pallas_call(
        partial(out_grad_kernel, nf),
        in_specs=[whole()] * 3,
        out_specs=[whole()] * nf,
        out_shape=[shaped((width // nf, local), BF)] * nf,
        **params(4 * half * width * local, 2 * width * local + 4 * half * (width + local)),
    )(l_own, l_oth, o_rows)


def norm_back_kernel(gain_row, gx_ref, a_ref, b_ref, y_ref, table_ref, gy_ref, low_ref, sums_ref):
    step = pl.program_id(0)
    grad = a_ref[...].astype(F32) + b_ref[...].astype(F32)
    n, scale = norm_stats(y_ref[...].astype(F32))
    e = grad * table_ref[gain_row : gain_row + 1, :]
    mean_e = jnp.mean(e, axis=-1, keepdims=True)
    mean_en = jnp.mean(e * n, axis=-1, keepdims=True)
    gy = gx_ref[...].astype(F32) + scale * (e - mean_e - n * mean_en)
    gy_ref[...] = gy
    low = gy.astype(BF)
    low_ref[...] = low
    sums = [
        jnp.sum(grad * n, axis=0, keepdims=True),
        jnp.sum(grad, axis=0, keepdims=True),
        jnp.sum(low.astype(F32), axis=0, keepdims=True),
        jnp.sum(gx_ref[...].astype(BF).astype(F32), axis=0, keepdims=True),
    ]
    packed = jnp.concatenate(sums + [jnp.zeros((4, sums[0].shape[1]), F32)], axis=0)

    @pl.when(step == 0)
    def _():
        sums_ref[...] = packed

    @pl.when(step > 0)
    def _():
        sums_ref[...] += packed


def norm_backward(gx, a, b, y, table, gain_row):
    rows, width = gx.shape
    step = min(rows, 128)
    spec = pl.BlockSpec((step, width), lambda i: (i, 0))
    return pl.pallas_call(
        partial(norm_back_kernel, gain_row),
        grid=(rows // step,),
        in_specs=[spec] * 4 + [fixed(table.shape)],
        out_specs=[spec, spec, fixed((8, width))],
        out_shape=[shaped((rows, width), F32), shaped((rows, width), BF), shaped((8, width), F32)],
        **params(rows * width * 25, rows * width * 18),
    )(gx, a, b, y, table)


def out_back_kernel(nf, depth, *refs):
    g_refs, w_refs, out_ref = refs[:2], refs[2 : 2 + nf], refs[2 + nf]
    half = g_refs[0].shape[0]
    heads = out_ref.shape[0]
    weights = [rows_of(w, depth) for w in w_refs]
    span = weights[0].shape[0]
    for number, g_ref in enumerate(g_refs):
        total = 0.0
        for y in range(nf):
            total = total + dot(g_ref[:, y * span : (y + 1) * span], weights[y])
        turned = total.astype(BF).T
        for j in range(heads):
            out_ref[j, :, number * half : (number + 1) * half] = turned[j * HD : (j + 1) * HD, :]


def out_backward(g_own, g_oth, packs, col, depth, local):
    half, width = g_own.shape
    nc = packs[0].shape[0]
    nf = len(packs)
    return pl.pallas_call(
        partial(out_back_kernel, nf, depth),
        grid=(1,),
        in_specs=[fixed((half, width))] * 2
        + [pl.BlockSpec((nc, depth, local), lambda i: (0, 0, col // local))] * nf,
        out_specs=fixed((local // HD, HD, 2 * half)),
        out_shape=shaped((local // HD, HD, 2 * half), BF),
        **params(4 * half * width * local, 2 * width * local + 4 * half * (width + local)),
    )(g_own, g_oth, *packs)


def qkv_back_kernel(nf, depth, *refs):
    g_ref, w_refs = refs[0], refs[1 : 1 + nf]
    rows_ref, sum_ref, oth_ref, own_ref = refs[1 + nf :]
    heads = g_ref.shape[0]
    half = own_ref.shape[0]
    weights = [rows_of(w, depth) for w in w_refs]
    span = weights[0].shape[0]
    local = heads * HD
    planes = [
        jnp.concatenate([g_ref[j, i * HD : (i + 1) * HD, :] for j in range(heads)], axis=0).T
        for i in range(3)
    ]
    grads = jnp.concatenate(planes, axis=1)
    rows_ref[...] = grads
    for y in range(nf):
        cols = slice(y * span, (y + 1) * span)
        oth_ref[:, cols] = dot(grads[half:, :], weights[y], NT).astype(BF)
        own_ref[:, cols] = dot(grads[:half, :], weights[y], NT)
    sum_ref[...] = jnp.sum(grads.astype(F32), axis=0, keepdims=True)


def qkv_backward(g, packs, depth):
    heads, _, rows = g.shape
    half = rows // 2
    cols = 3 * heads * HD
    nc, pad_depth = packs[0].shape[:2]
    nf = len(packs)
    width = nf * nc * depth
    return pl.pallas_call(
        partial(qkv_back_kernel, nf, depth),
        grid=(1,),
        in_specs=[fixed(g.shape)] + [fixed((nc, pad_depth, cols))] * nf,
        out_specs=[fixed((rows, cols)), fixed((1, cols)), fixed((half, width)), fixed((half, width))],
        out_shape=[
            shaped((rows, cols), BF),
            shaped((1, cols), F32),
            shaped((half, width), BF),
            shaped((half, width), F32),
        ],
        **params(2 * rows * width * cols, 2 * width * cols + 4 * rows * cols + 3 * rows * width),
    )(g, *packs)


def gather_blocks(source_ref, src_ref, dest_ref, per_device):
    for s in range(dest_ref.shape[1] // BLK):
        src = src_ref[s]
        z = src // per_device
        start = pl.multiple_of((src - z * per_device) * BLK, BLK)
        dest_ref[:, s * BLK : (s + 1) * BLK] = source_ref[z, :, pl.ds(start, BLK)]


def scatter_blocks(dest_ref, src_ref, source, per_device, low, first):
    depth, columns = source.shape
    for s in range(columns // BLK):
        src = src_ref[first + s]
        z = src // per_device
        start = pl.multiple_of((src - z * per_device) * BLK, BLK)
        dest_ref[z, low : low + depth, pl.ds(start, BLK)] = source[:, s * BLK : (s + 1) * BLK]


def segment_columns(seg_ref, column_ref):
    for s in range(seg_ref.shape[1] // BLK):
        row = seg_ref[:, s * BLK : (s + 1) * BLK]
        row = jnp.where(row < 0, -2, row).astype(F32)
        column_ref[s * BLK : (s + 1) * BLK, :] = jnp.broadcast_to(row, (BLK, BLK)).T


def score_tile(keys, queries, column_ref, seg_ref, slope, base, first, last):
    depth = keys.shape[0]
    width = last - first
    scores = dot(keys, queries)
    key_row = lax.broadcasted_iota(jnp.int32, (depth, width), 0)
    query_row = lax.broadcasted_iota(jnp.int32, (depth, width), 1) + (first - base)
    distance = query_row - key_row
    scores = scores - slope * distance.astype(F32)
    columns = column_ref[base : base + depth, :]
    key_seg = jnp.concatenate([columns] * (width // BLK), axis=1)
    query_seg = seg_ref[:, first:last].astype(F32)
    allowed = ((key_seg == query_seg) & (distance >= 0)) | (distance == 0)
    return scores, allowed


def attend_kernel(per_device, src_ref, slope_ref, seg_ref, qkv_ref, o_ref, lse_ref, stream_ref, column_ref):
    gather_blocks(qkv_ref, src_ref, stream_ref, per_device)
    segment_columns(seg_ref, column_ref)
    slope = slope_ref[0]
    run = RUN_BLOCKS * BLK
    for base in range(0, stream_ref.shape[1], run):
        keys = stream_ref[HD : 2 * HD, base : base + run].T
        for first in range(base, base + run, QB):
            last = first + QB
            depth = last - base
            queries = stream_ref[:HD, first:last] * jnp.asarray(HD**-0.5, BF)
            scores, allowed = score_tile(
                keys[:depth], queries, column_ref, seg_ref, slope, base, first, last
            )
            scores = jnp.where(allowed, scores, MASKED)
            top = jnp.max(scores, axis=0, keepdims=True)
            weights = jnp.exp(scores - top)
            total = jnp.sum(weights, axis=0, keepdims=True)
            lse_ref[:, first:last] = top + jnp.log(total)
            values = stream_ref[2 * HD :, base : base + depth]
            out = (dot(values, weights.astype(BF)) / total).astype(BF)
            scatter_blocks(o_ref, src_ref, out, per_device, 0, first // BLK)


def attend(qkv, source, slope, segments):
    nc, depth, rows = qkv.shape
    length = nc * rows
    smem = pl.BlockSpec(memory_space=pltpu.SMEM)
    return pl.pallas_call(
        partial(attend_kernel, rows // BLK),
        in_specs=[smem, smem, whole(), whole()],
        out_specs=[whole(), whole()],
        out_shape=[shaped((nc, HD, rows), BF), shaped((1, length), F32)],
        scratch_shapes=[pltpu.VMEM((3 * HD, length), BF), pltpu.VMEM((length, BLK), F32)],
        **params(length * RUN_BLOCKS * BLK * HD * 3, length * HD * 8, length * RUN_BLOCKS * BLK // 2),
    )(source, slope, segments, qkv)


def attend_back_kernel(
    per_device, src_ref, slope_ref, seg_ref, qkv_ref, g_ref, lse_ref, out_ref, stream_ref, grad_ref, column_ref, k_acc, v_acc
):
    gather_blocks(qkv_ref, src_ref, stream_ref, per_device)
    gather_blocks(g_ref, src_ref, grad_ref, per_device)
    segment_columns(seg_ref, column_ref)
    slope = slope_ref[0]
    run = RUN_BLOCKS * BLK
    scale = HD**-0.5
    for base in range(0, stream_ref.shape[1], run):
        rows = slice(base, base + run)
        keys_turned = stream_ref[HD : 2 * HD, rows]
        keys = keys_turned.T
        values = stream_ref[2 * HD :, rows].T
        queries_rows = stream_ref[:HD, rows].T
        grads_rows = grad_ref[:, rows].T
        for first in range(base + run - QB, base - 1, -QB):
            last = first + QB
            depth = last - base
            inner = slice(first - base, last - base)
            queries = stream_ref[:HD, first:last] * jnp.asarray(scale, BF)
            scores, allowed = score_tile(
                keys[:depth], queries, column_ref, seg_ref, slope, base, first, last
            )
            weights = jnp.where(allowed, jnp.exp(scores - lse_ref[:, first:last]), 0.0)
            back = dot(values[:depth], grad_ref[:, first:last])
            delta = jnp.sum(weights * back, axis=0, keepdims=True)
            low = (weights * (back - delta)).astype(BF)
            v_piece = dot(weights.astype(BF), grads_rows[inner])
            k_piece = dot(low, queries_rows[inner])
            if depth == run:
                v_acc[...] = v_piece
                k_acc[...] = k_piece
            else:
                v_acc[:depth, :] += v_piece
                k_acc[:depth, :] += k_piece
            q_grad = (dot(keys_turned[:, :depth], low) * scale).astype(BF)
            scatter_blocks(out_ref, src_ref, q_grad, per_device, 0, first // BLK)
        scatter_blocks(out_ref, src_ref, (k_acc[...] * scale).T.astype(BF), per_device, HD, base // BLK)
        scatter_blocks(out_ref, src_ref, v_acc[...].T.astype(BF), per_device, 2 * HD, base // BLK)


def attend_backward(qkv, grads, lse, source, slope, segments):
    nc, depth, rows = qkv.shape
    length = nc * rows
    run = RUN_BLOCKS * BLK
    smem = pl.BlockSpec(memory_space=pltpu.SMEM)
    return pl.pallas_call(
        partial(attend_back_kernel, rows // BLK),
        in_specs=[smem, smem, whole(), whole(), whole(), whole()],
        out_specs=whole(),
        out_shape=shaped((nc, depth, rows), BF),
        scratch_shapes=[
            pltpu.VMEM((3 * HD, length), BF),
            pltpu.VMEM((HD, length), BF),
            pltpu.VMEM((length, BLK), F32),
            pltpu.VMEM((run, HD), F32),
            pltpu.VMEM((run, HD), F32),
        ],
        **params(length * run * HD * 7, length * HD * 16, length * run // 2),
    )(source, slope, segments, qkv, grads, lse)


def on_device(
    nf,
    nc,
    nt,
    tokens,
    cotangent,
    block_place,
    segment_ids,
    qkv_weight,
    out_weight,
    up_weight,
    down_weight,
    query_value_bias,
    up_bias,
    norm_gains,
    row_biases,
):
    rows, width = tokens.shape
    half = rows // 2
    depth = qkv_weight.shape[1]
    local = qkv_weight.shape[3]
    heads = local // HD
    hidden = up_weight.shape[2]
    span = nc * depth
    y_index = lax.axis_index("fsdp")
    z_index = lax.axis_index("ctx")
    t_index = lax.axis_index("tp")
    side = t_index % 2

    def swap(value, axis, size, bit):
        return lax.ppermute(value, axis, [(i, i ^ bit) for i in range(size)])

    def sibling(value):
        return swap(value, "tp", nt, 1)

    def across(value):
        return lax.all_to_all(value, "ctx", 0, 0)

    def gather(shard):
        mine = across(jnp.broadcast_to(shard[None], (nc,) + shard.shape))
        return [mine] + [swap(mine, "fsdp", nf, bit) for bit in range(1, nf)]

    def reduce_rows(parts):
        total = parts[0].astype(F32)
        for bit in range(1, nf):
            total = total + swap(parts[bit], "fsdp", nf, bit).astype(F32)
        pieces = across(total.astype(parts[0].dtype).reshape((nc, -1) + total.shape[1:]))
        return jnp.sum(pieces.astype(F32), axis=0)

    def tensor_sum(other, own):
        term = (own + sibling(other).astype(F32)).astype(BF)
        bit = 2
        while bit * 2 < nt:
            term = (term.astype(F32) + swap(term, "tp", nt, bit).astype(F32)).astype(BF)
            bit *= 2
        return term, swap(term, "tp", nt, bit)

    def columns_relative(value):
        return jnp.concatenate(
            [
                lax.dynamic_slice_in_dim(value, (y_index ^ bit) * span, span, axis=1)
                for bit in range(nf)
            ],
            axis=1,
        )

    def take_half(value, which):
        return lax.dynamic_slice_in_dim(value, which * half, half)

    def columns_canonical(own, oth):
        rows_all = jnp.where(
            side == 0, jnp.concatenate([own, oth], axis=0), jnp.concatenate([oth, own], axis=0)
        )
        return columns_relative(rows_all)

    per_device = rows // BLK
    count = nc * per_device
    place = block_place[0]
    stored = jnp.arange(count, dtype=jnp.int32)
    relative = (stored // per_device) * per_device + (stored % per_device + side * (per_device // 2)) % per_device
    source = jnp.sum(
        jnp.where(place[None, :] == jnp.arange(count, dtype=jnp.int32)[:, None], relative[None, :], 0), axis=1
    ).astype(jnp.int32)
    head = (t_index * heads + z_index).astype(F32)
    slope = jnp.exp2(-8.0 * (head + 1.0) / HEADS).reshape(1)
    segments = segment_ids

    def qkv_shard(layer):
        return jnp.concatenate([qkv_weight[layer, :, i, :] for i in range(3)], axis=1)

    table_rows = []
    for layer in range(LAYERS):
        table_rows += [norm_gains[layer].T, row_biases[layer].T, jnp.zeros((2, depth), BF)]
    table_shard = jnp.concatenate(table_rows, axis=0)
    extra = table_shard.shape[0]
    table_padded = jnp.pad(table_shard, ((0, 0), (0, 3 * local - depth)))
    first_packs = gather(jnp.concatenate([qkv_shard(0), table_padded], axis=0))
    table = jnp.concatenate(
        [
            jnp.transpose(part[:, depth:, :depth], (1, 0, 2)).reshape(extra, span)
            for part in first_packs
        ],
        axis=1,
    ).astype(F32)
    out_up = [gather(jnp.concatenate([out_weight[0], up_weight[0]], axis=1)), None]
    down = [gather(down_weight[0]), None]
    qkv_out_1 = gather(jnp.concatenate([out_weight[1], qkv_shard(1)], axis=1))
    up_down_1 = gather(jnp.concatenate([up_weight[1], down_weight[1]], axis=1))

    biases = [
        jnp.stack([query_value_bias[l, 0], jnp.zeros((local,), BF), query_value_bias[l, 1]])
        .astype(F32)
        .reshape(3, 1, local)
        for l in range(LAYERS)
    ]
    up_biases = [up_bias[l].astype(F32).reshape(1, hidden) for l in range(LAYERS)]

    qkv_1 = [part[:, :, local:] for part in qkv_out_1]
    qkv_packs = [first_packs, qkv_1]
    out_packs = [(out_up[0], 0), (qkv_out_1, 0)]
    up_packs = [([p[:, :, local:] for p in out_up[0]], 0), (up_down_1, 0)]
    down_packs = [(down[0], 0), (up_down_1, hidden)]

    x_all = columns_relative(tokens)
    x_half = take_half(x_all, side)
    h_own = first_norm(x_half, table, 0)
    h_oth = first_norm(take_half(x_all, 1 - side), table, 0)
    records = []
    for l in range(LAYERS):
        row = l * NORM_ROWS
        qkv = across(qkv_project(h_own, h_oth, biases[l], qkv_packs[l], depth))
        o_stream, lse = attend(qkv, source, slope, segments)
        o_rows = across(o_stream)
        packs, col = out_packs[l]
        other = out_project(o_rows, packs, depth, col, half, BF)
        own = out_project(o_rows, packs, depth, col, 0, F32)
        a, b = tensor_sum(other, own)
        y_half, h2_own = add_norm(x_half, a, b, table, row + 3, row + 1, row + 4)
        h2_oth = sibling(h2_own)
        u, other, own = mlp_forward(
            h2_own, h2_oth, up_biases[l], *up_packs[l], *down_packs[l], depth, hidden
        )
        a, b = tensor_sum(other, own)
        following = row + NORM_ROWS if l + 1 < LAYERS else row
        records.append((x_half, h_own, h_oth, qkv, lse, o_rows, y_half, h2_own, h2_oth, u))
        x_half, h_own = add_norm(y_half, a, b, table, row + 5, following, following + 2)
        if l + 1 < LAYERS:
            h_oth = sibling(h_own)
    final_low = x_half.astype(BF)
    block_output = columns_canonical(final_low, sibling(final_low))

    g_all = columns_relative(cotangent)
    gz_own, gz_oth = take_half(g_all, side), take_half(g_all, 1 - side)
    gx_half = gz_own.astype(F32)
    grads = [None] * LAYERS
    sums = [None] * LAYERS
    for l in reversed(range(LAYERS)):
        row = l * NORM_ROWS
        x_half, h_own, h_oth, qkv, lse, o_rows, y_half, h2_own, h2_oth, u = records[l]
        act, gu, up_sum, other, own = mlp_backward(
            gz_own, gz_oth, u, *up_packs[l], *down_packs[l], depth
        )
        a, b = tensor_sum(other, own)
        grad_down = reduce_rows(weight_grad(gz_own, gz_oth, act, nf))
        grad_up = reduce_rows(weight_grad(h2_own, h2_oth, gu, nf))
        gy_half, ga_own, sums_two = norm_backward(gx_half, a, b, y_half, table, row + 1)
        ga_oth = sibling(ga_own)
        packs, col = out_packs[l]
        g_stream = across(out_backward(ga_own, ga_oth, packs, col, depth, local))
        grad_out = reduce_rows(out_grad(ga_own, ga_oth, o_rows, nf))
        g_rows = across(attend_backward(qkv, g_stream, lse, source, slope, segments))
        g_proj, qkv_sum, other, own = qkv_backward(g_rows, qkv_packs[l], depth)
        a, b = tensor_sum(other, own)
        grad_qkv = reduce_rows(weight_grad(h_own, h_oth, g_proj, nf))
        gx_half, gz_own, sums_one = norm_backward(gy_half, a, b, x_half, table, row)
        if l > 0:
            gz_oth = sibling(gz_own)
        grads[l] = (grad_qkv, grad_out, grad_up, grad_down)
        sums[l] = (sums_one, sums_two, qkv_sum, up_sum)

    grad_tokens = columns_canonical(gx_half, sibling(gx_half))

    norm_parts = []
    for l in range(LAYERS):
        one, two = sums[l][0], sums[l][1]
        norm_parts += [one[0], two[0], one[1], two[2], two[1], two[3]]
    norm_all = jnp.stack(norm_parts)
    bias_all = jnp.concatenate(
        [sums[l][2][0, :local] for l in range(LAYERS)]
        + [sums[l][2][0, 2 * local :] for l in range(LAYERS)]
        + [sums[l][3][0] for l in range(LAYERS)]
    )
    count_norm = norm_all.shape[0]
    by_part = norm_all.reshape(count_norm, nf, nc, depth).transpose(1, 2, 3, 0).reshape(nf, -1)
    norm_total = by_part[0]
    bias_total = bias_all
    for bit in range(1, nf):
        came = swap(jnp.concatenate([by_part[bit], bias_all]), "fsdp", nf, bit)
        norm_total = norm_total + came[: norm_total.size]
        bias_total = bias_total + came[norm_total.size :]
    sent = jnp.concatenate(
        [
            norm_total.reshape(nc, depth * count_norm),
            jnp.broadcast_to(bias_total[None], (nc, bias_total.size)),
        ],
        axis=1,
    )
    came = jnp.sum(across(sent), axis=0)
    norm_mine = came[: depth * count_norm]
    norm_mine = (norm_mine + sibling(norm_mine)).reshape(depth, LAYERS, count_norm // LAYERS)
    norm_mine = norm_mine.transpose(1, 0, 2)
    bias_sum = came[depth * count_norm :]
    queries, values = bias_sum[: LAYERS * local], bias_sum[LAYERS * local : 2 * LAYERS * local]
    grad_bias = jnp.stack([queries.reshape(LAYERS, local), values.reshape(LAYERS, local)], axis=1)
    grad_up_bias = bias_sum[2 * LAYERS * local :].reshape(LAYERS, hidden)

    grad_qkv = jnp.stack(
        [jnp.stack([grads[l][0][:, i * local : (i + 1) * local] for i in range(3)], axis=1) for l in range(LAYERS)]
    )
    return (
        block_output,
        grad_tokens,
        grad_qkv,
        jnp.stack([grads[l][1] for l in range(LAYERS)]),
        jnp.stack([grads[l][2] for l in range(LAYERS)]),
        jnp.stack([grads[l][3] for l in range(LAYERS)]),
        grad_bias,
        grad_up_bias,
        norm_mine[:, :, :2],
        norm_mine[:, :, 2:],
    )


def solution(mesh):
    placed = (
        P(("fsdp", "ctx"), None),
        P(("fsdp", "ctx"), None),
        P("fsdp", None),
        P("fsdp", None),
        P(None, ("fsdp", "ctx"), None, "tp"),
        P(None, ("fsdp", "ctx"), "tp"),
        P(None, ("fsdp", "ctx"), "tp"),
        P(None, ("fsdp", "ctx"), "tp"),
        P(None, None, "tp"),
        P(None, "tp"),
        P(None, ("fsdp", "ctx"), None),
        P(None, ("fsdp", "ctx"), None),
    )
    return jax.shard_map(
        partial(on_device, mesh.shape["fsdp"], mesh.shape["ctx"], mesh.shape["tp"]),
        mesh=mesh,
        in_specs=placed,
        out_specs=(
            P(("fsdp", "ctx"), None),
            P(("fsdp", "ctx"), None),
            P(None, ("fsdp", "ctx"), None, "tp"),
            P(None, ("fsdp", "ctx"), "tp"),
            P(None, ("fsdp", "ctx"), "tp"),
            P(None, ("fsdp", "ctx"), "tp"),
            P(None, None, "tp"),
            P(None, "tp"),
            P(None, ("fsdp", "ctx"), None),
            P(None, ("fsdp", "ctx"), None),
        ),
        check_vma=False,
    )
```

time: 2110 us -> 750 us (0.36)
  waiting for transfers between devices: 1560 us -> 379 us
  matrix products: 175 us -> 0 us
  blocking collectives: 179 us -> 23.9 us
  Pallas kernels: 0 us -> 112 us
  starting transfers between devices: 2.51 us -> 114 us
  other arithmetic: 101 us -> 44.6 us
    reduce_scatter x10 -> x0, waiting for transfers between devices: 780 us -> none  [the longest x2 181 us: on_device(): lax.psum_scatter(grad_up, ('fsdp', 'ctx'), scatter_dimension=0, tiled=True)]
    psum x7 -> x0, waiting for transfers between devices: 320 us -> none  [the longest x4 167 us: tensor_sum(): return lax.psum(partial_sum, 'tp')]
    all_gather x8 -> x0, waiting for transfers between devices: 263 us -> none  [the longest x6 245 us: on_device(): lax.all_gather(shortened(layer_pieces(layer_number)), ('fsdp', 'ctx'), ax...]
    all_to_all x0 -> x21, waiting for transfers between devices: none -> 207 us  [across(): return lax.all_to_all(value, 'ctx', 0, 0)]
    unnamed x33 -> x0, waiting for transfers between devices: 197 us -> none
    dot_general x36 -> x0, matrix products: 175 us -> none  [the longest x2 19.4 us: score_block(): jnp.einsum('qhd,khd->hqk', queries, key_heads, preferred_element_type=jnp...]
    ppermute x0 -> x39, waiting for transfers between devices: none -> 172 us  [swap(): return lax.ppermute(value, axis, [(i, i ^ bit) for i in range(size)])]
    all_gather x6 -> x0, blocking collectives: 143 us -> none  [on_device(): lax.all_gather(shortened(layer_pieces(layer_number)), ('fsdp', 'ctx'), ax...]
  transfers between devices with their start and end apart: 29 -> 60, of which waited for: 29 -> 42; matrix products, arithmetic and copies ran while one was open for 6% -> 7% of each run, Pallas kernels for 0% -> 11%
where the time goes in v1:
time: 750 us; the launch traced here: 739 us
  waiting for transfers between devices  379 us (51%)
  starting transfers between devices  114 us (15%)
  Pallas kernels  112 us (15%)
  local copies, waits for them, and re-layouts  62.6 us (8%)
  other arithmetic  44.6 us (6%)
  blocking collectives  23.9 us (3%)
    all_to_all x21, waiting for transfers between devices, across(): return lax.all_to_all(value, 'ctx', 0, 0)  207 us
    ppermute x39, waiting for transfers between devices, swap(): return lax.ppermute(value, axis, [(i, i ^ bit) for i in range(size)])  172 us
    all_to_all x21, starting transfers between devices, across(): return lax.all_to_all(value, 'ctx', 0, 0)  87.7 us
    unnamed x262, local copies, waits for them, and re-layouts  39.4 us
    ppermute x39, starting transfers between devices, swap(): return lax.ppermute(value, axis, [(i, i ^ bit) for i in range(size)])  26.3 us
    all_to_all x1, blocking collectives, across(): return lax.all_to_all(value, 'ctx', 0, 0)  23.9 us
    pallas_call x2, Pallas kernels, mlp_backward(): pl.pallas_call(partial(mlp_back_kernel, nf, depth), grid=(hidden // tile,...  20.8 us
    pallas_call x2, Pallas kernels, mlp_forward(): pl.pallas_call(partial(mlp_kernel, nf, depth), grid=(hidden // tile,), in...  20.1 us
  transfers between devices with their start and end apart: 60, of which 42 were waited for; matrix products, arithmetic and copies ran while one was open for 7% of the time, Pallas kernels for 11%

profile of v1, /device:TPU:0, one launch (start us, length us, event | category | flops | bytes accessed | tf_op | source)
XLA Modules:
  0.0 739.0 jit_solution(8112647910824600450)
XLA Ops:
  12.6 20.8 %all-to-all-done.refs_3_.refs_1_ = bf16[4,144,768]{2,1,0:T(8,128)(2,1)S(1)} async-done(((bf16[4,144,768]{2,1,0:T(8,128)(2,1)}), bf16[4,144,768]{2,1,0:T(8,128)(2,1)S(1)}, u32[]{:S(2)}, u32[]{:S(2)}) %all-to-all-start) | async-done | bytes 884768 | tf_op jit(solution)/shard_map/all_to_all | solution.py:665
  41.4 17.5 %collective-permute-done.refs_4_.refs_2_ = bf16[4,144,768]{2,1,0:T(8,128)(2,1)S(1)} collective-permute-done((bf16[4,144,768]{2,1,0:T(8,128)(2,1)S(1)}, bf16[4,144,768]{2,1,0:T(8,128)(2,1)S(1)}, u32[]{:S(2)}, u32[]{:S(2)}) %collective-permute-start) | collective-permute-done | bytes 884768 | tf_op jit(solution)/shard_map/ppermute | solution.py:659
  75.0 17.9 %all-to-all-done.1.qkv_ref = bf16[4,192,512]{2,1,0:T(8,128)(2,1)} async-done(((bf16[4,192,512]{2,1,0:T(8,128)(2,1)}), bf16[4,192,512]{2,1,0:T(8,128)(2,1)}, u32[]{:S(2)}, u32[]{:S(2)}) %all-to-all-start.1) | async-done | bytes 786464 | tf_op jit(solution)/shard_map/all_to_all | solution.py:665
  122.1 18.7 %all-to-all-done.4.refs_5_ = bf16[4,128,1024]{2,1,0:T(8,128)(2,1)} async-done(((bf16[4,128,1024]{2,1,0:T(8,128)(2,1)}), bf16[4,128,1024]{2,1,0:T(8,128)(2,1)}, u32[]{:S(2)}, u32[]{:S(2)}) %all-to-all-start.4) | async-done | bytes 1048608 | tf_op jit(solution)/shard_map/all_to_all | solution.py:665
  150.9 14.4 %collective-permute-done.5.refs_6_ = bf16[4,128,1024]{2,1,0:T(8,128)(2,1)} collective-permute-done((bf16[4,128,1024]{2,1,0:T(8,128)(2,1)}, bf16[4,128,1024]{2,1,0:T(8,128)(2,1)}, u32[]{:S(2)}, u32[]{:S(2)}) %collective-permute-start.5) | collective-permute-done | bytes 1048608 | tf_op jit(solution)/shard_map/ppermute | solution.py:659
  165.3 10.0 %shard_map.202 = (f32[512,1024]{1,0:T(8,128)S(1)}, bf16[256,1024]{1,0:T(8,128)(2,1)S(1)}, f32[256,1024]{1,0:T(8,128)S(1)}) custom-call(bf16[256,1024]{1,0:T(8,128)(2,1)S(1)} %get-tuple-element.74.refs_0_, bf16[256,1024]{1,0:T(8,128)(2,1)S(1)} %collective-permute-done.4.refs_1_, f32[1,1024]{1,0:T(1,128)S(1)} %get-tuple-element.216.refs_2_, ...), custom_call_target="tpu_custom_call" | custom-call | flops 2147483648 | bytes 6291456 | tf_op jit(solution)/shard_map/pallas_call | solution.py:217
  181.3 11.3 %collective-permute-done.7.b_ref = bf16[256,1024]{1,0:T(8,128)(2,1)} collective-permute-done((bf16[256,1024]{1,0:T(8,128)(2,1)}, bf16[256,1024]{1,0:T(8,128)(2,1)}, u32[]{:S(2)}, u32[]{:S(2)}) %collective-permute-start.7) | collective-permute-done | bytes 524320 | tf_op jit(solution)/shard_map/ppermute | solution.py:659
  195.6 9.1 %collective-permute-done.9.refs_1_.refs_3_ = bf16[4,128,1024]{2,1,0:T(8,128)(2,1)S(1)} collective-permute-done((bf16[4,128,1024]{2,1,0:T(8,128)(2,1)S(1)}, bf16[4,128,1024]{2,1,0:T(8,128)(2,1)S(1)}, u32[]{:S(2)}, u32[]{:S(2)}) %collective-permute-start.9) | collective-permute-done | bytes 1048608 | tf_op jit(solution)/shard_map/ppermute | solution.py:659
  213.7 18.4 %all-to-all-done.6.qkv_ref = bf16[4,192,512]{2,1,0:T(8,128)(2,1)S(1)} async-done(((bf16[4,192,512]{2,1,0:T(8,128)(2,1)}), bf16[4,192,512]{2,1,0:T(8,128)(2,1)S(1)}, u32[]{:S(2)}, u32[]{:S(2)}) %all-to-all-start.6) | async-done | bytes 786464 | tf_op jit(solution)/shard_map/all_to_all | solution.py:665
  243.8 41.4 %all-to-all-done.8.refs_3_.refs_5_ = bf16[4,128,2048]{2,1,0:T(8,128)(2,1)S(1)} async-done(((bf16[4,128,2048]{2,1,0:T(8,128)(2,1)}), bf16[4,128,2048]{2,1,0:T(8,128)(2,1)S(1)}, u32[]{:S(2)}, u32[]{:S(2)}) %all-to-all-start.8) | async-done | bytes 2097184 | tf_op jit(solution)/shard_map/all_to_all | solution.py:665
  304.2 13.4 %collective-permute-done.11.b_ref = bf16[256,1024]{1,0:T(8,128)(2,1)S(1)} collective-permute-done((bf16[256,1024]{1,0:T(8,128)(2,1)S(1)}, bf16[256,1024]{1,0:T(8,128)(2,1)S(1)}, u32[]{:S(2)}, u32[]{:S(2)}) %collective-permute-start.11) | collective-permute-done | bytes 524320 | tf_op jit(solution)/shard_map/ppermute | solution.py:659
  318.3 17.7 %collective-permute-done.13.refs_4_.refs_6_ = bf16[4,128,2048]{2,1,0:T(8,128)(2,1)} collective-permute-done((bf16[4,128,2048]{2,1,0:T(8,128)(2,1)S(1)}, bf16[4,128,2048]{2,1,0:T(8,128)(2,1)}, u32[]{:S(2)}, u32[]{:S(2)}) %collective-permute-start.13) | collective-permute-done | bytes 2097184 | tf_op jit(solution)/shard_map/ppermute | solution.py:659
  336.1 10.1 %shard_map.209 = (f32[512,1024]{1,0:T(8,128)S(1)}, bf16[256,1024]{1,0:T(8,128)(2,1)S(1)}, f32[256,1024]{1,0:T(8,128)S(1)}) custom-call(bf16[256,1024]{1,0:T(8,128)(2,1)S(1)} %get-tuple-element.81.refs_0_, bf16[256,1024]{1,0:T(8,128)(2,1)S(1)} %collective-permute-done.12.refs_1_, f32[1,1024]{1,0:T(1,128)S(1)} %get-tuple-element.215.refs_2_, ...), custom_call_target="tpu_custom_call" | custom-call | flops 2147483648 | bytes 6291456 | tf_op jit(solution)/shard_map/pallas_call | solution.py:217
  350.2 13.4 %collective-permute-done.15.b_ref = bf16[256,1024]{1,0:T(8,128)(2,1)S(1)} collective-permute-done((bf16[256,1024]{1,0:T(8,128)(2,1)S(1)}, bf16[256,1024]{1,0:T(8,128)(2,1)S(1)}, u32[]{:S(2)}, u32[]{:S(2)}) %collective-permute-start.15) | collective-permute-done | bytes 524320 | tf_op jit(solution)/shard_map/ppermute | solution.py:659
  373.2 10.4 %shard_map.211 = (bf16[512,1024]{1,0:T(8,128)(2,1)S(1)}, bf16[512,1024]{1,0:T(8,128)(2,1)S(1)}, f32[1,1024]{1,0:T(1,128)S(1)}, bf16[256,1024]{1,0:T(8,128)(2,1)S(1)}, f32[256,1024]{1,0:T(8,128)S(1)}) custom-call(bf16[256,1024]{1,0:T(8,128)(2,1)S(1)} %get-tuple-element.165.refs_0_, bf16[256,1024]{1,0:T(8,128)(2,1)S(1)} %get-tuple-element.168.refs_1_, ...), custom_call_target="tpu_custom_call" | custom-call | flops 2147483648 | bytes 8388608 | tf_op jit(solution)/shard_map/pallas_call | solution.py:292
  388.3 13.4 %collective-permute-done.18.b_ref = bf16[256,1024]{1,0:T(8,128)(2,1)S(1)} collective-permute-done((bf16[256,1024]{1,0:T(8,128)(2,1)S(1)}, bf16[256,1024]{1,0:T(8,128)(2,1)S(1)}, u32[]{:S(2)}, u32[]{:S(2)}) %collective-permute-start.18) | collective-permute-done | bytes 524320 | tf_op jit(solution)/shard_map/ppermute | solution.py:659
  406.7 23.9 %all_to_all.114.g_ref = bf16[4,64,512]{2,1,0:T(8,128)(2,1)S(1)} all-to-all(bf16[4,64,512]{2,1,0:T(8,128)(2,1)S(1)} %shard_map.213), channel_id=1, replica_groups=mesh['fsdp'=2,'ctx'=4,'tp'=4] {'ctx'}, dimensions={0} | all-to-all | bytes 524288 | tf_op jit(solution)/shard_map/all_to_all | solution.py:665
  463.7 13.2 %collective-permute-done.32 = bf16[512,256]{1,0:T(8,128)(2,1)S(1)} collective-permute-done((bf16[512,256]{1,0:T(8,128)(2,1)}, bf16[512,256]{1,0:T(8,128)(2,1)S(1)}, u32[]{:S(2)}, u32[]{:S(2)}) %collective-permute-start.32) | collective-permute-done | bytes 262176 | tf_op jit(solution)/shard_map/ppermute | solution.py:659
  509.6 10.4 %shard_map.217 = (bf16[512,1024]{1,0:T(8,128)(2,1)S(1)}, bf16[512,1024]{1,0:T(8,128)(2,1)S(1)}, f32[1,1024]{1,0:T(1,128)S(1)}, bf16[256,1024]{1,0:T(8,128)(2,1)S(1)}, f32[256,1024]{1,0:T(8,128)S(1)}) custom-call(bf16[256,1024]{1,0:T(8,128)(2,1)S(1)} %get-tuple-element.94.refs_0_, bf16[256,1024]{1,0:T(8,128)(2,1)S(1)} %collective-permute-done.22.refs_1_, ...), custom_call_target="tpu_custom_call" | custom-call | flops 2147483648 | bytes 8388608 | tf_op jit(solution)/shard_map/pallas_call | solution.py:292
  534.3 8.5 %collective-permute-done.24.b_ref = bf16[256,1024]{1,0:T(8,128)(2,1)S(1)} collective-permute-done((bf16[256,1024]{1,0:T(8,128)(2,1)S(1)}, bf16[256,1024]{1,0:T(8,128)(2,1)S(1)}, u32[]{:S(2)}, u32[]{:S(2)}) %collective-permute-start.24) | collective-permute-done | bytes 524320 | tf_op jit(solution)/shard_map/ppermute | solution.py:659
  620.0 14.7 %collective-permute-done.31 = bf16[512,256]{1,0:T(8,128)(2,1)} collective-permute-done((bf16[512,256]{1,0:T(8,128)(2,1)}, bf16[512,256]{1,0:T(8,128)(2,1)}, u32[]{:S(2)}, u32[]{:S(2)}) %collective-permute-start.31) | collective-permute-done | bytes 262176 | tf_op jit(solution)/shard_map/ppermute | solution.py:659
  663.8 11.4 %all-to-all-done.17 = bf16[4,128,1024]{2,1,0:T(8,128)(2,1)} async-done(((bf16[4,128,1024]{2,1,0:T(8,128)(2,1)}), bf16[4,128,1024]{2,1,0:T(8,128)(2,1)}, u32[]{:S(2)}, u32[]{:S(2)}) %all-to-all-start.17) | async-done | bytes 1048608 | tf_op jit(solution)/shard_map/all_to_all | solution.py:665
  686.6 17.9 %all-to-all-done.19 = bf16[4,128,1024]{2,1,0:T(8,128)(2,1)} async-done(((bf16[4,128,1024]{2,1,0:T(8,128)(2,1)}), bf16[4,128,1024]{2,1,0:T(8,128)(2,1)}, u32[]{:S(2)}, u32[]{:S(2)}) %all-to-all-start.19) | async-done | bytes 1048608 | tf_op jit(solution)/shard_map/all_to_all | solution.py:665
  727.3 8.2 %all-to-all-done.13 = bf16[4,128,768]{2,1,0:T(8,128)(2,1)S(1)} async-done(((bf16[4,128,768]{2,1,0:T(8,128)(2,1)}), bf16[4,128,768]{2,1,0:T(8,128)(2,1)S(1)}, u32[]{:S(2)}, u32[]{:S(2)}) %all-to-all-start.13) | async-done | bytes 786464 | tf_op jit(solution)/shard_map/all_to_all | solution.py:665
  (496 shorter events, 370.0 us)
Async XLA Ops:
  4.9 28.5 %all-to-all-start = ((bf16[4,144,768]{2,1,0:T(8,128)(2,1)}), bf16[4,144,768]{2,1,0:T(8,128)(2,1)S(1)}, u32[]{:S(2)}, u32[]{:S(2)}) async-start(bf16[4,144,768]{2,1,0:T(8,128)(2,1)} %broadcast_in_dim.28), calls=%async_computation | async-start | bytes 1769472 | tf_op jit(solution)/shard_map/all_to_all | solution.py:665
  34.7 34.4 %all-to-all-start.3 = ((bf16[4,128,1280]{2,1,0:T(8,128)(2,1)}), bf16[4,128,1280]{2,1,0:T(8,128)(2,1)S(1)}, u32[]{:S(2)}, u32[]{:S(2)}) async-start(bf16[4,128,1280]{2,1,0:T(8,128)(2,1)} %broadcast_in_dim.29), calls=%async_computation.3 | async-start | bytes 2621440 | tf_op jit(solution)/shard_map/all_to_all | solution.py:665
  69.0 23.9 %all-to-all-start.1 = ((bf16[4,192,512]{2,1,0:T(8,128)(2,1)}), bf16[4,192,512]{2,1,0:T(8,128)(2,1)}, u32[]{:S(2)}, u32[]{:S(2)}) async-start(bf16[4,192,512]{2,1,0:T(8,128)(2,1)} %copy-done.27), calls=%async_computation.1 | async-start | bytes 1572864 | tf_op jit(solution)/shard_map/all_to_all | solution.py:665
  73.2 44.1 %collective-permute-start.1 = (bf16[4,128,1280]{2,1,0:T(8,128)(2,1)S(1)}, bf16[4,128,1280]{2,1,0:T(8,128)(2,1)S(1)}, u32[]{:S(2)}, u32[]{:S(2)}) collective-permute-start(bf16[4,128,1280]{2,1,0:T(8,128)(2,1)S(1)} %all-to-all-done.3.refs_0_.refs_2_), channel_id=1, source_target_pairs={{0,16},{16,0},{1,17},{17,1},{2,18},{18,2},{3,19},{19,3},{4,20},{20... | collective-permute-start | bytes 3932168 | tf_op jit(solution)/shard_map/ppermute | solution.py:659
  113.1 27.8 %all-to-all-start.4 = ((bf16[4,128,1024]{2,1,0:T(8,128)(2,1)}), bf16[4,128,1024]{2,1,0:T(8,128)(2,1)}, u32[]{:S(2)}, u32[]{:S(2)}) async-start(bf16[4,128,1024]{2,1,0:T(8,128)(2,1)} %broadcast_in_dim.31), calls=%async_computation.4 | async-start | bytes 2097152 | tf_op jit(solution)/shard_map/all_to_all | solution.py:665
  120.6 27.5 %collective-permute-start.3 = (bf16[256,1024]{1,0:T(8,128)(2,1)}, bf16[256,1024]{1,0:T(8,128)(2,1)}, u32[]{:S(2)}, u32[]{:S(2)}) collective-permute-start(bf16[256,1024]{1,0:T(8,128)(2,1)} %add_convert_fusion.13.a_ref), channel_id=1, source_target_pairs={{0,2},{1,3},{2,0},{3,1},{4,6},{5,7},{6,4},{7,5},{8,10},{9,11},{10,... | collective-permute-start | bytes 1572872 | tf_op jit(solution)/shard_map/ppermute | solution.py:659
  140.9 24.4 %collective-permute-start.5 = (bf16[4,128,1024]{2,1,0:T(8,128)(2,1)}, bf16[4,128,1024]{2,1,0:T(8,128)(2,1)}, u32[]{:S(2)}, u32[]{:S(2)}) collective-permute-start(bf16[4,128,1024]{2,1,0:T(8,128)(2,1)} %all-to-all-done.4.refs_5_), channel_id=1, source_target_pairs={{0,16},{16,0},{1,17},{17,1},{2,18},{18,2},{3,19},{19,3},{4,20},{20... | collective-permute-start | bytes 3145736 | tf_op jit(solution)/shard_map/ppermute | solution.py:659
  144.4 35.4 %all-to-all-start.5 = ((bf16[4,128,1024]{2,1,0:T(8,128)(2,1)}), bf16[4,128,1024]{2,1,0:T(8,128)(2,1)S(1)}, u32[]{:S(2)}, u32[]{:S(2)}) async-start(bf16[4,128,1024]{2,1,0:T(8,128)(2,1)} %broadcast_in_dim.32), calls=%async_computation.5 | async-start | bytes 2097152 | tf_op jit(solution)/shard_map/all_to_all | solution.py:665
  179.8 24.9 %collective-permute-start.9 = (bf16[4,128,1024]{2,1,0:T(8,128)(2,1)S(1)}, bf16[4,128,1024]{2,1,0:T(8,128)(2,1)S(1)}, u32[]{:S(2)}, u32[]{:S(2)}) collective-permute-start(bf16[4,128,1024]{2,1,0:T(8,128)(2,1)S(1)} %all-to-all-done.5.refs_0_.refs_2_), channel_id=1, source_target_pairs={{0,16},{16,0},{1,17},{17,1},{2,18},{18,2},{3,19},{19,3},{4,20},{20... | collective-permute-start | bytes 3145736 | tf_op jit(solution)/shard_map/ppermute | solution.py:659
  233.7 51.5 %all-to-all-start.8 = ((bf16[4,128,2048]{2,1,0:T(8,128)(2,1)}), bf16[4,128,2048]{2,1,0:T(8,128)(2,1)S(1)}, u32[]{:S(2)}, u32[]{:S(2)}) async-start(bf16[4,128,2048]{2,1,0:T(8,128)(2,1)} %broadcast_in_dim.58), calls=%async_computation.8 | async-start | bytes 4194304 | tf_op jit(solution)/shard_map/all_to_all | solution.py:665
  289.3 46.8 %collective-permute-start.13 = (bf16[4,128,2048]{2,1,0:T(8,128)(2,1)S(1)}, bf16[4,128,2048]{2,1,0:T(8,128)(2,1)}, u32[]{:S(2)}, u32[]{:S(2)}) collective-permute-start(bf16[4,128,2048]{2,1,0:T(8,128)(2,1)S(1)} %all-to-all-done.8.refs_3_.refs_5_), channel_id=1, source_target_pairs={{0,16},{16,0},{1,17},{17,1},{2,18},{18,2},{3,19},{19,3},{4,20},{20... | collective-permute-start | bytes 6291464 | tf_op jit(solution)/shard_map/ppermute | solution.py:659
  448.3 34.1 %collective-permute-start.34 = (bf16[512,1024]{1,0:T(8,128)(2,1)}, bf16[512,1024]{1,0:T(8,128)(2,1)}, u32[]{:S(2)}, u32[]{:S(2)}) collective-permute-start(bf16[512,1024]{1,0:T(8,128)(2,1)} %get-tuple-element.119), channel_id=1, source_target_pairs={{0,16},{16,0},{1,17},{17,1},{2,18},{18,2},{3,19},{19,3},{4,20},{20... | collective-permute-start | bytes 3145736 | tf_op jit(solution)/shard_map/ppermute | solution.py:659
  452.7 24.2 %collective-permute-start.32 = (bf16[512,256]{1,0:T(8,128)(2,1)}, bf16[512,256]{1,0:T(8,128)(2,1)S(1)}, u32[]{:S(2)}, u32[]{:S(2)}) collective-permute-start(bf16[512,256]{1,0:T(8,128)(2,1)} %get-tuple-element.113), channel_id=1, source_target_pairs={{0,16},{16,0},{1,17},{17,1},{2,18},{18,2},{3,19},{19,3},{4,20},{20... | collective-permute-start | bytes 786440 | tf_op jit(solution)/shard_map/ppermute | solution.py:659
  463.7 30.6 %collective-permute-start.20 = (bf16[256,1024]{1,0:T(8,128)(2,1)}, bf16[256,1024]{1,0:T(8,128)(2,1)}, u32[]{:S(2)}, u32[]{:S(2)}) collective-permute-start(bf16[256,1024]{1,0:T(8,128)(2,1)} %get-tuple-element.92), channel_id=1, source_target_pairs={{0,1},{1,0},{2,3},{3,2},{4,5},{5,4},{6,7},{7,6},{8,9},{9,8},{10,11... | collective-permute-start | bytes 1572872 | tf_op jit(solution)/shard_map/ppermute | solution.py:659
  489.9 33.6 %all-to-all-start.18 = ((bf16[4,128,1024]{2,1,0:T(8,128)(2,1)}), bf16[4,128,1024]{2,1,0:T(8,128)(2,1)}, u32[]{:S(2)}, u32[]{:S(2)}) async-start(bf16[4,128,1024]{2,1,0:T(8,128)(2,1)} %bitcast.105), calls=%async_computation.18 | async-start | bytes 2097152 | tf_op jit(solution)/shard_map/all_to_all | solution.py:665
  523.6 31.4 %all-to-all-start.20 = ((bf16[4,128,1024]{2,1,0:T(8,128)(2,1)}), bf16[4,128,1024]{2,1,0:T(8,128)(2,1)}, u32[]{:S(2)}, u32[]{:S(2)}) async-start(bf16[4,128,1024]{2,1,0:T(8,128)(2,1)} %bitcast.106), calls=%async_computation.20 | async-start | bytes 2097152 | tf_op jit(solution)/shard_map/all_to_all | solution.py:665
  532.8 25.6 %collective-permute-start.30 = (bf16[512,768]{1,0:T(8,128)(2,1)}, bf16[512,768]{1,0:T(8,128)(2,1)}, u32[]{:S(2)}, u32[]{:S(2)}) collective-permute-start(bf16[512,768]{1,0:T(8,128)(2,1)} %get-tuple-element.109), channel_id=1, source_target_pairs={{0,16},{16,0},{1,17},{17,1},{2,18},{18,2},{3,19},{19,3},{4,20},{20... | collective-permute-start | bytes 2359304 | tf_op jit(solution)/shard_map/ppermute | solution.py:659
  566.9 25.1 %all-to-all-start.14 = ((bf16[4,128,768]{2,1,0:T(8,128)(2,1)}), bf16[4,128,768]{2,1,0:T(8,128)(2,1)S(1)}, u32[]{:S(2)}, u32[]{:S(2)}) async-start(bf16[4,128,768]{2,1,0:T(8,128)(2,1)} %bitcast.108), calls=%async_computation.14 | async-start | bytes 1572864 | tf_op jit(solution)/shard_map/all_to_all | solution.py:665
  583.0 25.8 %collective-permute-start.33 = (bf16[512,1024]{1,0:T(8,128)(2,1)}, bf16[512,1024]{1,0:T(8,128)(2,1)}, u32[]{:S(2)}, u32[]{:S(2)}) collective-permute-start(bf16[512,1024]{1,0:T(8,128)(2,1)} %get-tuple-element.116), channel_id=1, source_target_pairs={{0,16},{16,0},{1,17},{17,1},{2,18},{18,2},{3,19},{19,3},{4,20},{20... | collective-permute-start | bytes 3145736 | tf_op jit(solution)/shard_map/ppermute | solution.py:659
  604.1 37.1 %collective-permute-start.35 = (bf16[512,1024]{1,0:T(8,128)(2,1)}, bf16[512,1024]{1,0:T(8,128)(2,1)}, u32[]{:S(2)}, u32[]{:S(2)}) collective-permute-start(bf16[512,1024]{1,0:T(8,128)(2,1)} %get-tuple-element.122), channel_id=1, source_target_pairs={{0,16},{16,0},{1,17},{17,1},{2,18},{18,2},{3,19},{19,3},{4,20},{20... | collective-permute-start | bytes 3145736 | tf_op jit(solution)/shard_map/ppermute | solution.py:659
  606.8 27.9 %collective-permute-start.31 = (bf16[512,256]{1,0:T(8,128)(2,1)}, bf16[512,256]{1,0:T(8,128)(2,1)}, u32[]{:S(2)}, u32[]{:S(2)}) collective-permute-start(bf16[512,256]{1,0:T(8,128)(2,1)} %get-tuple-element.111), channel_id=1, source_target_pairs={{0,16},{16,0},{1,17},{17,1},{2,18},{18,2},{3,19},{19,3},{4,20},{20... | collective-permute-start | bytes 786440 | tf_op jit(solution)/shard_map/ppermute | solution.py:659
  620.0 23.9 %collective-permute-start.26 = (bf16[256,1024]{1,0:T(8,128)(2,1)}, bf16[256,1024]{1,0:T(8,128)(2,1)S(1)}, u32[]{:S(2)}, u32[]{:S(2)}) collective-permute-start(bf16[256,1024]{1,0:T(8,128)(2,1)} %get-tuple-element.102), channel_id=1, source_target_pairs={{0,1},{1,0},{2,3},{3,2},{4,5},{5,4},{6,7},{7,6},{8,9},{9,8},{10,11... | collective-permute-start | bytes 1572872 | tf_op jit(solution)/shard_map/ppermute | solution.py:659
  648.0 27.2 %all-to-all-start.17 = ((bf16[4,128,1024]{2,1,0:T(8,128)(2,1)}), bf16[4,128,1024]{2,1,0:T(8,128)(2,1)}, u32[]{:S(2)}, u32[]{:S(2)}) async-start(bf16[4,128,1024]{2,1,0:T(8,128)(2,1)} %bitcast.104), calls=%async_computation.17 | async-start | bytes 2097152 | tf_op jit(solution)/shard_map/all_to_all | solution.py:665
  675.2 29.3 %all-to-all-start.19 = ((bf16[4,128,1024]{2,1,0:T(8,128)(2,1)}), bf16[4,128,1024]{2,1,0:T(8,128)(2,1)}, u32[]{:S(2)}, u32[]{:S(2)}) async-start(bf16[4,128,1024]{2,1,0:T(8,128)(2,1)} %bitcast.42), calls=%async_computation.19 | async-start | bytes 2097152 | tf_op jit(solution)/shard_map/all_to_all | solution.py:665
  (163 other events, 1548.5 us)

commit v2 on v1

v2 whole, which is shorter than its diff:
```python
from functools import partial

import jax
import jax.numpy as jnp
from jax import lax
from jax.experimental import pallas as pl
from jax.experimental.pallas import tpu as pltpu
from jax.sharding import PartitionSpec as P

HEADS = 16
HD = 64
BLK = 128
RUN_BLOCKS = 8
LAYERS = 2
NORM_ROWS = 8
NORM_EPS = 1e-05
MASKED = -1000000000.0
QB = 256
GELU_A = 0.7978845608028654
GELU_B = 0.044715
BF = jnp.bfloat16
F32 = jnp.float32
NN = ((1,), (0,))
NT = ((1,), (1,))
VMEM_LIMIT = 40 * 1024 * 1024


def dot(left, right, dims=NN):
    return lax.dot_general(left, right, (dims, ((), ())), preferred_element_type=F32)


def shaped(shape, dtype):
    return jax.ShapeDtypeStruct(shape, dtype)


def whole():
    return pl.BlockSpec(memory_space=pltpu.VMEM)


def params(flops, bytes_accessed, transcendentals=0):
    return dict(
        compiler_params=pltpu.CompilerParams(vmem_limit_bytes=VMEM_LIMIT),
        cost_estimate=pl.CostEstimate(
            flops=int(flops), bytes_accessed=int(bytes_accessed), transcendentals=int(transcendentals)
        ),
    )


def rows_of(refs, col, cols, depth, extra=0):
    pieces = []
    for ref in refs:
        for start in range(0, ref.shape[0], depth + extra):
            pieces.append(ref[start : start + depth, col : col + cols])
    return jnp.concatenate(pieces, axis=0)


def call(kernel, out_shape, args, flops, scratch=(), transcendentals=0, smem=0):
    outs = out_shape if isinstance(out_shape, (list, tuple)) else [out_shape]
    moved = sum(a.size * a.dtype.itemsize for a in args) + sum(
        o.size * jnp.dtype(o.dtype).itemsize for o in outs
    )
    specs = [pl.BlockSpec(memory_space=pltpu.SMEM)] * smem + [whole()] * (len(args) - smem)
    return pl.pallas_call(
        kernel,
        in_specs=specs,
        out_specs=[whole()] * len(outs) if outs is out_shape else whole(),
        out_shape=out_shape,
        scratch_shapes=list(scratch),
        **params(flops, moved, transcendentals),
    )(*args)


def norm_stats(values):
    average = jnp.mean(values, axis=-1, keepdims=True)
    centred = values - average
    variance = jnp.mean(centred * centred, axis=-1, keepdims=True)
    scale = lax.rsqrt(variance + NORM_EPS)
    return centred * scale, scale


def gelu_parts(u):
    inner = GELU_A * (u + GELU_B * u * u * u)
    t = jnp.tanh(inner)
    return t


def add_norm_kernel(bias_row, gain_row, shift_row, x_ref, a_ref, b_ref, table_ref, y_ref, h_ref):
    branch = a_ref[...].astype(F32) + b_ref[...].astype(F32) + table_ref[bias_row : bias_row + 1, :]
    y = x_ref[...].astype(F32) + branch
    y_ref[...] = y
    n, _ = norm_stats(y)
    h_ref[...] = (
        n * table_ref[gain_row : gain_row + 1, :] + table_ref[shift_row : shift_row + 1, :]
    ).astype(BF)


def add_norm(x, a, b, table, bias_row, gain_row, shift_row):
    rows, width = x.shape
    return call(
        partial(add_norm_kernel, bias_row, gain_row, shift_row),
        [shaped((rows, width), F32), shaped((rows, width), BF)],
        [x, a, b, table],
        rows * width * 12,
    )


def heads_out(out_ref, total, number, row):
    half = total.shape[0]
    turned = total.astype(BF).T
    for j in range(out_ref.shape[0]):
        out_ref[j, row : row + HD, number * half : (number + 1) * half] = turned[j * HD : (j + 1) * HD, :]


def qkv_rows(h_refs, bias_ref, w_refs, out_ref, col, depth, extra):
    local = out_ref.shape[0] * HD
    h = jnp.concatenate([h_ref[...] for h_ref in h_refs], axis=0)
    for i in range(3):
        weights = rows_of(w_refs, col + i * local, local, depth, extra)
        heads_out(out_ref, dot(h, weights) + bias_ref[i : i + 1, :], 0, i * HD)


def qkv_kernel(col, depth, h_own, h_oth, bias_ref, *refs):
    qkv_rows([h_own, h_oth], bias_ref, refs[:-1], refs[-1], col, depth, 0)


def qkv_project(h_own, h_oth, bias, pack, col, depth):
    half, width = h_own.shape
    local = bias.shape[1]
    return call(
        partial(qkv_kernel, col, depth),
        shaped((local // HD, 3 * HD, 2 * half), BF),
        [h_own, h_oth, bias, *pack],
        12 * half * width * local,
    )


def first_qkv_kernel(row, depth, extra, n_own, n_oth, table_ref, bias_ref, *refs):
    w_refs, (h_own, h_oth, out_ref) = refs[:-3], refs[-3:]
    for n_ref, h_ref in ((n_own, h_own), (n_oth, h_oth)):
        h_ref[...] = (n_ref[...] * table_ref[row : row + 1, :] + table_ref[row + 2 : row + 3, :]).astype(BF)
    qkv_rows([h_own, h_oth], bias_ref, w_refs, out_ref, 0, depth, extra)


def first_qkv(n_own, n_oth, table, row, bias, pack, depth, extra):
    half, width = n_own.shape
    local = bias.shape[1]
    return call(
        partial(first_qkv_kernel, row, depth, extra),
        [
            shaped((half, width), BF),
            shaped((half, width), BF),
            shaped((local // HD, 3 * HD, 2 * half), BF),
        ],
        [n_own, n_oth, table, bias, *pack],
        12 * half * width * local,
    )


def out_kernel(col, depth, start, o_ref, *refs):
    w_refs, out_ref = refs[:-1], refs[-1]
    half = out_ref.shape[0]
    heads = o_ref.shape[0]
    o = jnp.concatenate([o_ref[j, :, start : start + half] for j in range(heads)], axis=0).T
    weights = rows_of(w_refs, col, heads * HD, depth)
    out_ref[...] = dot(o, weights, NT).astype(out_ref.dtype)


def out_project(o_rows, pack, col, depth, width, start, dtype):
    heads, _, rows = o_rows.shape
    half = rows // 2
    return call(
        partial(out_kernel, col, depth, start),
        shaped((half, width), dtype),
        [o_rows, *pack],
        2 * half * width * heads * HD,
    )


def mlp_kernel(counts, up_col, down_col, depth, h_own, h_oth, bias_ref, *refs):
    ups, downs = refs[: counts[0]], refs[counts[0] : counts[0] + counts[1]]
    u_ref, oth_ref, own_ref = refs[counts[0] + counts[1] :]
    half = h_own.shape[0]
    hidden = u_ref.shape[1]
    h = jnp.concatenate([h_own[...], h_oth[...]], axis=0)
    u = dot(h, rows_of(ups, up_col, hidden, depth)) + bias_ref[...]
    u_ref[...] = u
    act = (0.5 * u * (1.0 + gelu_parts(u))).astype(BF)
    total = dot(act, rows_of(downs, down_col, hidden, depth), NT)
    own_ref[...] = total[:half, :]
    oth_ref[...] = total[half:, :].astype(BF)


def mlp_forward(h_own, h_oth, bias, up, down, depth):
    half, width = h_own.shape
    hidden = bias.shape[1]
    return call(
        partial(mlp_kernel, (len(up[0]), len(down[0])), up[1], down[1], depth),
        [
            shaped((2 * half, hidden), F32),
            shaped((half, width), BF),
            shaped((half, width), F32),
        ],
        [h_own, h_oth, bias, *up[0], *down[0]],
        8 * half * width * hidden,
        transcendentals=2 * half * hidden,
    )


def mlp_back_kernel(counts, up_col, down_col, depth, g_own, g_oth, u_ref, *refs):
    ups, downs = refs[: counts[0]], refs[counts[0] : counts[0] + counts[1]]
    act_ref, gu_ref, sum_ref, oth_ref, own_ref = refs[counts[0] + counts[1] :]
    half = g_own.shape[0]
    hidden = u_ref.shape[1]
    g = jnp.concatenate([g_own[...], g_oth[...]], axis=0)
    grad = dot(g, rows_of(downs, down_col, hidden, depth))
    u = u_ref[...]
    t = gelu_parts(u)
    act_ref[...] = (0.5 * u * (1.0 + t)).astype(BF)
    slope = 0.5 * (1.0 + t) + 0.5 * u * (1.0 - t * t) * (GELU_A * (1.0 + 3.0 * GELU_B * u * u))
    gu = (grad * slope).astype(BF)
    gu_ref[...] = gu
    sum_ref[...] = jnp.sum(gu.astype(F32), axis=0, keepdims=True)
    total = dot(gu, rows_of(ups, up_col, hidden, depth), NT)
    own_ref[...] = total[:half, :]
    oth_ref[...] = total[half:, :].astype(BF)


def mlp_backward(g_own, g_oth, u, up, down, depth):
    half, width = g_own.shape
    hidden = u.shape[1]
    return call(
        partial(mlp_back_kernel, (len(up[0]), len(down[0])), up[1], down[1], depth),
        [
            shaped((2 * half, hidden), BF),
            shaped((2 * half, hidden), BF),
            shaped((1, hidden), F32),
            shaped((half, width), BF),
            shaped((half, width), F32),
        ],
        [g_own, g_oth, u, *up[0], *down[0]],
        8 * half * width * hidden,
        transcendentals=2 * half * hidden,
    )


def grads_out(out_refs, total, col):
    span = out_refs[0].shape[0]
    for y, out_ref in enumerate(out_refs):
        out_ref[:, col : col + total.shape[1]] = total[y * span : (y + 1) * span].astype(BF)


def mlp_grad_kernel(g_own, g_oth, h_own, h_oth, act_ref, gu_ref, *out_refs):
    hidden = act_ref.shape[1]
    h = jnp.concatenate([h_own[...], h_oth[...]], axis=0).T
    grads_out(out_refs, dot(h, gu_ref[...]), 0)
    g = jnp.concatenate([g_own[...], g_oth[...]], axis=0).T
    grads_out(out_refs, dot(g, act_ref[...]), hidden)


def mlp_grad(g_own, g_oth, h_own, h_oth, act, gu, nf):
    half, width = g_own.shape
    hidden = act.shape[1]
    return call(
        mlp_grad_kernel,
        [shaped((width // nf, 2 * hidden), BF)] * nf,
        [g_own, g_oth, h_own, h_oth, act, gu],
        8 * half * width * hidden,
    )


def out_q_grad_kernel(g_own, g_oth, o_ref, h_own, h_oth, p_ref, *out_refs):
    heads = o_ref.shape[0]
    local = heads * HD
    g = jnp.concatenate([g_own[...], g_oth[...]], axis=0).T
    o = jnp.concatenate([o_ref[j] for j in range(heads)], axis=0)
    grads_out(out_refs, dot(g, o, NT), 0)
    h = jnp.concatenate([h_own[...], h_oth[...]], axis=0).T
    grads_out(out_refs, dot(h, p_ref[:, :local]), local)


def out_q_grad(g_own, g_oth, o_rows, h_own, h_oth, g_proj, nf):
    half, width = g_own.shape
    local = o_rows.shape[0] * HD
    return call(
        out_q_grad_kernel,
        [shaped((width // nf, 2 * local), BF)] * nf,
        [g_own, g_oth, o_rows, h_own, h_oth, g_proj],
        8 * half * width * local,
    )


def kv_grad_kernel(h_own, h_oth, p_ref, *out_refs):
    local = p_ref.shape[1] // 3
    h = jnp.concatenate([h_own[...], h_oth[...]], axis=0).T
    grads_out(out_refs, dot(h, p_ref[:, local:]), 0)


def kv_grad(h_own, h_oth, g_proj, nf):
    half, width = h_own.shape
    local = g_proj.shape[1] // 3
    return call(
        kv_grad_kernel,
        [shaped((width // nf, 2 * local), BF)] * nf,
        [h_own, h_oth, g_proj],
        8 * half * width * local,
    )


def part_sum_kernel(depth, own_ref, *refs):
    count = (len(refs) - own_ref.shape[0] // depth)
    came, outs = refs[:count], refs[count:]
    for number, out_ref in enumerate(outs):
        rows = slice(number * depth, (number + 1) * depth)
        total = own_ref[rows, :].astype(F32)
        for ref in came:
            total = total + ref[rows, :].astype(F32)
        out_ref[...] = total.astype(out_ref.dtype)


def part_sum(own, came, depth):
    rows, cols = own.shape
    pieces = rows // depth
    return call(
        partial(part_sum_kernel, depth),
        [shaped((depth, cols), F32 if k == 0 else BF) for k in range(pieces)],
        [own, *came],
        rows * cols * 2,
    )


def final_kernel(plans, *refs):
    outs = refs[-len(plans) :]
    for out_ref, plan in zip(outs, plans):
        for index, first, count, col in plan:
            cols = out_ref.shape[-1]
            total = refs[first][:, col : col + cols].astype(F32)
            for k in range(1, count):
                total = total + refs[first + k][:, col : col + cols].astype(F32)
            out_ref[index] = total


def final_sums(plans, shapes, pieces):
    return call(partial(final_kernel, plans), shapes, pieces, sum(p.size for p in pieces))


def norm_back_kernel(gain_row, gx_ref, a_ref, b_ref, y_ref, table_ref, gy_ref, low_ref, sums_ref):
    grad = a_ref[...].astype(F32) + b_ref[...].astype(F32)
    n, scale = norm_stats(y_ref[...].astype(F32))
    e = grad * table_ref[gain_row : gain_row + 1, :]
    mean_e = jnp.mean(e, axis=-1, keepdims=True)
    mean_en = jnp.mean(e * n, axis=-1, keepdims=True)
    gx = gx_ref[...].astype(F32)
    gy = gx + scale * (e - mean_e - n * mean_en)
    gy_ref[...] = gy
    low = gy.astype(BF)
    low_ref[...] = low
    sums_ref[0:1, :] = jnp.sum(grad * n, axis=0, keepdims=True)
    sums_ref[1:2, :] = jnp.sum(grad, axis=0, keepdims=True)
    sums_ref[2:3, :] = jnp.sum(low.astype(F32), axis=0, keepdims=True)
    sums_ref[3:4, :] = jnp.sum(gx.astype(BF).astype(F32), axis=0, keepdims=True)
    sums_ref[4:, :] = jnp.zeros((4, gx.shape[1]), F32)


def norm_backward(gx, a, b, y, table, gain_row):
    rows, width = gx.shape
    return call(
        partial(norm_back_kernel, gain_row),
        [shaped((rows, width), F32), shaped((rows, width), BF), shaped((8, width), F32)],
        [gx, a, b, y, table],
        rows * width * 25,
    )


def out_back_kernel(col, depth, g_own, g_oth, *refs):
    w_refs, out_ref = refs[:-1], refs[-1]
    g = jnp.concatenate([g_own[...], g_oth[...]], axis=0)
    heads_out(out_ref, dot(g, rows_of(w_refs, col, out_ref.shape[0] * HD, depth)), 0, 0)


def out_backward(g_own, g_oth, pack, col, depth, local):
    half, width = g_own.shape
    return call(
        partial(out_back_kernel, col, depth),
        shaped((local // HD, HD, 2 * half), BF),
        [g_own, g_oth, *pack],
        4 * half * width * local,
    )


def qkv_back_kernel(col, depth, extra, g_ref, *refs):
    w_refs, (rows_ref, sum_ref, oth_ref, own_ref) = refs[:-4], refs[-4:]
    heads = g_ref.shape[0]
    half = own_ref.shape[0]
    local = heads * HD
    planes = [
        jnp.concatenate([g_ref[j, i * HD : (i + 1) * HD, :] for j in range(heads)], axis=0).T
        for i in range(3)
    ]
    grads = jnp.concatenate(planes, axis=1)
    rows_ref[...] = grads
    total = dot(grads, rows_of(w_refs, col, 3 * local, depth, extra), NT)
    oth_ref[...] = total[half:].astype(BF)
    own_ref[...] = total[:half]
    sum_ref[...] = jnp.sum(grads.astype(F32), axis=0, keepdims=True)


def qkv_backward(g, pack, col, depth, extra, width):
    heads, _, rows = g.shape
    half = rows // 2
    cols = 3 * heads * HD
    return call(
        partial(qkv_back_kernel, col, depth, extra),
        [
            shaped((rows, cols), BF),
            shaped((1, cols), F32),
            shaped((half, width), BF),
            shaped((half, width), F32),
        ],
        [g, *pack],
        2 * rows * width * cols,
    )


def gather_blocks(source_ref, src_ref, dest_ref, per_device):
    for s in range(dest_ref.shape[1] // BLK):
        src = src_ref[s]
        z = src // per_device
        start = pl.multiple_of((src - z * per_device) * BLK, BLK)
        dest_ref[:, s * BLK : (s + 1) * BLK] = source_ref[z, :, pl.ds(start, BLK)]


def scatter_blocks(dest_ref, src_ref, source, per_device, low, first):
    depth, columns = source.shape
    for s in range(columns // BLK):
        src = src_ref[first + s]
        z = src // per_device
        start = pl.multiple_of((src - z * per_device) * BLK, BLK)
        dest_ref[z, low : low + depth, pl.ds(start, BLK)] = source[:, s * BLK : (s + 1) * BLK]


def segment_columns(seg_ref, column_ref):
    for s in range(seg_ref.shape[1] // BLK):
        row = seg_ref[:, s * BLK : (s + 1) * BLK]
        row = jnp.where(row < 0, -2, row).astype(F32)
        column_ref[s * BLK : (s + 1) * BLK, :] = jnp.broadcast_to(row, (BLK, BLK)).T


def score_tile(keys, queries, column_ref, seg_ref, slope, base, first, last):
    depth = keys.shape[0]
    width = last - first
    scores = dot(keys, queries)
    key_row = lax.broadcasted_iota(jnp.int32, (depth, width), 0)
    query_row = lax.broadcasted_iota(jnp.int32, (depth, width), 1) + (first - base)
    distance = query_row - key_row
    scores = scores - slope * distance.astype(F32)
    columns = column_ref[base : base + depth, :]
    key_seg = jnp.concatenate([columns] * (width // BLK), axis=1)
    query_seg = seg_ref[:, first:last].astype(F32)
    allowed = ((key_seg == query_seg) & (distance >= 0)) | (distance == 0)
    return scores, allowed


def attend_kernel(per_device, src_ref, slope_ref, seg_ref, qkv_ref, o_ref, lse_ref, stream_ref, column_ref):
    gather_blocks(qkv_ref, src_ref, stream_ref, per_device)
    segment_columns(seg_ref, column_ref)
    slope = slope_ref[0]
    run = RUN_BLOCKS * BLK
    for base in range(0, stream_ref.shape[1], run):
        keys = stream_ref[HD : 2 * HD, base : base + run].T
        for first in range(base, base + run, QB):
            last = first + QB
            depth = last - base
            queries = stream_ref[:HD, first:last] * jnp.asarray(HD**-0.5, BF)
            scores, allowed = score_tile(
                keys[:depth], queries, column_ref, seg_ref, slope, base, first, last
            )
            scores = jnp.where(allowed, scores, MASKED)
            top = jnp.max(scores, axis=0, keepdims=True)
            weights = jnp.exp(scores - top)
            total = jnp.sum(weights, axis=0, keepdims=True)
            lse_ref[:, first:last] = top + jnp.log(total)
            values = stream_ref[2 * HD :, base : base + depth]
            out = (dot(values, weights.astype(BF)) / total).astype(BF)
            scatter_blocks(o_ref, src_ref, out, per_device, 0, first // BLK)


def attend(qkv, source, slope, segments):
    nc, depth, rows = qkv.shape
    length = nc * rows
    smem = pl.BlockSpec(memory_space=pltpu.SMEM)
    return pl.pallas_call(
        partial(attend_kernel, rows // BLK),
        in_specs=[smem, smem, whole(), whole()],
        out_specs=[whole(), whole()],
        out_shape=[shaped((nc, HD, rows), BF), shaped((1, length), F32)],
        scratch_shapes=[pltpu.VMEM((3 * HD, length), BF), pltpu.VMEM((length, BLK), F32)],
        **params(length * RUN_BLOCKS * BLK * HD * 3, length * HD * 8, length * RUN_BLOCKS * BLK // 2),
    )(source, slope, segments, qkv)


def attend_back_kernel(
    per_device, src_ref, slope_ref, seg_ref, qkv_ref, g_ref, lse_ref, out_ref, stream_ref, grad_ref, column_ref, k_acc, v_acc
):
    gather_blocks(qkv_ref, src_ref, stream_ref, per_device)
    gather_blocks(g_ref, src_ref, grad_ref, per_device)
    segment_columns(seg_ref, column_ref)
    slope = slope_ref[0]
    run = RUN_BLOCKS * BLK
    scale = HD**-0.5
    for base in range(0, stream_ref.shape[1], run):
        rows = slice(base, base + run)
        keys_turned = stream_ref[HD : 2 * HD, rows]
        keys = keys_turned.T
        values = stream_ref[2 * HD :, rows].T
        queries_rows = stream_ref[:HD, rows].T
        grads_rows = grad_ref[:, rows].T
        for first in range(base + run - QB, base - 1, -QB):
            last = first + QB
            depth = last - base
            inner = slice(first - base, last - base)
            queries = stream_ref[:HD, first:last] * jnp.asarray(scale, BF)
            scores, allowed = score_tile(
                keys[:depth], queries, column_ref, seg_ref, slope, base, first, last
            )
            weights = jnp.where(allowed, jnp.exp(scores - lse_ref[:, first:last]), 0.0)
            back = dot(values[:depth], grad_ref[:, first:last])
            delta = jnp.sum(weights * back, axis=0, keepdims=True)
            low = (weights * (back - delta)).astype(BF)
            v_piece = dot(weights.astype(BF), grads_rows[inner])
            k_piece = dot(low, queries_rows[inner])
            if depth == run:
                v_acc[...] = v_piece
                k_acc[...] = k_piece
            else:
                v_acc[:depth, :] += v_piece
                k_acc[:depth, :] += k_piece
            q_grad = (dot(keys_turned[:, :depth], low) * scale).astype(BF)
            scatter_blocks(out_ref, src_ref, q_grad, per_device, 0, first // BLK)
        scatter_blocks(out_ref, src_ref, (k_acc[...] * scale).T.astype(BF), per_device, HD, base // BLK)
        scatter_blocks(out_ref, src_ref, v_acc[...].T.astype(BF), per_device, 2 * HD, base // BLK)


def attend_backward(qkv, grads, lse, source, slope, segments):
    nc, depth, rows = qkv.shape
    length = nc * rows
    run = RUN_BLOCKS * BLK
    smem = pl.BlockSpec(memory_space=pltpu.SMEM)
    return pl.pallas_call(
        partial(attend_back_kernel, rows // BLK),
        in_specs=[smem, smem, whole(), whole(), whole(), whole()],
        out_specs=whole(),
        out_shape=shaped((nc, depth, rows), BF),
        scratch_shapes=[
            pltpu.VMEM((3 * HD, length), BF),
            pltpu.VMEM((HD, length), BF),
            pltpu.VMEM((length, BLK), F32),
            pltpu.VMEM((run, HD), F32),
            pltpu.VMEM((run, HD), F32),
        ],
        **params(length * run * HD * 7, length * HD * 16, length * run // 2),
    )(source, slope, segments, qkv, grads, lse)


def on_device(
    nf,
    nc,
    nt,
    tokens,
    cotangent,
    block_place,
    segment_ids,
    qkv_weight,
    out_weight,
    up_weight,
    down_weight,
    query_value_bias,
    up_bias,
    norm_gains,
    row_biases,
):
    rows, width = tokens.shape
    half = rows // 2
    depth = qkv_weight.shape[1]
    local = qkv_weight.shape[3]
    heads = local // HD
    hidden = up_weight.shape[2]
    span = nc * depth
    y_index = lax.axis_index("fsdp")
    z_index = lax.axis_index("ctx")
    t_index = lax.axis_index("tp")
    side = t_index % 2

    def swap(value, axis, size, bit):
        return lax.ppermute(value, axis, [(i, i ^ bit) for i in range(size)])

    def sibling(value):
        return swap(value, "tp", nt, 1)

    def across(value):
        return lax.all_to_all(value, "ctx", 0, 0)

    def tie(value, *others):
        return lax.optimization_barrier((value, *others))[0]

    def gather_z(shard):
        return [swap(shard, "ctx", nc, bit) for bit in range(1, nc)]

    def gather_y(shard, came, apart=False):
        pack = [shard, *came]
        for bit in range(1, nf):
            if apart:
                pack.append(swap(shard, "fsdp", nf, bit))
                pack.append(swap(jnp.concatenate(came, axis=0), "fsdp", nf, bit))
            else:
                pack.append(swap(jnp.concatenate([shard, *came], axis=0), "fsdp", nf, bit))
        return pack

    def send_y(parts):
        return [swap(parts[bit], "fsdp", nf, bit) for bit in range(1, nf)]

    def send_z(pieces):
        return [pieces[0]] + [swap(pieces[bit], "ctx", nc, bit) for bit in range(1, nc)]

    def tensor_sum(other, own):
        term = (own + sibling(other).astype(F32)).astype(BF)
        bit = 2
        while bit * 2 < nt:
            term = (term.astype(F32) + swap(term, "tp", nt, bit).astype(F32)).astype(BF)
            bit *= 2
        return term, swap(term, "tp", nt, bit)

    def columns_relative(value):
        return jnp.concatenate(
            [
                lax.dynamic_slice_in_dim(
                    value, ((y_index ^ a) * nc + (z_index ^ b)) * depth, depth, axis=1
                )
                for a in range(nf)
                for b in range(nc)
            ],
            axis=1,
        )

    def take_half(value, which):
        return lax.dynamic_slice_in_dim(value, which * half, half)

    def columns_canonical(own, oth):
        rows_all = jnp.where(
            side == 0, jnp.concatenate([own, oth], axis=0), jnp.concatenate([oth, own], axis=0)
        )
        return columns_relative(rows_all)

    per_device = rows // BLK
    count = nc * per_device
    place = block_place[0]
    stored = jnp.arange(count, dtype=jnp.int32)
    relative = (stored // per_device) * per_device + (stored % per_device + side * (per_device // 2)) % per_device
    source = jnp.sum(
        jnp.where(place[None, :] == jnp.arange(count, dtype=jnp.int32)[:, None], relative[None, :], 0), axis=1
    ).astype(jnp.int32)
    head = (t_index * heads + z_index).astype(F32)
    slope = jnp.exp2(-8.0 * (head + 1.0) / HEADS).reshape(1)
    segments = segment_ids

    def qkv_shard(layer):
        return [qkv_weight[layer, :, i, :] for i in range(3)]

    table_rows = []
    for layer in range(LAYERS):
        table_rows += [norm_gains[layer].T, row_biases[layer].T, jnp.zeros((2, depth), BF)]
    table_shard = jnp.concatenate(table_rows, axis=0)
    extra = table_shard.shape[0]
    table_padded = jnp.pad(table_shard, ((0, 0), (0, 3 * local - depth)))
    first_shard = jnp.concatenate([jnp.concatenate(qkv_shard(0), axis=1), table_padded], axis=0)
    first_z = gather_z(first_shard)
    first_pack = gather_y(first_shard, first_z, apart=True)
    table = jnp.concatenate(
        [
            ref[start + depth : start + depth + extra, :depth]
            for ref in first_pack
            for start in range(0, ref.shape[0], depth + extra)
        ],
        axis=1,
    ).astype(F32)

    biases = [
        jnp.stack([query_value_bias[l, 0], jnp.zeros((local,), BF), query_value_bias[l, 1]]).astype(F32)
        for l in range(LAYERS)
    ]
    up_biases = [up_bias[l].astype(F32).reshape(1, hidden) for l in range(LAYERS)]

    x_all = columns_relative(tokens)
    x_half = take_half(x_all, side)
    n_own = norm_stats(x_half.astype(F32))[0]
    n_oth = norm_stats(take_half(x_all, 1 - side).astype(F32))[0]
    h_own, h_oth, qkv_sent = first_qkv(n_own, n_oth, table, 0, biases[0], first_pack, depth, extra)

    out_up_shard = tie(jnp.concatenate([out_weight[0], up_weight[0]], axis=1), *first_z)
    out_up_z = gather_z(out_up_shard)
    out_up = gather_y(out_up_shard, out_up_z)
    out_packs, up_packs, down_packs, qkv_packs = [(out_up, 0)], [(out_up, local)], [], [(first_pack, 0, extra)]

    records = []
    last_other = last_own = None
    for l in range(LAYERS):
        row = l * NORM_ROWS
        qkv = across(qkv_sent)
        if l == 0:
            down_shard = tie(down_weight[0], qkv, *out_up_z)
            down_z = gather_z(down_shard)
            down_packs.append((gather_y(down_shard, down_z), 0))
            next_shard = tie(jnp.concatenate([out_weight[1], *qkv_shard(1)], axis=1), *down_z)
            next_z = gather_z(next_shard)
            next_pack = gather_y(next_shard, next_z)
            out_packs.append((next_pack, 0))
            qkv_packs.append((next_pack, local, 0))
            up_shard = tie(up_weight[1], *next_z)
            up_z = gather_z(up_shard)
            up_packs.append((gather_y(up_shard, up_z), 0))
            down_shard = tie(down_weight[1], *up_z)
            down_packs.append((gather_y(down_shard, gather_z(down_shard)), 0))
        o_stream, lse = attend(qkv, source, slope, segments)
        o_rows = across(o_stream)
        other = out_project(o_rows, *out_packs[l], depth, width, half, BF)
        own = out_project(tie(o_rows, other), *out_packs[l], depth, width, 0, F32)
        a, b = tensor_sum(other, own)
        y_half, h2_own = add_norm(x_half, a, b, table, row + 3, row + 1, row + 4)
        h2_oth = sibling(h2_own)
        u, other, own = mlp_forward(h2_own, h2_oth, up_biases[l], up_packs[l], down_packs[l], depth)
        records.append((x_half, h_own, h_oth, qkv, lse, o_rows, y_half, h2_own, h2_oth, u))
        if l + 1 < LAYERS:
            a, b = tensor_sum(other, own)
            following = row + NORM_ROWS
            x_half, h_own = add_norm(y_half, a, b, table, row + 5, following, following + 2)
            h_oth = sibling(h_own)
            qkv_sent = qkv_project(h_own, h_oth, biases[l + 1], *qkv_packs[l + 1][:2], depth)
        else:
            last_other, last_own = other, own

    g_all = columns_relative(cotangent)
    gz_own, gz_oth = take_half(g_all, side), take_half(g_all, 1 - side)
    gx_half = gz_own.astype(F32)
    sums = [None] * LAYERS
    pieces = [None] * LAYERS
    waiting = None
    for l in reversed(range(LAYERS)):
        row = l * NORM_ROWS
        x_half, h_own, h_oth, qkv, lse, o_rows, y_half, h2_own, h2_oth, u = records[l]
        act, gu, up_sum, other, own = mlp_backward(gz_own, gz_oth, u, up_packs[l], down_packs[l], depth)
        a, b = tensor_sum(other, own)
        parts = mlp_grad(gz_own, gz_oth, h2_own, h2_oth, tie(act, a), gu, nf)
        mlp_came = send_y(parts)
        mlp_own = parts[0]
        b = tie(b, *parts)
        if waiting is not None:
            out_q, kv = (part_sum(tie(mine, a), came, depth) for mine, came in waiting)
            b = tie(b, *out_q, *kv)
            pieces[l + 1] = (pieces[l + 1], send_z(out_q), send_z(kv))
        gy_half, ga_own, sums_two = norm_backward(gx_half, a, b, y_half, table, row + 1)
        ga_oth = sibling(ga_own)
        g_stream = across(out_backward(ga_own, ga_oth, *out_packs[l], depth, local))
        if l == LAYERS - 1:
            a, b = tensor_sum(tie(last_other, g_stream), last_own)
            final_half = y_half + (a.astype(F32) + b.astype(F32) + table[row + 5])
            final_low = final_half.astype(BF)
            block_output = columns_canonical(final_low, sibling(final_low))
        g_sent = attend_backward(qkv, g_stream, lse, source, slope, segments)
        mlp_pieces = part_sum(tie(mlp_own, g_sent), mlp_came, depth)
        g_rows = tie(across(g_sent), *mlp_pieces)
        pieces[l] = send_z(mlp_pieces)
        g_proj, qkv_sum, other, own = qkv_backward(
            g_rows, qkv_packs[l][0], qkv_packs[l][1], depth, qkv_packs[l][2], width
        )
        a, b = tensor_sum(other, own)
        out_q_parts = out_q_grad(ga_own, ga_oth, o_rows, h_own, h_oth, tie(g_proj, a), nf)
        out_q_came = send_y(out_q_parts)
        kv_parts = kv_grad(h_own, h_oth, tie(g_proj, *out_q_parts), nf)
        kv_came = send_y(kv_parts)
        b = tie(b, *kv_parts)
        waiting = [(out_q_parts[0], out_q_came), (kv_parts[0], kv_came)]
        gx_half, gz_own, sums_one = norm_backward(gy_half, a, b, x_half, table, row)
        if l > 0:
            gz_oth = sibling(gz_own)
        sums[l] = (sums_one, sums_two, qkv_sum, up_sum)
    out_q, kv = (part_sum(mine, came, depth) for mine, came in waiting)
    pieces[0] = (pieces[0], send_z(out_q), send_z(kv))

    grad_tokens = columns_canonical(gx_half, sibling(gx_half))

    def plan(which, col, index=lambda layer: layer):
        return [(index(layer), which * LAYERS * nc + layer * nc, nc, col) for layer in range(LAYERS)]

    def weight_sums(which, plans, shapes):
        return final_sums(plans, shapes, [p for layer in range(LAYERS) for p in pieces[layer][which]])

    grad_up, grad_down = weight_sums(
        0, [plan(0, 0), plan(0, hidden)], [shaped((LAYERS, depth, hidden), F32)] * 2
    )
    out_q_all = [p for layer in range(LAYERS) for p in pieces[layer][1]]
    kv_all = [p for layer in range(LAYERS) for p in pieces[layer][2]]
    qkv_plan = []
    for i in range(3):
        which, col = (0, local) if i == 0 else (1, (i - 1) * local)
        qkv_plan += [
            ((layer, i), which * LAYERS * nc + layer * nc, nc, col) for layer in range(LAYERS)
        ]
    grad_out, grad_qkv = final_sums(
        [plan(0, 0), qkv_plan],
        [shaped((LAYERS, depth, local), F32), shaped((LAYERS, 3, depth, local), F32)],
        out_q_all + kv_all,
    )
    grad_qkv = grad_qkv.transpose(0, 2, 1, 3)

    norm_parts = []
    for l in range(LAYERS):
        one, two = sums[l][0], sums[l][1]
        norm_parts += [one[0], two[0], one[1], two[2], two[1], two[3]]
    norm_all = jnp.stack(norm_parts)
    bias_all = jnp.concatenate(
        [sums[l][2][0, :local] for l in range(LAYERS)]
        + [sums[l][2][0, 2 * local :] for l in range(LAYERS)]
        + [sums[l][3][0] for l in range(LAYERS)]
    )
    count_norm = norm_all.shape[0]
    by_part = norm_all.reshape(count_norm, nf, nc, depth).transpose(1, 2, 3, 0).reshape(nf, nc, -1)
    norm_total = by_part[0]
    bias_total = bias_all
    size = nc * depth * count_norm
    for bit in range(1, nf):
        came = swap(jnp.concatenate([by_part[bit].reshape(-1), bias_all]), "fsdp", nf, bit)
        norm_total = norm_total + came[:size].reshape(norm_total.shape)
        bias_total = bias_total + came[size:]
    norm_mine = norm_total[0]
    bias_sum = bias_total
    for bit in range(1, nc):
        came = swap(jnp.concatenate([norm_total[bit], bias_total]), "ctx", nc, bit)
        norm_mine = norm_mine + came[: depth * count_norm]
        bias_sum = bias_sum + came[depth * count_norm :]
    norm_mine = (norm_mine + sibling(norm_mine)).reshape(depth, LAYERS, count_norm // LAYERS)
    norm_mine = norm_mine.transpose(1, 0, 2)
    queries, values = bias_sum[: LAYERS * local], bias_sum[LAYERS * local : 2 * LAYERS * local]
    grad_bias = jnp.stack([queries.reshape(LAYERS, local), values.reshape(LAYERS, local)], axis=1)
    grad_up_bias = bias_sum[2 * LAYERS * local :].reshape(LAYERS, hidden)

    return (
        block_output,
        grad_tokens,
        grad_qkv,
        grad_out,
        grad_up,
        grad_down,
        grad_bias,
        grad_up_bias,
        norm_mine[:, :, :2],
        norm_mine[:, :, 2:],
    )


def solution(mesh):
    placed = (
        P(("fsdp", "ctx"), None),
        P(("fsdp", "ctx"), None),
        P("fsdp", None),
        P("fsdp", None),
        P(None, ("fsdp", "ctx"), None, "tp"),
        P(None, ("fsdp", "ctx"), "tp"),
        P(None, ("fsdp", "ctx"), "tp"),
        P(None, ("fsdp", "ctx"), "tp"),
        P(None, None, "tp"),
        P(None, "tp"),
        P(None, ("fsdp", "ctx"), None),
        P(None, ("fsdp", "ctx"), None),
    )
    return jax.shard_map(
        partial(on_device, mesh.shape["fsdp"], mesh.shape["ctx"], mesh.shape["tp"]),
        mesh=mesh,
        in_specs=placed,
        out_specs=(
            P(("fsdp", "ctx"), None),
            P(("fsdp", "ctx"), None),
            P(None, ("fsdp", "ctx"), None, "tp"),
            P(None, ("fsdp", "ctx"), "tp"),
            P(None, ("fsdp", "ctx"), "tp"),
            P(None, ("fsdp", "ctx"), "tp"),
            P(None, None, "tp"),
            P(None, "tp"),
            P(None, ("fsdp", "ctx"), None),
            P(None, ("fsdp", "ctx"), None),
        ),
        check_vma=False,
    )
```

time: 750 us -> 666 us (0.89)
  waiting for transfers between devices: 379 us -> 333 us
  Pallas kernels: 112 us -> 76.3 us
  other arithmetic: 44.6 us -> 11.8 us
  blocking collectives: 23.9 us -> 45.2 us
  local copies, waits for them, and re-layouts: 62.6 us -> 77.2 us
    all_to_all x21 -> x5, waiting for transfers between devices: 207 us -> 30.7 us  [across(): return lax.all_to_all(value, 'ctx', 0, 0)]
    ppermute x39 -> x78, waiting for transfers between devices: 172 us -> 302 us  [swap(): return lax.ppermute(value, axis, [(i, i ^ bit) for i in range(size)])]
    all_to_all x21 -> x5, starting transfers between devices: 87.7 us -> 19.5 us  [across(): return lax.all_to_all(value, 'ctx', 0, 0)]
    ppermute x39 -> x78, starting transfers between devices: 26.3 us -> 92.3 us  [swap(): return lax.ppermute(value, axis, [(i, i ^ bit) for i in range(size)])]
    pallas_call x32 -> x35, Pallas kernels: 88.6 us -> 54.3 us  [call(): pl.pallas_call(kernel, in_specs=specs, out_specs=[whole()] * len(outs) if...]
    all_to_all x1 -> x3, blocking collectives: 23.9 us -> 45.2 us  [across(): return lax.all_to_all(value, 'ctx', 0, 0)]
    unnamed x262 -> x318, local copies, waits for them, and re-layouts: 39.4 us -> 56.7 us
    convert_element_type x11 -> x3, other arithmetic: 16.4 us -> 2.27 us  [the longest x1 1.43 us: on_device(): final_low = final_half.astype(BF)]
  transfers between devices with their start and end apart: 60 -> 83, of which waited for: 42 -> 33; matrix products, arithmetic and copies ran while one was open for 7% -> 7% of each run, Pallas kernels for 11% -> 8%
where the time goes in v2:
time: 666 us; the launch traced here: 658 us
  waiting for transfers between devices  333 us (50%)
  starting transfers between devices  112 us (17%)
  local copies, waits for them, and re-layouts  77.2 us (12%)
  Pallas kernels  76.3 us (11%)
  blocking collectives  45.2 us (7%)
  other arithmetic  11.8 us (2%)
    ppermute x78, waiting for transfers between devices, swap(): return lax.ppermute(value, axis, [(i, i ^ bit) for i in range(size)])  302 us
    ppermute x78, starting transfers between devices, swap(): return lax.ppermute(value, axis, [(i, i ^ bit) for i in range(size)])  92.3 us
    unnamed x318, local copies, waits for them, and re-layouts  56.7 us
    pallas_call x35, Pallas kernels, call(): pl.pallas_call(kernel, in_specs=specs, out_specs=[whole()] * len(outs) if...  54.3 us
    all_to_all x3, blocking collectives, across(): return lax.all_to_all(value, 'ctx', 0, 0)  45.2 us
    all_to_all x5, waiting for transfers between devices, across(): return lax.all_to_all(value, 'ctx', 0, 0)  30.7 us
    all_to_all x5, starting transfers between devices, across(): return lax.all_to_all(value, 'ctx', 0, 0)  19.5 us
  transfers between devices with their start and end apart: 83, of which 33 were waited for; matrix products, arithmetic and copies ran while one was open for 7% of the time, Pallas kernels for 8%

profile of v2, /device:TPU:0, one launch (start us, length us, event | category | flops | bytes accessed | tf_op | source)
XLA Modules:
  0.0 658.2 jit_solution(13288505197785895174)
XLA Ops:
  19.6 9.4 %collective-permute-done.1.refs_2_ = bf16[144,768]{1,0:T(8,128)(2,1)S(1)} collective-permute-done((bf16[144,768]{1,0:T(8,128)(2,1)S(1)}, bf16[144,768]{1,0:T(8,128)(2,1)S(1)}, u32[]{:S(2)}, u32[]{:S(2)}) %collective-permute-start.1) | collective-permute-done | bytes 221216 | tf_op jit(solution)/shard_map/ppermute | solution.py:594
  37.1 11.5 %collective-permute-done.4.refs_5_ = bf16[432,768]{1,0:T(8,128)(2,1)S(1)} collective-permute-done((bf16[432,768]{1,0:T(8,128)(2,1)S(1)}, bf16[432,768]{1,0:T(8,128)(2,1)S(1)}, u32[]{:S(2)}, u32[]{:S(2)}) %collective-permute-start.4) | collective-permute-done | bytes 663584 | tf_op jit(solution)/shard_map/ppermute | solution.py:594
  62.2 16.0 %all-to-all-done.qkv_ref = bf16[4,192,512]{2,1,0:T(8,128)(2,1)} async-done(((bf16[4,192,512]{2,1,0:T(8,128)(2,1)}), bf16[4,192,512]{2,1,0:T(8,128)(2,1)}, u32[]{:S(2)}, u32[]{:S(2)}) %all-to-all-start) | async-done | bytes 786464 | tf_op jit(solution)/shard_map/all_to_all | solution.py:600
  108.4 13.5 %collective-permute-done.13.refs_7_ = bf16[128,1024]{1,0:T(8,128)(2,1)S(1)} collective-permute-done((bf16[128,1024]{1,0:T(8,128)(2,1)S(1)}, bf16[128,1024]{1,0:T(8,128)(2,1)S(1)}, u32[]{:S(2)}, u32[]{:S(2)}) %collective-permute-start.13) | collective-permute-done | bytes 262176 | tf_op jit(solution)/shard_map/ppermute | solution.py:594
  123.1 22.8 %collective-permute-done.15.refs_9_ = bf16[512,1024]{1,0:T(8,128)(2,1)S(1)} collective-permute-done((bf16[512,1024]{1,0:T(8,128)(2,1)S(1)}, bf16[512,1024]{1,0:T(8,128)(2,1)S(1)}, u32[]{:S(2)}, u32[]{:S(2)}) %collective-permute-start.15) | collective-permute-done | bytes 1048608 | tf_op jit(solution)/shard_map/ppermute | solution.py:594
  161.0 12.6 %collective-permute-done.20.refs_2_ = bf16[128,1024]{1,0:T(8,128)(2,1)S(1)} collective-permute-done((bf16[128,1024]{1,0:T(8,128)(2,1)S(1)}, bf16[128,1024]{1,0:T(8,128)(2,1)S(1)}, u32[]{:S(2)}, u32[]{:S(2)}) %collective-permute-start.20) | collective-permute-done | bytes 262176 | tf_op jit(solution)/shard_map/ppermute | solution.py:594
  174.9 23.7 %collective-permute-done.22.refs_4_ = bf16[512,1024]{1,0:T(8,128)(2,1)S(1)} collective-permute-done((bf16[512,1024]{1,0:T(8,128)(2,1)S(1)}, bf16[512,1024]{1,0:T(8,128)(2,1)S(1)}, u32[]{:S(2)}, u32[]{:S(2)}) %collective-permute-start.22) | collective-permute-done | bytes 1048608 | tf_op jit(solution)/shard_map/ppermute | solution.py:594
  200.4 22.5 %all_to_all.40.qkv_ref = bf16[4,192,512]{2,1,0:T(8,128)(2,1)S(1)} all-to-all(bf16[4,192,512]{2,1,0:T(8,128)(2,1)S(1)} %shard_map.202), channel_id=1, replica_groups=mesh['fsdp'=2,'ctx'=4,'tp'=4] {'ctx'}, dimensions={0} | all-to-all | bytes 1572864 | tf_op jit(solution)/shard_map/all_to_all | solution.py:600
  227.3 10.9 %all_to_all.41.o_ref = bf16[4,64,512]{2,1,0:T(8,128)(2,1)S(1)} all-to-all(bf16[4,64,512]{2,1,0:T(8,128)(2,1)S(1)} %get-tuple-element.135), channel_id=1, replica_groups=mesh['fsdp'=2,'ctx'=4,'tp'=4] {'ctx'}, dimensions={0} | all-to-all | bytes 524288 | tf_op jit(solution)/shard_map/all_to_all | solution.py:600
  249.7 14.3 %collective-permute-done.27.refs_2_ = bf16[128,1024]{1,0:T(8,128)(2,1)S(1)} collective-permute-done((bf16[128,1024]{1,0:T(8,128)(2,1)S(1)}, bf16[128,1024]{1,0:T(8,128)(2,1)S(1)}, u32[]{:S(2)}, u32[]{:S(2)}) %collective-permute-start.27) | collective-permute-done | bytes 262176 | tf_op jit(solution)/shard_map/ppermute | solution.py:594
  275.2 11.5 %collective-permute-done.31.refs_7_ = bf16[128,1024]{1,0:T(8,128)(2,1)S(1)} collective-permute-done((bf16[128,1024]{1,0:T(8,128)(2,1)S(1)}, bf16[128,1024]{1,0:T(8,128)(2,1)S(1)}, u32[]{:S(2)}, u32[]{:S(2)}) %collective-permute-start.31) | collective-permute-done | bytes 262176 | tf_op jit(solution)/shard_map/ppermute | solution.py:594
  294.7 20.2 %collective-permute-done.33.refs_9_ = bf16[512,1024]{1,0:T(8,128)(2,1)S(1)} collective-permute-done((bf16[512,1024]{1,0:T(8,128)(2,1)S(1)}, bf16[512,1024]{1,0:T(8,128)(2,1)S(1)}, u32[]{:S(2)}, u32[]{:S(2)}) %collective-permute-start.33) | collective-permute-done | bytes 1048608 | tf_op jit(solution)/shard_map/ppermute | solution.py:594
  343.3 11.8 %all_to_all.42.g_ref = bf16[4,64,512]{2,1,0:T(8,128)(2,1)S(1)} all-to-all(bf16[4,64,512]{2,1,0:T(8,128)(2,1)S(1)} %shard_map.211), channel_id=1, replica_groups=mesh['fsdp'=2,'ctx'=4,'tp'=4] {'ctx'}, dimensions={0} | all-to-all | bytes 524288 | tf_op jit(solution)/shard_map/all_to_all | solution.py:600
  366.4 22.8 %collective-permute-done.40.refs_0_ = bf16[512,2048]{1,0:T(8,128)(2,1)} collective-permute-done((bf16[512,2048]{1,0:T(8,128)(2,1)}, bf16[512,2048]{1,0:T(8,128)(2,1)}, u32[]{:S(2)}, u32[]{:S(2)}) %collective-permute-start.40) | collective-permute-done | bytes 2097184 | tf_op jit(solution)/shard_map/ppermute | solution.py:594
  405.3 10.8 %collective-permute-done.42.b_ref = bf16[256,1024]{1,0:T(8,128)(2,1)S(1)} collective-permute-done((bf16[256,1024]{1,0:T(8,128)(2,1)S(1)}, bf16[256,1024]{1,0:T(8,128)(2,1)S(1)}, u32[]{:S(2)}, u32[]{:S(2)}) %collective-permute-start.42) | collective-permute-done | bytes 524320 | tf_op jit(solution)/shard_map/ppermute | solution.py:594
  427.3 11.0 %collective-permute-done.47.refs_0_ = bf16[512,512]{1,0:T(8,128)(2,1)S(1)} collective-permute-done((bf16[512,512]{1,0:T(8,128)(2,1)S(1)}, bf16[512,512]{1,0:T(8,128)(2,1)S(1)}, u32[]{:S(2)}, u32[]{:S(2)}) %collective-permute-start.47) | collective-permute-done | bytes 524320 | tf_op jit(solution)/shard_map/ppermute | solution.py:594
  439.6 9.3 %collective-permute-done.46.refs_0_ = bf16[512,512]{1,0:T(8,128)(2,1)S(1)} collective-permute-done((bf16[512,512]{1,0:T(8,128)(2,1)S(1)}, bf16[512,512]{1,0:T(8,128)(2,1)S(1)}, u32[]{:S(2)}, u32[]{:S(2)}) %collective-permute-start.46) | collective-permute-done | bytes 524320 | tf_op jit(solution)/shard_map/ppermute | solution.py:594
  467.3 8.5 %all-to-all-done.6.g_ref = bf16[4,64,512]{2,1,0:T(8,128)(2,1)S(1)} async-done(((bf16[4,64,512]{2,1,0:T(8,128)(2,1)}), bf16[4,64,512]{2,1,0:T(8,128)(2,1)S(1)}, u32[]{:S(2)}, u32[]{:S(2)}) %all-to-all-start.6) | async-done | bytes 262176 | tf_op jit(solution)/shard_map/all_to_all | solution.py:600
  475.8 6.7 %shard_map.224 = bf16[4,192,512]{2,1,0:T(8,128)(2,1)S(1)} custom-call(s32[16]{0:T(128)S(1)} %select_reduce_fusion.src_ref, f32[1]{0:T(128)} %bitcast.1.slope_ref, s32[1,2048]{1,0:T(1,128)S(1)} %copy-done.114, bf16[4,192,512]{2,1,0:T(8,128)(2,1)} %all-to-all-done.qkv_ref, bf16[4,64,512]{2,1,0:T(8,128)(2,1)S(1)} %all-to-all-done.6.g_ref, f32[1,2048]{1,0:T(1,128)S(1)} %copy-done.122), custom_call_target="tpu_custom_call" | custom-call | flops 939524096 | bytes 2097152 | tf_op jit(solution)/shard_map/pallas_call | solution.py:548
  495.0 11.3 %collective-permute-done.49.refs_0_ = bf16[512,2048]{1,0:T(8,128)(2,1)} collective-permute-done((bf16[512,2048]{1,0:T(8,128)(2,1)}, bf16[512,2048]{1,0:T(8,128)(2,1)}, u32[]{:S(2)}, u32[]{:S(2)}) %collective-permute-start.49) | collective-permute-done | bytes 2097184 | tf_op jit(solution)/shard_map/ppermute | solution.py:594
  527.9 9.9 %collective-permute-done.51.b_ref = bf16[256,1024]{1,0:T(8,128)(2,1)S(1)} collective-permute-done((bf16[256,1024]{1,0:T(8,128)(2,1)S(1)}, bf16[256,1024]{1,0:T(8,128)(2,1)S(1)}, u32[]{:S(2)}, u32[]{:S(2)}) %collective-permute-start.51) | collective-permute-done | bytes 524320 | tf_op jit(solution)/shard_map/ppermute | solution.py:594
  553.7 31.8 %collective-permute-done.68.refs_2_ = bf16[128,2048]{1,0:T(8,128)(2,1)} collective-permute-done((bf16[128,2048]{1,0:T(8,128)(2,1)}, bf16[128,2048]{1,0:T(8,128)(2,1)}, u32[]{:S(2)}, u32[]{:S(2)}) %collective-permute-start.68) | collective-permute-done | bytes 524320 | tf_op jit(solution)/shard_map/ppermute | solution.py:594
  585.5 10.7 %collective-permute-start.74 = (f32[4608]{0:T(1024)S(1)}, f32[4608]{0:T(1024)S(1)}, u32[]{:S(2)}, u32[]{:S(2)}) collective-permute-start(f32[4608]{0:T(1024)S(1)} %get-tuple-element.294), channel_id=1, source_target_pairs={{0,4},{4,0},{8,12},{12,8},{1,5},{5,1},{9,13},{13,9},{2,6},{6,2},{1... | collective-permute-start | bytes 55304 | tf_op jit(solution)/shard_map/ppermute | solution.py:594
  612.9 8.2 %collective-permute-done.58.refs_6_ = bf16[128,512]{1,0:T(8,128)(2,1)S(1)} collective-permute-done((bf16[128,512]{1,0:T(8,128)(2,1)S(1)}, bf16[128,512]{1,0:T(8,128)(2,1)S(1)}, u32[]{:S(2)}, u32[]{:S(2)}) %collective-permute-start.58) | collective-permute-done | bytes 131104 | tf_op jit(solution)/shard_map/ppermute | solution.py:594
  (581 shorter events, 314.0 us)
Async XLA Ops:
  3.9 32.0 %collective-permute-start.3 = (bf16[144,768]{1,0:T(8,128)(2,1)S(1)}, bf16[144,768]{1,0:T(8,128)(2,1)}, u32[]{:S(2)}, u32[]{:S(2)}) collective-permute-start(bf16[144,768]{1,0:T(8,128)(2,1)S(1)} %fusion.7.refs_0_), channel_id=1, source_target_pairs={{0,16},{16,0},{1,17},{17,1},{2,18},{18,2},{3,19},{19,3},{4,20},{20... | collective-permute-start | bytes 663560 | tf_op jit(solution)/shard_map/ppermute | solution.py:594
  29.0 31.1 %collective-permute-start.7 = (bf16[128,1280]{1,0:T(8,128)(2,1)S(1)}, bf16[128,1280]{1,0:T(8,128)(2,1)S(1)}, u32[]{:S(2)}, u32[]{:S(2)}) collective-permute-start(bf16[128,1280]{1,0:T(8,128)(2,1)S(1)} %pad_maximum_fusion.6.refs_0_), channel_id=1, source_target_pairs={{0,12},{4,8},{8,4},{12,0},{1,13},{5,9},{9,5},{13,1},{2,14},{6,10},... | collective-permute-start | bytes 983048 | tf_op jit(solution)/shard_map/ppermute | solution.py:594
  31.8 28.4 %collective-permute-start.6 = (bf16[128,1280]{1,0:T(8,128)(2,1)S(1)}, bf16[128,1280]{1,0:T(8,128)(2,1)S(1)}, u32[]{:S(2)}, u32[]{:S(2)}) collective-permute-start(bf16[128,1280]{1,0:T(8,128)(2,1)S(1)} %pad_maximum_fusion.6.refs_0_), channel_id=1, source_target_pairs={{0,8},{4,12},{8,0},{12,4},{1,9},{5,13},{9,1},{13,5},{2,10},{6,14},... | collective-permute-start | bytes 983048 | tf_op jit(solution)/shard_map/ppermute | solution.py:594
  31.8 28.4 %collective-permute-start.5 = (bf16[128,1280]{1,0:T(8,128)(2,1)S(1)}, bf16[128,1280]{1,0:T(8,128)(2,1)S(1)}, u32[]{:S(2)}, u32[]{:S(2)}) collective-permute-start(bf16[128,1280]{1,0:T(8,128)(2,1)S(1)} %pad_maximum_fusion.6.refs_0_), channel_id=1, source_target_pairs={{0,4},{4,0},{8,12},{12,8},{1,5},{5,1},{9,13},{13,9},{2,6},{6,2},{1... | collective-permute-start | bytes 983048 | tf_op jit(solution)/shard_map/ppermute | solution.py:594
  61.5 28.2 %collective-permute-start.8 = (bf16[512,1280]{1,0:T(8,128)(2,1)}, bf16[512,1280]{1,0:T(8,128)(2,1)S(1)}, u32[]{:S(2)}, u32[]{:S(2)}) collective-permute-start(bf16[512,1280]{1,0:T(8,128)(2,1)} %pad_maximum_fusion), channel_id=1, source_target_pairs={{0,16},{16,0},{1,17},{17,1},{2,18},{18,2},{3,19},{19,3},{4,20},{20... | collective-permute-start | bytes 3932168 | tf_op jit(solution)/shard_map/ppermute | solution.py:594
  238.5 30.9 %collective-permute-start.23 = (bf16[256,1024]{1,0:T(8,128)(2,1)S(1)}, bf16[256,1024]{1,0:T(8,128)(2,1)S(1)}, u32[]{:S(2)}, u32[]{:S(2)}) collective-permute-start(bf16[256,1024]{1,0:T(8,128)(2,1)S(1)} %shard_map.204), channel_id=1, source_target_pairs={{0,1},{1,0},{2,3},{3,2},{4,5},{5,4},{6,7},{7,6},{8,9},{9,8},{10,11... | collective-permute-start | bytes 1572872 | tf_op jit(solution)/shard_map/ppermute | solution.py:594
  286.7 28.2 %collective-permute-start.33 = (bf16[512,1024]{1,0:T(8,128)(2,1)S(1)}, bf16[512,1024]{1,0:T(8,128)(2,1)S(1)}, u32[]{:S(2)}, u32[]{:S(2)}) collective-permute-start(bf16[512,1024]{1,0:T(8,128)(2,1)S(1)} %pad_maximum_fusion.4), channel_id=1, source_target_pairs={{0,16},{16,0},{1,17},{17,1},{2,18},{18,2},{3,19},{19,3},{4,20},{20... | collective-permute-start | bytes 3145736 | tf_op jit(solution)/shard_map/ppermute | solution.py:594
  288.0 26.9 %collective-permute-start.25 = (bf16[256,1024]{1,0:T(8,128)(2,1)S(1)}, bf16[256,1024]{1,0:T(8,128)(2,1)S(1)}, u32[]{:S(2)}, u32[]{:S(2)}) collective-permute-start(bf16[256,1024]{1,0:T(8,128)(2,1)S(1)} %get-tuple-element.138.h_own), channel_id=1, source_target_pairs={{0,1},{1,0},{2,3},{3,2},{4,5},{5,4},{6,7},{7,6},{8,9},{9,8},{10,11... | collective-permute-start | bytes 1572872 | tf_op jit(solution)/shard_map/ppermute | solution.py:594
  340.9 48.4 %collective-permute-start.40 = (bf16[512,2048]{1,0:T(8,128)(2,1)}, bf16[512,2048]{1,0:T(8,128)(2,1)}, u32[]{:S(2)}, u32[]{:S(2)}) collective-permute-start(bf16[512,2048]{1,0:T(8,128)(2,1)} %get-tuple-element.150), channel_id=1, source_target_pairs={{0,16},{16,0},{1,17},{17,1},{2,18},{18,2},{3,19},{19,3},{4,20},{20... | collective-permute-start | bytes 6291464 | tf_op jit(solution)/shard_map/ppermute | solution.py:594
  362.0 32.7 %all-to-all-start.5 = ((bf16[4,192,512]{2,1,0:T(8,128)(2,1)}), bf16[4,192,512]{2,1,0:T(8,128)(2,1)}, u32[]{:S(2)}, u32[]{:S(2)}) async-start(bf16[4,192,512]{2,1,0:T(8,128)(2,1)} %copy-done.63), calls=%async_computation.5 | async-start | bytes 1572864 | tf_op jit(solution)/shard_map/all_to_all | solution.py:600
  425.7 31.1 %collective-permute-start.45 = (bf16[256,1024]{1,0:T(8,128)(2,1)S(1)}, bf16[256,1024]{1,0:T(8,128)(2,1)S(1)}, u32[]{:S(2)}, u32[]{:S(2)}) collective-permute-start(bf16[256,1024]{1,0:T(8,128)(2,1)S(1)} %add_convert_fusion.1.a_ref), channel_id=1, source_target_pairs={{0,2},{1,3},{2,0},{3,1},{4,6},{5,7},{6,4},{7,5},{8,10},{9,11},{10,... | collective-permute-start | bytes 1572872 | tf_op jit(solution)/shard_map/ppermute | solution.py:594
  427.3 31.3 %collective-permute-start.37 = (bf16[256,1024]{1,0:T(8,128)(2,1)S(1)}, bf16[256,1024]{1,0:T(8,128)(2,1)S(1)}, u32[]{:S(2)}, u32[]{:S(2)}) collective-permute-start(bf16[256,1024]{1,0:T(8,128)(2,1)S(1)} %copy-done.98), channel_id=1, source_target_pairs={{0,1},{1,0},{2,3},{3,2},{4,5},{5,4},{6,7},{7,6},{8,9},{9,8},{10,11... | collective-permute-start | bytes 1572872 | tf_op jit(solution)/shard_map/ppermute | solution.py:594
  457.9 48.4 %collective-permute-start.49 = (bf16[512,2048]{1,0:T(8,128)(2,1)}, bf16[512,2048]{1,0:T(8,128)(2,1)}, u32[]{:S(2)}, u32[]{:S(2)}) collective-permute-start(bf16[512,2048]{1,0:T(8,128)(2,1)} %get-tuple-element.181), channel_id=1, source_target_pairs={{0,16},{16,0},{1,17},{17,1},{2,18},{18,2},{3,19},{19,3},{4,20},{20... | collective-permute-start | bytes 6291464 | tf_op jit(solution)/shard_map/ppermute | solution.py:594
  459.5 27.5 %collective-permute-start.38 = (bf16[256,1024]{1,0:T(8,128)(2,1)}, bf16[256,1024]{1,0:T(8,128)(2,1)}, u32[]{:S(2)}, u32[]{:S(2)}) collective-permute-start(bf16[256,1024]{1,0:T(8,128)(2,1)} %add_convert_fusion.4), channel_id=1, source_target_pairs={{0,2},{1,3},{2,0},{3,1},{4,6},{5,7},{6,4},{7,5},{8,10},{9,11},{10,... | collective-permute-start | bytes 1572872 | tf_op jit(solution)/shard_map/ppermute | solution.py:594
  483.4 29.1 %all-to-all-start.7 = ((bf16[4,192,512]{2,1,0:T(8,128)(2,1)}), bf16[4,192,512]{2,1,0:T(8,128)(2,1)S(1)}, u32[]{:S(2)}, u32[]{:S(2)}) async-start(bf16[4,192,512]{2,1,0:T(8,128)(2,1)} %copy-done.61), calls=%async_computation.7 | async-start | bytes 1572864 | tf_op jit(solution)/shard_map/all_to_all | solution.py:600
  488.6 55.6 %collective-permute-start.70 = (bf16[128,2048]{1,0:T(8,128)(2,1)}, bf16[128,2048]{1,0:T(8,128)(2,1)}, u32[]{:S(2)}, u32[]{:S(2)}) collective-permute-start(bf16[128,2048]{1,0:T(8,128)(2,1)} %get-tuple-element.158), channel_id=1, source_target_pairs={{0,4},{4,0},{8,12},{12,8},{1,5},{5,1},{9,13},{13,9},{2,6},{6,2},{1... | collective-permute-start | bytes 1572872 | tf_op jit(solution)/shard_map/ppermute | solution.py:594
  490.6 55.8 %collective-permute-start.71 = (bf16[128,2048]{1,0:T(8,128)(2,1)}, bf16[128,2048]{1,0:T(8,128)(2,1)}, u32[]{:S(2)}, u32[]{:S(2)}) collective-permute-start(bf16[128,2048]{1,0:T(8,128)(2,1)} %get-tuple-element.159), channel_id=1, source_target_pairs={{0,8},{4,12},{8,0},{12,4},{1,9},{5,13},{9,1},{13,5},{2,10},{6,14},... | collective-permute-start | bytes 1572872 | tf_op jit(solution)/shard_map/ppermute | solution.py:594
  493.0 55.7 %collective-permute-start.72 = (bf16[128,2048]{1,0:T(8,128)(2,1)}, bf16[128,2048]{1,0:T(8,128)(2,1)}, u32[]{:S(2)}, u32[]{:S(2)}) collective-permute-start(bf16[128,2048]{1,0:T(8,128)(2,1)} %get-tuple-element.160), channel_id=1, source_target_pairs={{0,12},{4,8},{8,4},{12,0},{1,13},{5,9},{9,5},{13,1},{2,14},{6,10},... | collective-permute-start | bytes 1572872 | tf_op jit(solution)/shard_map/ppermute | solution.py:594
  525.2 28.4 %collective-permute-start.67 = (bf16[128,2048]{1,0:T(8,128)(2,1)}, bf16[128,2048]{1,0:T(8,128)(2,1)}, u32[]{:S(2)}, u32[]{:S(2)}) collective-permute-start(bf16[128,2048]{1,0:T(8,128)(2,1)} %get-tuple-element.199), channel_id=1, source_target_pairs={{0,4},{4,0},{8,12},{12,8},{1,5},{5,1},{9,13},{13,9},{2,6},{6,2},{1... | collective-permute-start | bytes 1572872 | tf_op jit(solution)/shard_map/ppermute | solution.py:594
  537.8 47.6 %collective-permute-start.68 = (bf16[128,2048]{1,0:T(8,128)(2,1)}, bf16[128,2048]{1,0:T(8,128)(2,1)}, u32[]{:S(2)}, u32[]{:S(2)}) collective-permute-start(bf16[128,2048]{1,0:T(8,128)(2,1)} %get-tuple-element.200), channel_id=1, source_target_pairs={{0,8},{4,12},{8,0},{12,4},{1,9},{5,13},{9,1},{13,5},{2,10},{6,14},... | collective-permute-start | bytes 1572872 | tf_op jit(solution)/shard_map/ppermute | solution.py:594
  546.4 39.1 %collective-permute-start.69 = (bf16[128,2048]{1,0:T(8,128)(2,1)}, bf16[128,2048]{1,0:T(8,128)(2,1)}, u32[]{:S(2)}, u32[]{:S(2)}) collective-permute-start(bf16[128,2048]{1,0:T(8,128)(2,1)} %copy-done.96), channel_id=1, source_target_pairs={{0,12},{4,8},{8,4},{12,0},{1,13},{5,9},{9,5},{13,1},{2,14},{6,10},... | collective-permute-start | bytes 1572872 | tf_op jit(solution)/shard_map/ppermute | solution.py:594
  548.7 47.4 %collective-permute-start.60 = (bf16[512,512]{1,0:T(8,128)(2,1)}, bf16[512,512]{1,0:T(8,128)(2,1)}, u32[]{:S(2)}, u32[]{:S(2)}) collective-permute-start(bf16[512,512]{1,0:T(8,128)(2,1)} %copy-done.100), channel_id=1, source_target_pairs={{0,16},{16,0},{1,17},{17,1},{2,18},{18,2},{3,19},{19,3},{4,20},{20... | collective-permute-start | bytes 1572872 | tf_op jit(solution)/shard_map/ppermute | solution.py:594
  550.3 45.9 %collective-permute-start.53 = (bf16[512,512]{1,0:T(8,128)(2,1)}, bf16[512,512]{1,0:T(8,128)(2,1)}, u32[]{:S(2)}, u32[]{:S(2)}) collective-permute-start(bf16[512,512]{1,0:T(8,128)(2,1)} %copy-done.99), channel_id=1, source_target_pairs={{0,16},{16,0},{1,17},{17,1},{2,18},{18,2},{3,19},{19,3},{4,20},{20... | collective-permute-start | bytes 1572872 | tf_op jit(solution)/shard_map/ppermute | solution.py:594
  553.5 100.9 %collective-permute-start.52 = (f32[256,1024]{1,0:T(8,128)S(1)}, f32[256,1024]{1,0:T(8,128)}, u32[]{:S(2)}, u32[]{:S(2)}) collective-permute-start(f32[256,1024]{1,0:T(8,128)S(1)} %get-tuple-element.215), channel_id=1, source_target_pairs={{0,1},{1,0},{2,3},{3,2},{4,5},{5,4},{6,7},{7,6},{8,9},{9,8},{10,11... | collective-permute-start | bytes 3145736 | tf_op jit(solution)/shard_map/ppermute | solution.py:594
  (197 other events, 3237.9 us)

commit v3 on v2

--- a/solution.py
+++ b/solution.py
@@ -46,8 +46,14 @@
     )
 
 
-def rows_of(refs, col, cols, depth, extra=0):
+def rows_of(order, refs, col, cols, depth, extra=0):
     pieces = []
+    if all(ref.shape == refs[0].shape for ref in refs):
+        held = refs[0].shape[0] // depth
+        for number in range(order.shape[0]):
+            start = pl.multiple_of(lax.rem(order[number], held) * depth, depth)
+            pieces.append(refs[number // held][pl.ds(start, depth), col : col + cols])
+        return jnp.concatenate(pieces, axis=0)
     for ref in refs:
         for start in range(0, ref.shape[0], depth + extra):
             pieces.append(ref[start : start + depth, col : col + cols])
@@ -111,37 +117,38 @@
         out_ref[j, row : row + HD, number * half : (number + 1) * half] = turned[j * HD : (j + 1) * HD, :]
 
 
-def qkv_rows(h_refs, bias_ref, w_refs, out_ref, col, depth, extra):
+def qkv_rows(order, h_refs, bias_ref, w_refs, out_ref, col, depth, extra):
     local = out_ref.shape[0] * HD
     h = jnp.concatenate([h_ref[...] for h_ref in h_refs], axis=0)
     for i in range(3):
-        weights = rows_of(w_refs, col + i * local, local, depth, extra)
+        weights = rows_of(order, w_refs, col + i * local, local, depth, extra)
         heads_out(out_ref, dot(h, weights) + bias_ref[i : i + 1, :], 0, i * HD)
 
 
-def qkv_kernel(col, depth, h_own, h_oth, bias_ref, *refs):
-    qkv_rows([h_own, h_oth], bias_ref, refs[:-1], refs[-1], col, depth, 0)
-
-
-def qkv_project(h_own, h_oth, bias, pack, col, depth):
+def qkv_kernel(col, depth, order, h_own, h_oth, bias_ref, *refs):
+    qkv_rows(order, [h_own, h_oth], bias_ref, refs[:-1], refs[-1], col, depth, 0)
+
+
+def qkv_project(order, h_own, h_oth, bias, pack, col, depth):
     half, width = h_own.shape
     local = bias.shape[1]
     return call(
         partial(qkv_kernel, col, depth),
         shaped((local // HD, 3 * HD, 2 * half), BF),
-        [h_own, h_oth, bias, *pack],
+        [order, h_own, h_oth, bias, *pack],
         12 * half * width * local,
-    )
-
-
-def first_qkv_kernel(row, depth, extra, n_own, n_oth, table_ref, bias_ref, *refs):
+        smem=1,
+    )
+
+
+def first_qkv_kernel(row, depth, extra, order, n_own, n_oth, table_ref, bias_ref, *refs):
     w_refs, (h_own, h_oth, out_ref) = refs[:-3], refs[-3:]
     for n_ref, h_ref in ((n_own, h_own), (n_oth, h_oth)):
         h_ref[...] = (n_ref[...] * table_ref[row : row + 1, :] + table_ref[row + 2 : row + 3, :]).astype(BF)
-    qkv_rows([h_own, h_oth], bias_ref, w_refs, out_ref, 0, depth, extra)
-
-
-def first_qkv(n_own, n_oth, table, row, bias, pack, depth, extra):
+    qkv_rows(order, [h_own, h_oth], bias_ref, w_refs, out_ref, 0, depth, extra)
+
+
+def first_qkv(order, n_own, n_oth, table, row, bias, pack, depth, extra):
     half, width = n_own.shape
     local = bias.shape[1]
     return call(
@@ -151,46 +158,48 @@
             shaped((half, width), BF),
             shaped((local // HD, 3 * HD, 2 * half), BF),
         ],
-        [n_own, n_oth, table, bias, *pack],
+        [order, n_own, n_oth, table, bias, *pack],
         12 * half * width * local,
-    )
-
-
-def out_kernel(col, depth, start, o_ref, *refs):
+        smem=1,
+    )
+
+
+def out_kernel(col, depth, start, order, o_ref, *refs):
     w_refs, out_ref = refs[:-1], refs[-1]
     half = out_ref.shape[0]
     heads = o_ref.shape[0]
     o = jnp.concatenate([o_ref[j, :, start : start + half] for j in range(heads)], axis=0).T
-    weights = rows_of(w_refs, col, heads * HD, depth)
+    weights = rows_of(order, w_refs, col, heads * HD, depth)
     out_ref[...] = dot(o, weights, NT).astype(out_ref.dtype)
 
 
-def out_project(o_rows, pack, col, depth, width, start, dtype):
+def out_project(order, o_rows, pack, col, depth, width, start, dtype):
     heads, _, rows = o_rows.shape
     half = rows // 2
     return call(
         partial(out_kernel, col, depth, start),
         shaped((half, width), dtype),
-        [o_rows, *pack],
+        [order, o_rows, *pack],
         2 * half * width * heads * HD,
-    )
-
-
-def mlp_kernel(counts, up_col, down_col, depth, h_own, h_oth, bias_ref, *refs):
+        smem=1,
+    )
+
+
+def mlp_kernel(counts, up_col, down_col, depth, order, h_own, h_oth, bias_ref, *refs):
     ups, downs = refs[: counts[0]], refs[counts[0] : counts[0] + counts[1]]
     u_ref, oth_ref, own_ref = refs[counts[0] + counts[1] :]
     half = h_own.shape[0]
     hidden = u_ref.shape[1]
     h = jnp.concatenate([h_own[...], h_oth[...]], axis=0)
-    u = dot(h, rows_of(ups, up_col, hidden, depth)) + bias_ref[...]
+    u = dot(h, rows_of(order, ups, up_col, hidden, depth)) + bias_ref[...]
     u_ref[...] = u
     act = (0.5 * u * (1.0 + gelu_parts(u))).astype(BF)
-    total = dot(act, rows_of(downs, down_col, hidden, depth), NT)
+    total = dot(act, rows_of(order, downs, down_col, hidden, depth), NT)
     own_ref[...] = total[:half, :]
     oth_ref[...] = total[half:, :].astype(BF)
 
 
-def mlp_forward(h_own, h_oth, bias, up, down, depth):
+def mlp_forward(order, h_own, h_oth, bias, up, down, depth):
     half, width = h_own.shape
     hidden = bias.shape[1]
     return call(
@@ -200,19 +209,20 @@
             shaped((half, width), BF),
             shaped((half, width), F32),
         ],
-        [h_own, h_oth, bias, *up[0], *down[0]],
+        [order, h_own, h_oth, bias, *up[0], *down[0]],
         8 * half * width * hidden,
         transcendentals=2 * half * hidden,
-    )
-
-
-def mlp_back_kernel(counts, up_col, down_col, depth, g_own, g_oth, u_ref, *refs):
+        smem=1,
+    )
+
+
+def mlp_back_kernel(counts, up_col, down_col, depth, order, g_own, g_oth, u_ref, *refs):
     ups, downs = refs[: counts[0]], refs[counts[0] : counts[0] + counts[1]]
     act_ref, gu_ref, sum_ref, oth_ref, own_ref = refs[counts[0] + counts[1] :]
     half = g_own.shape[0]
     hidden = u_ref.shape[1]
     g = jnp.concatenate([g_own[...], g_oth[...]], axis=0)
-    grad = dot(g, rows_of(downs, down_col, hidden, depth))
+    grad = dot(g, rows_of(order, downs, down_col, hidden, depth))
     u = u_ref[...]
     t = gelu_parts(u)
     act_ref[...] = (0.5 * u * (1.0 + t)).astype(BF)
@@ -220,12 +230,12 @@
     gu = (grad * slope).astype(BF)
     gu_ref[...] = gu
     sum_ref[...] = jnp.sum(gu.astype(F32), axis=0, keepdims=True)
-    total = dot(gu, rows_of(ups, up_col, hidden, depth), NT)
+    total = dot(gu, rows_of(order, ups, up_col, hidden, depth), NT)
     own_ref[...] = total[:half, :]
     oth_ref[...] = total[half:, :].astype(BF)
 
 
-def mlp_backward(g_own, g_oth, u, up, down, depth):
+def mlp_backward(order, g_own, g_oth, u, up, down, depth):
     half, width = g_own.shape
     hidden = u.shape[1]
     return call(
@@ -237,105 +247,106 @@
             shaped((half, width), BF),
             shaped((half, width), F32),
         ],
-        [g_own, g_oth, u, *up[0], *down[0]],
+        [order, g_own, g_oth, u, *up[0], *down[0]],
         8 * half * width * hidden,
         transcendentals=2 * half * hidden,
-    )
-
-
-def grads_out(out_refs, total, col):
+        smem=1,
+    )
+
+
+def grads_out(order, out_refs, total, col):
+    cols = slice(col, col + total.shape[1])
+    if len(out_refs) == 1:
+        depth = total.shape[0] // order.shape[0]
+        for number in range(order.shape[0]):
+            start = pl.multiple_of(order[number] * depth, depth)
+            out_refs[0][pl.ds(start, depth), cols] = total[number * depth : (number + 1) * depth].astype(BF)
+        return
     span = out_refs[0].shape[0]
     for y, out_ref in enumerate(out_refs):
-        out_ref[:, col : col + total.shape[1]] = total[y * span : (y + 1) * span].astype(BF)
-
-
-def mlp_grad_kernel(g_own, g_oth, h_own, h_oth, act_ref, gu_ref, *out_refs):
+        out_ref[:, cols] = total[y * span : (y + 1) * span].astype(BF)
+
+
+def mlp_grad_kernel(order, g_own, g_oth, h_own, h_oth, act_ref, gu_ref, *out_refs):
     hidden = act_ref.shape[1]
     h = jnp.concatenate([h_own[...], h_oth[...]], axis=0).T
-    grads_out(out_refs, dot(h, gu_ref[...]), 0)
+    grads_out(order, out_refs, dot(h, gu_ref[...]), 0)
     g = jnp.concatenate([g_own[...], g_oth[...]], axis=0).T
-    grads_out(out_refs, dot(g, act_ref[...]), hidden)
-
-
-def mlp_grad(g_own, g_oth, h_own, h_oth, act, gu, nf):
+    grads_out(order, out_refs, dot(g, act_ref[...]), hidden)
+
+
+def mlp_grad(order, g_own, g_oth, h_own, h_oth, act, gu, nf):
     half, width = g_own.shape
     hidden = act.shape[1]
     return call(
         mlp_grad_kernel,
         [shaped((width // nf, 2 * hidden), BF)] * nf,
-        [g_own, g_oth, h_own, h_oth, act, gu],
+        [order, g_own, g_oth, h_own, h_oth, act, gu],
         8 * half * width * hidden,
-    )
-
-
-def out_q_grad_kernel(g_own, g_oth, o_ref, h_own, h_oth, p_ref, *out_refs):
+        smem=1,
+    )
+
+
+def attention_grad_kernel(first, last, order, g_own, g_oth, o_ref, h_own, h_oth, p_ref, *out_refs):
     heads = o_ref.shape[0]
     local = heads * HD
-    g = jnp.concatenate([g_own[...], g_oth[...]], axis=0).T
-    o = jnp.concatenate([o_ref[j] for j in range(heads)], axis=0)
-    grads_out(out_refs, dot(g, o, NT), 0)
+    col = 0
+    if first == 0:
+        g = jnp.concatenate([g_own[...], g_oth[...]], axis=0).T
+        o = jnp.concatenate([o_ref[j] for j in range(heads)], axis=0)
+        grads_out(order, out_refs, dot(g, o, NT), 0)
+        col = local
     h = jnp.concatenate([h_own[...], h_oth[...]], axis=0).T
-    grads_out(out_refs, dot(h, p_ref[:, :local]), local)
-
-
-def out_q_grad(g_own, g_oth, o_rows, h_own, h_oth, g_proj, nf):
+    grads_out(order, out_refs, dot(h, p_ref[:, (max(first, 1) - 1) * local : (last - 1) * local]), col)
+
+
+def attention_grad(first, last, order, g_own, g_oth, o_rows, h_own, h_oth, g_proj, nf):
     half, width = g_own.shape
     local = o_rows.shape[0] * HD
-    return call(
-        out_q_grad_kernel,
-        [shaped((width // nf, 2 * local), BF)] * nf,
-        [g_own, g_oth, o_rows, h_own, h_oth, g_proj],
-        8 * half * width * local,
-    )
-
-
-def kv_grad_kernel(h_own, h_oth, p_ref, *out_refs):
-    local = p_ref.shape[1] // 3
-    h = jnp.concatenate([h_own[...], h_oth[...]], axis=0).T
-    grads_out(out_refs, dot(h, p_ref[:, local:]), 0)
-
-
-def kv_grad(h_own, h_oth, g_proj, nf):
-    half, width = h_own.shape
-    local = g_proj.shape[1] // 3
-    return call(
-        kv_grad_kernel,
-        [shaped((width // nf, 2 * local), BF)] * nf,
-        [h_own, h_oth, g_proj],
-        8 * half * width * local,
-    )
-
-
-def part_sum_kernel(depth, own_ref, *refs):
-    count = (len(refs) - own_ref.shape[0] // depth)
-    came, outs = refs[:count], refs[count:]
-    for number, out_ref in enumerate(outs):
+    cols = (last - first) * local
+    return call(
+        partial(attention_grad_kernel, first, last),
+        [shaped((width // nf, cols), BF)] * nf,
+        [order, g_own, g_oth, o_rows, h_own, h_oth, g_proj],
+        4 * half * width * cols,
+        smem=1,
+    )
+
+
+def part_sum_kernel(order, own_ref, *refs):
+    came, out_ref = refs[:-1], refs[-1]
+    slots, depth, _ = out_ref.shape
+    for number in range(slots):
         rows = slice(number * depth, (number + 1) * depth)
         total = own_ref[rows, :].astype(F32)
         for ref in came:
             total = total + ref[rows, :].astype(F32)
-        out_ref[...] = total.astype(out_ref.dtype)
-
-
-def part_sum(own, came, depth):
+        out_ref[lax.rem(order[number], slots)] = total.astype(BF)
+
+
+def part_sum(order, own, came, depth):
     rows, cols = own.shape
-    pieces = rows // depth
-    return call(
-        partial(part_sum_kernel, depth),
-        [shaped((depth, cols), F32 if k == 0 else BF) for k in range(pieces)],
-        [own, *came],
+    return call(
+        part_sum_kernel,
+        shaped((rows // depth, depth, cols), BF),
+        [order, own, *came],
         rows * cols * 2,
+        smem=1,
     )
 
 
 def final_kernel(plans, *refs):
     outs = refs[-len(plans) :]
     for out_ref, plan in zip(outs, plans):
-        for index, first, count, col in plan:
-            cols = out_ref.shape[-1]
-            total = refs[first][:, col : col + cols].astype(F32)
-            for k in range(1, count):
-                total = total + refs[first + k][:, col : col + cols].astype(F32)
+        cols = out_ref.shape[-1]
+        for index, which, col in plan:
+            ref = refs[which]
+            if len(ref.shape) == 2:
+                out_ref[index] = ref[:, col : col + cols].astype(F32)
+                continue
+            total = ref[0, :, col : col + cols].astype(F32)
+            for slot in range(1, ref.shape[0]):
+                total = total + ref[slot, :, col : col + cols].astype(F32)
             out_ref[index] = total
 
 
@@ -371,23 +382,24 @@
     )
 
 
-def out_back_kernel(col, depth, g_own, g_oth, *refs):
+def out_back_kernel(col, depth, order, g_own, g_oth, *refs):
     w_refs, out_ref = refs[:-1], refs[-1]
     g = jnp.concatenate([g_own[...], g_oth[...]], axis=0)
-    heads_out(out_ref, dot(g, rows_of(w_refs, col, out_ref.shape[0] * HD, depth)), 0, 0)
-
-
-def out_backward(g_own, g_oth, pack, col, depth, local):
+    heads_out(out_ref, dot(g, rows_of(order, w_refs, col, out_ref.shape[0] * HD, depth)), 0, 0)
+
+
+def out_backward(order, g_own, g_oth, pack, col, depth, local):
     half, width = g_own.shape
     return call(
         partial(out_back_kernel, col, depth),
         shaped((local // HD, HD, 2 * half), BF),
-        [g_own, g_oth, *pack],
+        [order, g_own, g_oth, *pack],
         4 * half * width * local,
-    )
-
-
-def qkv_back_kernel(col, depth, extra, g_ref, *refs):
+        smem=1,
+    )
+
+
+def qkv_back_kernel(col, depth, extra, order, g_ref, *refs):
     w_refs, (rows_ref, sum_ref, oth_ref, own_ref) = refs[:-4], refs[-4:]
     heads = g_ref.shape[0]
     half = own_ref.shape[0]
@@ -398,13 +410,13 @@
     ]
     grads = jnp.concatenate(planes, axis=1)
     rows_ref[...] = grads
-    total = dot(grads, rows_of(w_refs, col, 3 * local, depth, extra), NT)
+    total = dot(grads, rows_of(order, w_refs, col, 3 * local, depth, extra), NT)
     oth_ref[...] = total[half:].astype(BF)
     own_ref[...] = total[:half]
     sum_ref[...] = jnp.sum(grads.astype(F32), axis=0, keepdims=True)
 
 
-def qkv_backward(g, pack, col, depth, extra, width):
+def qkv_backward(order, g, pack, col, depth, extra, width):
     heads, _, rows = g.shape
     half = rows // 2
     cols = 3 * heads * HD
@@ -416,8 +428,9 @@
             shaped((half, width), BF),
             shaped((half, width), F32),
         ],
-        [g, *pack],
+        [order, g, *pack],
         2 * rows * width * cols,
+        smem=1,
     )
 
 
@@ -602,8 +615,14 @@
     def tie(value, *others):
         return lax.optimization_barrier((value, *others))[0]
 
-    def gather_z(shard):
-        return [swap(shard, "ctx", nc, bit) for bit in range(1, nc)]
+    def gather_z(shard, doubling=False):
+        if not doubling:
+            return [swap(shard, "ctx", nc, bit) for bit in range(1, nc)]
+        came, bit = [], 1
+        while bit < nc:
+            came.append(swap(jnp.concatenate([shard, *came], axis=0) if came else shard, "ctx", nc, bit))
+            bit *= 2
+        return came
 
     def gather_y(shard, came, apart=False):
         pack = [shard, *came]
@@ -615,11 +634,17 @@
                 pack.append(swap(jnp.concatenate([shard, *came], axis=0), "fsdp", nf, bit))
         return pack
 
+    def whole_gather(shard):
+        return lax.all_gather(shard, ("fsdp", "ctx"), axis=0, tiled=True)
+
+    def whole_scatter(total):
+        return lax.psum_scatter(total, ("fsdp", "ctx"), scatter_dimension=0, tiled=True)
+
     def send_y(parts):
         return [swap(parts[bit], "fsdp", nf, bit) for bit in range(1, nf)]
 
-    def send_z(pieces):
-        return [pieces[0]] + [swap(pieces[bit], "ctx", nc, bit) for bit in range(1, nc)]
+    def reduce_z(parts, came, *others):
+        return across(part_sum(order, tie(parts[0], *others), came, depth))
 
     def tensor_sum(other, own):
         term = (own + sibling(other).astype(F32)).astype(BF)
@@ -661,6 +686,9 @@
     head = (t_index * heads + z_index).astype(F32)
     slope = jnp.exp2(-8.0 * (head + 1.0) / HEADS).reshape(1)
     segments = segment_ids
+    order = jnp.stack(
+        [(y_index ^ a) * nc + (z_index ^ b) for a in range(nf) for b in range(nc)]
+    ).astype(jnp.int32)
 
     def qkv_shard(layer):
         return [qkv_weight[layer, :, i, :] for i in range(3)]
@@ -693,12 +721,18 @@
     x_half = take_half(x_all, side)
     n_own = norm_stats(x_half.astype(F32))[0]
     n_oth = norm_stats(take_half(x_all, 1 - side).astype(F32))[0]
-    h_own, h_oth, qkv_sent = first_qkv(n_own, n_oth, table, 0, biases[0], first_pack, depth, extra)
+    h_own, h_oth, qkv_sent = first_qkv(order, n_own, n_oth, table, 0, biases[0], first_pack, depth, extra)
 
     out_up_shard = tie(jnp.concatenate([out_weight[0], up_weight[0]], axis=1), *first_z)
     out_up_z = gather_z(out_up_shard)
     out_up = gather_y(out_up_shard, out_up_z)
-    out_packs, up_packs, down_packs, qkv_packs = [(out_up, 0)], [(out_up, local)], [], [(first_pack, 0, extra)]
+    out_packs, qkv_packs, up_packs = [(out_up, 0)], [(first_pack, 0, extra)], [(out_up, local)]
+    shared = whole_gather(
+        tie(jnp.concatenate([down_weight[0], out_weight[1], *qkv_shard(1)], axis=1), *first_z)
+    )
+    down_packs = [([shared], 0)]
+    out_packs.append(([shared], hidden))
+    qkv_packs.append(([shared], hidden + local, 0))
 
     records = []
     last_other = last_own = None
@@ -706,34 +740,28 @@
         row = l * NORM_ROWS
         qkv = across(qkv_sent)
         if l == 0:
-            down_shard = tie(down_weight[0], qkv, *out_up_z)
-            down_z = gather_z(down_shard)
-            down_packs.append((gather_y(down_shard, down_z), 0))
-            next_shard = tie(jnp.concatenate([out_weight[1], *qkv_shard(1)], axis=1), *down_z)
-            next_z = gather_z(next_shard)
-            next_pack = gather_y(next_shard, next_z)
-            out_packs.append((next_pack, 0))
-            qkv_packs.append((next_pack, local, 0))
-            up_shard = tie(up_weight[1], *next_z)
-            up_z = gather_z(up_shard)
-            up_packs.append((gather_y(up_shard, up_z), 0))
-            down_shard = tie(down_weight[1], *up_z)
-            down_packs.append((gather_y(down_shard, gather_z(down_shard)), 0))
+            next_mlp = whole_gather(
+                tie(jnp.concatenate([up_weight[1], down_weight[1]], axis=1), shared)
+            )
+            up_packs.append(([next_mlp], 0))
+            down_packs.append(([next_mlp], hidden))
         o_stream, lse = attend(qkv, source, slope, segments)
         o_rows = across(o_stream)
-        other = out_project(o_rows, *out_packs[l], depth, width, half, BF)
-        own = out_project(tie(o_rows, other), *out_packs[l], depth, width, 0, F32)
+        if l == 0:
+            pass
+        other = out_project(order, o_rows, *out_packs[l], depth, width, half, BF)
+        own = out_project(order, tie(o_rows, other), *out_packs[l], depth, width, 0, F32)
         a, b = tensor_sum(other, own)
         y_half, h2_own = add_norm(x_half, a, b, table, row + 3, row + 1, row + 4)
         h2_oth = sibling(h2_own)
-        u, other, own = mlp_forward(h2_own, h2_oth, up_biases[l], up_packs[l], down_packs[l], depth)
+        u, other, own = mlp_forward(order, h2_own, h2_oth, up_biases[l], up_packs[l], down_packs[l], depth)
         records.append((x_half, h_own, h_oth, qkv, lse, o_rows, y_half, h2_own, h2_oth, u))
         if l + 1 < LAYERS:
             a, b = tensor_sum(other, own)
             following = row + NORM_ROWS
             x_half, h_own = add_norm(y_half, a, b, table, row + 5, following, following + 2)
             h_oth = sibling(h_own)
-            qkv_sent = qkv_project(h_own, h_oth, biases[l + 1], *qkv_packs[l + 1][:2], depth)
+            qkv_sent = qkv_project(order, h_own, h_oth, biases[l + 1], *qkv_packs[l + 1][:2], depth)
         else:
             last_other, last_own = other, own
 
@@ -741,73 +769,63 @@
     gz_own, gz_oth = take_half(g_all, side), take_half(g_all, 1 - side)
     gx_half = gz_own.astype(F32)
     sums = [None] * LAYERS
-    pieces = [None] * LAYERS
-    waiting = None
+    mlp_pieces = [None] * LAYERS
+    above = None
     for l in reversed(range(LAYERS)):
         row = l * NORM_ROWS
         x_half, h_own, h_oth, qkv, lse, o_rows, y_half, h2_own, h2_oth, u = records[l]
-        act, gu, up_sum, other, own = mlp_backward(gz_own, gz_oth, u, up_packs[l], down_packs[l], depth)
+        act, gu, up_sum, other, own = mlp_backward(order, gz_own, gz_oth, u, up_packs[l], down_packs[l], depth)
         a, b = tensor_sum(other, own)
-        parts = mlp_grad(gz_own, gz_oth, h2_own, h2_oth, tie(act, a), gu, nf)
-        mlp_came = send_y(parts)
-        mlp_own = parts[0]
+        parts = mlp_grad(order, gz_own, gz_oth, h2_own, h2_oth, tie(act, a), gu, 1)
         b = tie(b, *parts)
-        if waiting is not None:
-            out_q, kv = (part_sum(tie(mine, a), came, depth) for mine, came in waiting)
-            b = tie(b, *out_q, *kv)
-            pieces[l + 1] = (pieces[l + 1], send_z(out_q), send_z(kv))
+        mlp_pieces[l] = whole_scatter(parts[0])
         gy_half, ga_own, sums_two = norm_backward(gx_half, a, b, y_half, table, row + 1)
         ga_oth = sibling(ga_own)
-        g_stream = across(out_backward(ga_own, ga_oth, *out_packs[l], depth, local))
+        g_stream = across(out_backward(order, ga_own, ga_oth, *out_packs[l], depth, local))
         if l == LAYERS - 1:
             a, b = tensor_sum(tie(last_other, g_stream), last_own)
             final_half = y_half + (a.astype(F32) + b.astype(F32) + table[row + 5])
             final_low = final_half.astype(BF)
             block_output = columns_canonical(final_low, sibling(final_low))
         g_sent = attend_backward(qkv, g_stream, lse, source, slope, segments)
-        mlp_pieces = part_sum(tie(mlp_own, g_sent), mlp_came, depth)
-        g_rows = tie(across(g_sent), *mlp_pieces)
-        pieces[l] = send_z(mlp_pieces)
+        g_rows = across(g_sent)
+        if l < LAYERS - 1:
+            above = reduce_z(*above, g_rows)
         g_proj, qkv_sum, other, own = qkv_backward(
-            g_rows, qkv_packs[l][0], qkv_packs[l][1], depth, qkv_packs[l][2], width
+            order, g_rows, qkv_packs[l][0], qkv_packs[l][1], depth, qkv_packs[l][2], width
         )
         a, b = tensor_sum(other, own)
-        out_q_parts = out_q_grad(ga_own, ga_oth, o_rows, h_own, h_oth, tie(g_proj, a), nf)
-        out_q_came = send_y(out_q_parts)
-        kv_parts = kv_grad(h_own, h_oth, tie(g_proj, *out_q_parts), nf)
-        kv_came = send_y(kv_parts)
-        b = tie(b, *kv_parts)
-        waiting = [(out_q_parts[0], out_q_came), (kv_parts[0], kv_came)]
+        sources = (order, ga_own, ga_oth, o_rows, h_own, h_oth)
+        if l == LAYERS - 1:
+            attn = attention_grad(0, 4, *sources, tie(g_proj, a), nf)
+            above = (attn, send_y(attn))
+            b = tie(b, *attn)
+        else:
+            out_q = attention_grad(0, 2, *sources, g_proj, nf)
+            out_q_came = send_y(out_q)
+            kv = attention_grad(2, 4, *sources, tie(g_proj, *out_q), nf)
+            kv_came = send_y(kv)
+            b = tie(b, *kv)
         gx_half, gz_own, sums_one = norm_backward(gy_half, a, b, x_half, table, row)
         if l > 0:
             gz_oth = sibling(gz_own)
         sums[l] = (sums_one, sums_two, qkv_sum, up_sum)
-    out_q, kv = (part_sum(mine, came, depth) for mine, came in waiting)
-    pieces[0] = (pieces[0], send_z(out_q), send_z(kv))
+    out_q_pieces = reduce_z(out_q, out_q_came, above)
+    kv_pieces = reduce_z(kv, kv_came, out_q_pieces)
 
     grad_tokens = columns_canonical(gx_half, sibling(gx_half))
 
-    def plan(which, col, index=lambda layer: layer):
-        return [(index(layer), which * LAYERS * nc + layer * nc, nc, col) for layer in range(LAYERS)]
-
-    def weight_sums(which, plans, shapes):
-        return final_sums(plans, shapes, [p for layer in range(LAYERS) for p in pieces[layer][which]])
-
-    grad_up, grad_down = weight_sums(
-        0, [plan(0, 0), plan(0, hidden)], [shaped((LAYERS, depth, hidden), F32)] * 2
-    )
-    out_q_all = [p for layer in range(LAYERS) for p in pieces[layer][1]]
-    kv_all = [p for layer in range(LAYERS) for p in pieces[layer][2]]
-    qkv_plan = []
-    for i in range(3):
-        which, col = (0, local) if i == 0 else (1, (i - 1) * local)
-        qkv_plan += [
-            ((layer, i), which * LAYERS * nc + layer * nc, nc, col) for layer in range(LAYERS)
-        ]
+    grad_up, grad_down = final_sums(
+        [[(l, l, col) for l in range(LAYERS)] for col in (0, hidden)],
+        [shaped((LAYERS, depth, hidden), F32)] * 2,
+        mlp_pieces,
+    )
+    qkv_plan = [((1, i), 2, (i + 1) * local) for i in range(3)]
+    qkv_plan += [((0, 0), 0, local), ((0, 1), 1, 0), ((0, 2), 1, local)]
     grad_out, grad_qkv = final_sums(
-        [plan(0, 0), qkv_plan],
+        [[(0, 0, 0), (1, 2, 0)], qkv_plan],
         [shaped((LAYERS, depth, local), F32), shaped((LAYERS, 3, depth, local), F32)],
-        out_q_all + kv_all,
+        [out_q_pieces, kv_pieces, above],
     )
     grad_qkv = grad_qkv.transpose(0, 2, 1, 3)
 

time: 666 us -> 596 us (0.89)
  waiting for transfers between devices: 333 us -> 222 us
  blocking collectives: 45.2 us -> 95.6 us
  starting transfers between devices: 112 us -> 64.1 us
  local copies, waits for them, and re-layouts: 77.2 us -> 96.5 us
  between operations: 2.83 us -> 15.9 us
    ppermute x78 -> x41, waiting for transfers between devices: 302 us -> 167 us  [swap(): return lax.ppermute(value, axis, [(i, i ^ bit) for i in range(size)])]
    ppermute x78 -> x41, starting transfers between devices: 92.3 us -> 34.6 us  [swap(): return lax.ppermute(value, axis, [(i, i ^ bit) for i in range(size)])]
    all_to_all x3 -> x4, blocking collectives: 45.2 us -> 95.6 us  [across(): return lax.all_to_all(value, 'ctx', 0, 0)]
    all_to_all x5 -> x7, waiting for transfers between devices: 30.7 us -> 52.9 us  [across(): return lax.all_to_all(value, 'ctx', 0, 0)]
    unnamed x318 -> x266, local copies, waits for them, and re-layouts: 56.7 us -> 78 us
    all_to_all x5 -> x7, starting transfers between devices: 19.5 us -> 29.1 us  [across(): return lax.all_to_all(value, 'ctx', 0, 0)]
    pallas_call x35 -> x31, Pallas kernels: 54.3 us -> 53.4 us  [call(): pl.pallas_call(kernel, in_specs=specs, out_specs=[whole()] * len(outs) if...]
  transfers between devices with their start and end apart: 83 -> 52, of which waited for: 33 -> 30; matrix products, arithmetic and copies ran while one was open for 7% -> 12% of each run, Pallas kernels for 8% -> 11%
where the time goes in v3:
time: 596 us; the launch traced here: 587 us
  waiting for transfers between devices  222 us (37%)
  local copies, waits for them, and re-layouts  96.5 us (16%)
  blocking collectives  95.6 us (16%)
  Pallas kernels  75.5 us (13%)
  starting transfers between devices  64.1 us (11%)
  other arithmetic  17.5 us (3%)
  between operations  15.9 us (3%)
    ppermute x41, waiting for transfers between devices, swap(): return lax.ppermute(value, axis, [(i, i ^ bit) for i in range(size)])  167 us
    all_to_all x4, blocking collectives, across(): return lax.all_to_all(value, 'ctx', 0, 0)  95.6 us
    unnamed x266, local copies, waits for them, and re-layouts  78 us
    pallas_call x31, Pallas kernels, call(): pl.pallas_call(kernel, in_specs=specs, out_specs=[whole()] * len(outs) if...  53.4 us
    all_to_all x7, waiting for transfers between devices, across(): return lax.all_to_all(value, 'ctx', 0, 0)  52.9 us
    ppermute x41, starting transfers between devices, swap(): return lax.ppermute(value, axis, [(i, i ^ bit) for i in range(size)])  34.6 us
    all_to_all x7, starting transfers between devices, across(): return lax.all_to_all(value, 'ctx', 0, 0)  29.1 us
    pallas_call x2, Pallas kernels, attend_backward(): pl.pallas_call(partial(attend_back_kernel, rows // BLK), in_specs=[smem,...  12.6 us
  transfers between devices with their start and end apart: 52, of which 30 were waited for; matrix products, arithmetic and copies ran while one was open for 12% of the time, Pallas kernels for 11%

profile of v3, /device:TPU:0, one launch (start us, length us, event | category | flops | bytes accessed | tf_op | source)
XLA Modules:
  0.0 586.8 jit_solution(5848938147274648439)
XLA Ops:
  23.1 11.7 %collective-permute-done.1.refs_2_ = bf16[144,768]{1,0:T(8,128)(2,1)S(1)} collective-permute-done((bf16[144,768]{1,0:T(8,128)(2,1)S(1)}, bf16[144,768]{1,0:T(8,128)(2,1)S(1)}, u32[]{:S(2)}, u32[]{:S(2)}) %collective-permute-start.1) | collective-permute-done | bytes 221216 | tf_op jit(solution)/shard_map/ppermute | solution.py:607
  49.2 15.6 %collective-permute-done.4.refs_5_ = bf16[432,768]{1,0:T(8,128)(2,1)S(1)} collective-permute-done((bf16[432,768]{1,0:T(8,128)(2,1)S(1)}, bf16[432,768]{1,0:T(8,128)(2,1)S(1)}, u32[]{:S(2)}, u32[]{:S(2)}) %collective-permute-start.4) | collective-permute-done | bytes 663584 | tf_op jit(solution)/shard_map/ppermute | solution.py:607
  69.0 4.7 all-to-all-start
  73.8 32.0 %collective-permute-done.6.refs_2_ = bf16[128,1280]{1,0:T(8,128)(2,1)S(1)} collective-permute-done((bf16[128,1280]{1,0:T(8,128)(2,1)S(1)}, bf16[128,1280]{1,0:T(8,128)(2,1)S(1)}, u32[]{:S(2)}, u32[]{:S(2)}) %collective-permute-start.6) | collective-permute-done | bytes 327712 | tf_op jit(solution)/shard_map/ppermute | solution.py:607
  108.1 18.6 %all-to-all-done.qkv_ref = bf16[4,192,512]{2,1,0:T(8,128)(2,1)} async-done(((bf16[4,192,512]{2,1,0:T(8,128)(2,1)}), bf16[4,192,512]{2,1,0:T(8,128)(2,1)}, u32[]{:S(2)}, u32[]{:S(2)}) %all-to-all-start) | async-done | bytes 786464 | tf_op jit(solution)/shard_map/all_to_all | solution.py:613
  126.8 5.0 shard_map.196
  137.6 8.7 %collective-permute-done.8.refs_4_ = bf16[512,1280]{1,0:T(8,128)(2,1)S(1)} collective-permute-done((bf16[512,1280]{1,0:T(8,128)(2,1)}, bf16[512,1280]{1,0:T(8,128)(2,1)S(1)}, u32[]{:S(2)}, u32[]{:S(2)}) %collective-permute-start.8) | collective-permute-done | bytes 1310752 | tf_op jit(solution)/shard_map/ppermute | solution.py:607
  158.3 12.4 %collective-permute-done.10.b_ref = bf16[256,1024]{1,0:T(8,128)(2,1)S(1)} collective-permute-done((bf16[256,1024]{1,0:T(8,128)(2,1)S(1)}, bf16[256,1024]{1,0:T(8,128)(2,1)S(1)}, u32[]{:S(2)}, u32[]{:S(2)}) %collective-permute-start.10) | collective-permute-done | bytes 524320 | tf_op jit(solution)/shard_map/ppermute | solution.py:607
  179.9 12.5 %collective-permute-done.13.b_ref = bf16[256,1024]{1,0:T(8,128)(2,1)S(1)} collective-permute-done((bf16[256,1024]{1,0:T(8,128)(2,1)S(1)}, bf16[256,1024]{1,0:T(8,128)(2,1)S(1)}, u32[]{:S(2)}, u32[]{:S(2)}) %collective-permute-start.13) | collective-permute-done | bytes 524320 | tf_op jit(solution)/shard_map/ppermute | solution.py:607
  198.0 41.8 %all_to_all.55.qkv_ref = bf16[4,192,512]{2,1,0:T(8,128)(2,1)S(1)} all-to-all(bf16[4,192,512]{2,1,0:T(8,128)(2,1)S(1)} %shard_map.202), channel_id=1, replica_groups=mesh['fsdp'=2,'ctx'=4,'tp'=4] {'ctx'}, dimensions={0} | all-to-all | bytes 1572864 | tf_op jit(solution)/shard_map/all_to_all | solution.py:613
  244.2 11.6 %all_to_all.56.o_ref = bf16[4,64,512]{2,1,0:T(8,128)(2,1)S(1)} all-to-all(bf16[4,64,512]{2,1,0:T(8,128)(2,1)S(1)} %get-tuple-element.96), channel_id=1, replica_groups=mesh['fsdp'=2,'ctx'=4,'tp'=4] {'ctx'}, dimensions={0} | all-to-all | bytes 524288 | tf_op jit(solution)/shard_map/all_to_all | solution.py:613
  260.6 12.3 %collective-permute-done.16.b_ref = bf16[256,1024]{1,0:T(8,128)(2,1)S(1)} collective-permute-done((bf16[256,1024]{1,0:T(8,128)(2,1)S(1)}, bf16[256,1024]{1,0:T(8,128)(2,1)S(1)}, u32[]{:S(2)}, u32[]{:S(2)}) %collective-permute-start.16) | collective-permute-done | bytes 524320 | tf_op jit(solution)/shard_map/ppermute | solution.py:607
  298.8 12.9 %collective-permute-done.19.b_ref = bf16[256,1024]{1,0:T(8,128)(2,1)S(1)} collective-permute-done((bf16[256,1024]{1,0:T(8,128)(2,1)}, bf16[256,1024]{1,0:T(8,128)(2,1)S(1)}, u32[]{:S(2)}, u32[]{:S(2)}) %collective-permute-start.19) | collective-permute-done | bytes 524320 | tf_op jit(solution)/shard_map/ppermute | solution.py:607
  321.5 19.7 %all_to_all.57.g_ref = bf16[4,64,512]{2,1,0:T(8,128)(2,1)S(1)} all-to-all(bf16[4,64,512]{2,1,0:T(8,128)(2,1)S(1)} %shard_map.211), channel_id=1, replica_groups=mesh['fsdp'=2,'ctx'=4,'tp'=4] {'ctx'}, dimensions={0} | all-to-all | bytes 524288 | tf_op jit(solution)/shard_map/all_to_all | solution.py:613
  341.3 6.0 %shard_map.212 = bf16[4,192,512]{2,1,0:T(8,128)(2,1)S(1)} custom-call(s32[16]{0:T(128)S(1)} %select_reduce_fusion.src_ref, f32[1]{0:T(128)} %bitcast.9.slope_ref, s32[1,2048]{1,0:T(1,128)S(1)} %copy-done.86, bf16[4,192,512]{2,1,0:T(8,128)(2,1)S(1)} %copy-done.57, bf16[4,64,512]{2,1,0:T(8,128)(2,1)S(1)} %all_to_all.57.g_ref, ...), custom_call_target="tpu_custom_call" | custom-call | flops 939524096 | bytes 2097152 | tf_op jit(solution)/shard_map/pallas_call | solution.py:561
  347.2 22.5 %all_to_all.58.g_ref = bf16[4,192,512]{2,1,0:T(8,128)(2,1)S(1)} all-to-all(bf16[4,192,512]{2,1,0:T(8,128)(2,1)S(1)} %shard_map.212), channel_id=1, replica_groups=mesh['fsdp'=2,'ctx'=4,'tp'=4] {'ctx'}, dimensions={0} | all-to-all | bytes 1572864 | tf_op jit(solution)/shard_map/all_to_all | solution.py:613
  378.7 8.8 %collective-permute-done.25.b_ref = bf16[256,1024]{1,0:T(8,128)(2,1)S(1)} collective-permute-done((bf16[256,1024]{1,0:T(8,128)(2,1)S(1)}, bf16[256,1024]{1,0:T(8,128)(2,1)S(1)}, u32[]{:S(2)}, u32[]{:S(2)}) %collective-permute-start.25) | collective-permute-done | bytes 524320 | tf_op jit(solution)/shard_map/ppermute | solution.py:607
  404.9 12.8 %collective-permute-done.28.b_ref = bf16[256,1024]{1,0:T(8,128)(2,1)S(1)} collective-permute-done((bf16[256,1024]{1,0:T(8,128)(2,1)}, bf16[256,1024]{1,0:T(8,128)(2,1)S(1)}, u32[]{:S(2)}, u32[]{:S(2)}) %collective-permute-start.28) | collective-permute-done | bytes 524320 | tf_op jit(solution)/shard_map/ppermute | solution.py:607
  431.8 16.2 %all-to-all-done.6.g_ref = bf16[4,64,512]{2,1,0:T(8,128)(2,1)S(1)} async-done(((bf16[4,64,512]{2,1,0:T(8,128)(2,1)}), bf16[4,64,512]{2,1,0:T(8,128)(2,1)S(1)}, u32[]{:S(2)}, u32[]{:S(2)}) %all-to-all-start.6) | async-done | bytes 262176 | tf_op jit(solution)/shard_map/all_to_all | solution.py:613
  448.0 6.7 %shard_map.220 = bf16[4,192,512]{2,1,0:T(8,128)(2,1)S(1)} custom-call(s32[16]{0:T(128)S(1)} %select_reduce_fusion.src_ref, f32[1]{0:T(128)} %bitcast.9.slope_ref, s32[1,2048]{1,0:T(1,128)S(1)} %copy-done.86, bf16[4,192,512]{2,1,0:T(8,128)(2,1)} %all-to-all-done.qkv_ref, bf16[4,64,512]{2,1,0:T(8,128)(2,1)S(1)} %all-to-all-done.6.g_ref, ...), custom_call_target="tpu_custom_call" | custom-call | flops 939524096 | bytes 2097152 | tf_op jit(solution)/shard_map/pallas_call | solution.py:561
  468.3 11.1 %all-to-all-done.7.g_ref = bf16[4,192,512]{2,1,0:T(8,128)(2,1)S(1)} async-done(((bf16[4,192,512]{2,1,0:T(8,128)(2,1)}), bf16[4,192,512]{2,1,0:T(8,128)(2,1)S(1)}, u32[]{:S(2)}, u32[]{:S(2)}) %all-to-all-start.7) | async-done | bytes 786464 | tf_op jit(solution)/shard_map/all_to_all | solution.py:613
  493.2 5.5 collective-permute-done.33.refs_0_
  501.1 5.3 all-to-all-start.8
  542.5 5.1 all-to-all-start.9
  (466 shorter events, 251.6 us)
Async XLA Ops:
  7.2 146.8 %all-gather.3.cloned.1.call-start = ((), (), s32[]{:S(2)}) async-start(), calls=%async_computation.13 | async-start | bytes 4718592 | tf_op jit(solution)/shard_map/all_gather | solution.py:638
  9.6 39.6 %collective-permute-start.3 = (bf16[144,768]{1,0:T(8,128)(2,1)S(1)}, bf16[144,768]{1,0:T(8,128)(2,1)S(1)}, u32[]{:S(2)}, u32[]{:S(2)}) collective-permute-start(bf16[144,768]{1,0:T(8,128)(2,1)S(1)} %fusion.7.refs_0_), channel_id=1, source_target_pairs={{0,16},{16,0},{1,17},{17,1},{2,18},{18,2},{3,19},{19,3},{4,20},{20... | collective-permute-start | bytes 663560 | tf_op jit(solution)/shard_map/ppermute | solution.py:607
  16.3 18.5 %collective-permute-start.1 = (bf16[144,768]{1,0:T(8,128)(2,1)S(1)}, bf16[144,768]{1,0:T(8,128)(2,1)S(1)}, u32[]{:S(2)}, u32[]{:S(2)}) collective-permute-start(bf16[144,768]{1,0:T(8,128)(2,1)S(1)} %fusion.7.refs_0_), channel_id=1, source_target_pairs={{0,8},{4,12},{8,0},{12,4},{1,9},{5,13},{9,1},{13,5},{2,10},{6,14},... | collective-permute-start | bytes 663560 | tf_op jit(solution)/shard_map/ppermute | solution.py:607
  16.3 18.5 %collective-permute-start = (bf16[144,768]{1,0:T(8,128)(2,1)S(1)}, bf16[144,768]{1,0:T(8,128)(2,1)S(1)}, u32[]{:S(2)}, u32[]{:S(2)}) collective-permute-start(bf16[144,768]{1,0:T(8,128)(2,1)S(1)} %fusion.7.refs_0_), channel_id=1, source_target_pairs={{0,4},{4,0},{8,12},{12,8},{1,5},{5,1},{9,13},{13,9},{2,6},{6,2},{1... | collective-permute-start | bytes 663560 | tf_op jit(solution)/shard_map/ppermute | solution.py:607
  44.1 29.7 %collective-permute-start.7 = (bf16[128,1280]{1,0:T(8,128)(2,1)S(1)}, bf16[128,1280]{1,0:T(8,128)(2,1)S(1)}, u32[]{:S(2)}, u32[]{:S(2)}) collective-permute-start(bf16[128,1280]{1,0:T(8,128)(2,1)S(1)} %pad_maximum_fusion.3.refs_0_), channel_id=1, source_target_pairs={{0,12},{4,8},{8,4},{12,0},{1,13},{5,9},{9,5},{13,1},{2,14},{6,10},... | collective-permute-start | bytes 983048 | tf_op jit(solution)/shard_map/ppermute | solution.py:607
  46.6 59.2 %collective-permute-start.6 = (bf16[128,1280]{1,0:T(8,128)(2,1)S(1)}, bf16[128,1280]{1,0:T(8,128)(2,1)S(1)}, u32[]{:S(2)}, u32[]{:S(2)}) collective-permute-start(bf16[128,1280]{1,0:T(8,128)(2,1)S(1)} %pad_maximum_fusion.3.refs_0_), channel_id=1, source_target_pairs={{0,8},{4,12},{8,0},{12,4},{1,9},{5,13},{9,1},{13,5},{2,10},{6,14},... | collective-permute-start | bytes 983048 | tf_op jit(solution)/shard_map/ppermute | solution.py:607
  46.6 59.2 %collective-permute-start.5 = (bf16[128,1280]{1,0:T(8,128)(2,1)S(1)}, bf16[128,1280]{1,0:T(8,128)(2,1)S(1)}, u32[]{:S(2)}, u32[]{:S(2)}) collective-permute-start(bf16[128,1280]{1,0:T(8,128)(2,1)S(1)} %pad_maximum_fusion.3.refs_0_), channel_id=1, source_target_pairs={{0,4},{4,0},{8,12},{12,8},{1,5},{5,1},{9,13},{13,9},{2,6},{6,2},{1... | collective-permute-start | bytes 983048 | tf_op jit(solution)/shard_map/ppermute | solution.py:607
  48.6 16.2 %collective-permute-start.4 = (bf16[432,768]{1,0:T(8,128)(2,1)S(1)}, bf16[432,768]{1,0:T(8,128)(2,1)S(1)}, u32[]{:S(2)}, u32[]{:S(2)}) collective-permute-start(bf16[432,768]{1,0:T(8,128)(2,1)S(1)} %pad_maximum_fusion.1), channel_id=1, source_target_pairs={{0,16},{16,0},{1,17},{17,1},{2,18},{18,2},{3,19},{19,3},{4,20},{20... | collective-permute-start | bytes 1990664 | tf_op jit(solution)/shard_map/ppermute | solution.py:607
  69.0 57.7 %all-to-all-start = ((bf16[4,192,512]{2,1,0:T(8,128)(2,1)}), bf16[4,192,512]{2,1,0:T(8,128)(2,1)}, u32[]{:S(2)}, u32[]{:S(2)}) async-start(bf16[4,192,512]{2,1,0:T(8,128)(2,1)} %copy-done.59), calls=%async_computation | async-start | bytes 1572864 | tf_op jit(solution)/shard_map/all_to_all | solution.py:613
  106.9 39.4 %collective-permute-start.8 = (bf16[512,1280]{1,0:T(8,128)(2,1)}, bf16[512,1280]{1,0:T(8,128)(2,1)S(1)}, u32[]{:S(2)}, u32[]{:S(2)}) collective-permute-start(bf16[512,1280]{1,0:T(8,128)(2,1)} %pad_maximum_fusion), channel_id=1, source_target_pairs={{0,16},{16,0},{1,17},{17,1},{2,18},{18,2},{3,19},{19,3},{4,20},{20... | collective-permute-start | bytes 3932168 | tf_op jit(solution)/shard_map/ppermute | solution.py:607
  132.5 17.3 %all-to-all-start.1 = ((bf16[4,64,512]{2,1,0:T(8,128)(2,1)}), bf16[4,64,512]{2,1,0:T(8,128)(2,1)S(1)}, u32[]{:S(2)}, u32[]{:S(2)}) async-start(bf16[4,64,512]{2,1,0:T(8,128)(2,1)} %copy-done.76), calls=%async_computation.1 | async-start | bytes 524288 | tf_op jit(solution)/shard_map/all_to_all | solution.py:613
  135.9 140.3 %all-gather.5.cloned.1.call-start = ((), (), s32[]{:S(2)}) async-start(), calls=%async_computation.14 | async-start | bytes 4718592 | tf_op jit(solution)/shard_map/all_gather | solution.py:638
  154.0 422.3 %reduce-scatter.5.cloned.1.call-start = ((), (), s32[]{:S(2)}) async-start(), calls=%async_computation.16 | async-start | bytes 4718592 | tf_op jit(solution)/shard_map/reduce_scatter | solution.py:641
  297.2 279.1 %reduce-scatter.3.cloned.1.call-start = ((), (), s32[]{:S(2)}) async-start(), calls=%async_computation.15 | async-start | bytes 4718592 | tf_op jit(solution)/shard_map/reduce_scatter | solution.py:641
  404.9 17.5 %collective-permute-start.21 = (bf16[256,1024]{1,0:T(8,128)(2,1)}, bf16[256,1024]{1,0:T(8,128)(2,1)S(1)}, u32[]{:S(2)}, u32[]{:S(2)}) collective-permute-start(bf16[256,1024]{1,0:T(8,128)(2,1)} %copy-done.85), channel_id=1, source_target_pairs={{0,1},{1,0},{2,3},{3,2},{4,5},{5,4},{6,7},{7,6},{8,9},{9,8},{10,11... | collective-permute-start | bytes 1572872 | tf_op jit(solution)/shard_map/ppermute | solution.py:607
  423.6 35.5 %collective-permute-start.22 = (bf16[256,1024]{1,0:T(8,128)(2,1)}, bf16[256,1024]{1,0:T(8,128)(2,1)}, u32[]{:S(2)}, u32[]{:S(2)}) collective-permute-start(bf16[256,1024]{1,0:T(8,128)(2,1)} %add_convert_fusion.4), channel_id=1, source_target_pairs={{0,2},{1,3},{2,0},{3,1},{4,6},{5,7},{6,4},{7,5},{8,10},{9,11},{10,... | collective-permute-start | bytes 1572872 | tf_op jit(solution)/shard_map/ppermute | solution.py:607
  427.5 20.5 %all-to-all-start.6 = ((bf16[4,64,512]{2,1,0:T(8,128)(2,1)}), bf16[4,64,512]{2,1,0:T(8,128)(2,1)S(1)}, u32[]{:S(2)}, u32[]{:S(2)}) async-start(bf16[4,64,512]{2,1,0:T(8,128)(2,1)} %copy-done.41), calls=%async_computation.6 | async-start | bytes 524288 | tf_op jit(solution)/shard_map/all_to_all | solution.py:613
  455.6 23.9 %all-to-all-start.7 = ((bf16[4,192,512]{2,1,0:T(8,128)(2,1)}), bf16[4,192,512]{2,1,0:T(8,128)(2,1)S(1)}, u32[]{:S(2)}, u32[]{:S(2)}) async-start(bf16[4,192,512]{2,1,0:T(8,128)(2,1)} %copy-done.58), calls=%async_computation.7 | async-start | bytes 1572864 | tf_op jit(solution)/shard_map/all_to_all | solution.py:613
  467.2 31.4 %collective-permute-start.33 = (bf16[512,1024]{1,0:T(8,128)(2,1)}, bf16[512,1024]{1,0:T(8,128)(2,1)}, u32[]{:S(2)}, u32[]{:S(2)}) collective-permute-start(bf16[512,1024]{1,0:T(8,128)(2,1)} %get-tuple-element.119), channel_id=1, source_target_pairs={{0,16},{16,0},{1,17},{17,1},{2,18},{18,2},{3,19},{19,3},{4,20},{20... | collective-permute-start | bytes 3145736 | tf_op jit(solution)/shard_map/ppermute | solution.py:607
  489.2 21.6 %collective-permute-start.31 = (bf16[256,1024]{1,0:T(8,128)(2,1)}, bf16[256,1024]{1,0:T(8,128)(2,1)}, u32[]{:S(2)}, u32[]{:S(2)}) collective-permute-start(bf16[256,1024]{1,0:T(8,128)(2,1)} %add_convert_fusion.a_ref), channel_id=1, source_target_pairs={{0,2},{1,3},{2,0},{3,1},{4,6},{5,7},{6,4},{7,5},{8,10},{9,11},{10,... | collective-permute-start | bytes 1572872 | tf_op jit(solution)/shard_map/ppermute | solution.py:607
  501.1 36.6 %all-to-all-start.8 = ((bf16[4,128,1024]{2,1,0:T(8,128)(2,1)}), bf16[4,128,1024]{2,1,0:T(8,128)(2,1)S(1)}, u32[]{:S(2)}, u32[]{:S(2)}) async-start(bf16[4,128,1024]{2,1,0:T(8,128)(2,1)} %copy-done.21), calls=%async_computation.8 | async-start | bytes 2097152 | tf_op jit(solution)/shard_map/all_to_all | solution.py:613
  527.1 23.5 %collective-permute-start.32 = (f32[256,1024]{1,0:T(8,128)S(1)}, f32[256,1024]{1,0:T(8,128)}, u32[]{:S(2)}, u32[]{:S(2)}) collective-permute-start(f32[256,1024]{1,0:T(8,128)S(1)} %get-tuple-element.144), channel_id=1, source_target_pairs={{0,1},{1,0},{2,3},{3,2},{4,5},{5,4},{6,7},{7,6},{8,9},{9,8},{10,11... | collective-permute-start | bytes 3145736 | tf_op jit(solution)/shard_map/ppermute | solution.py:607
  533.7 24.3 %collective-permute-start.35 = (bf16[512,512]{1,0:T(8,128)(2,1)}, bf16[512,512]{1,0:T(8,128)(2,1)}, u32[]{:S(2)}, u32[]{:S(2)}) collective-permute-start(bf16[512,512]{1,0:T(8,128)(2,1)} %copy-done.83), channel_id=1, source_target_pairs={{0,16},{16,0},{1,17},{17,1},{2,18},{18,2},{3,19},{19,3},{4,20},{20... | collective-permute-start | bytes 1572872 | tf_op jit(solution)/shard_map/ppermute | solution.py:607
  542.5 15.5 %all-to-all-start.9 = ((bf16[4,128,512]{2,1,0:T(8,128)(2,1)}), bf16[4,128,512]{2,1,0:T(8,128)(2,1)S(1)}, u32[]{:S(2)}, u32[]{:S(2)}) async-start(bf16[4,128,512]{2,1,0:T(8,128)(2,1)} %shard_map.226), calls=%async_computation.9 | async-start | bytes 1048576 | tf_op jit(solution)/shard_map/all_to_all | solution.py:613
  (138 other events, 1087.2 us)
Sparse Core Ops, SparseCore 0:
  34.9 119.0 all-gather.2
  156.1 85.0 all-gather.4
  297.3 92.8 reduce-scatter.4
  403.6 97.4 reduce-scatter.2

commit v4 on v3

--- a/solution.py
+++ b/solution.py
@@ -267,37 +267,48 @@
         out_ref[:, cols] = total[y * span : (y + 1) * span].astype(BF)
 
 
-def mlp_grad_kernel(order, g_own, g_oth, h_own, h_oth, act_ref, gu_ref, *out_refs):
+def late_grad_kernel(count, order, *refs):
+    g_own, g_oth, h_own, h_oth, act_ref, gu_ref = refs[:6]
+    out_refs = refs[count:]
     hidden = act_ref.shape[1]
     h = jnp.concatenate([h_own[...], h_oth[...]], axis=0).T
     grads_out(order, out_refs, dot(h, gu_ref[...]), 0)
     g = jnp.concatenate([g_own[...], g_oth[...]], axis=0).T
     grads_out(order, out_refs, dot(g, act_ref[...]), hidden)
-
-
-def mlp_grad(order, g_own, g_oth, h_own, h_oth, act, gu, nf):
-    half, width = g_own.shape
-    hidden = act.shape[1]
-    return call(
-        mlp_grad_kernel,
-        [shaped((width // nf, 2 * hidden), BF)] * nf,
-        [order, g_own, g_oth, h_own, h_oth, act, gu],
-        8 * half * width * hidden,
+    if count > 6:
+        attention_grad_body(0, 4, 2 * hidden, order, *refs[6:count], out_refs)
+
+
+def late_grad(order, mlp, attention):
+    half, width = mlp[0].shape
+    cols = 2 * mlp[4].shape[1]
+    if attention:
+        cols += 4 * attention[2].shape[0] * HD
+    args = [*mlp, *attention]
+    return call(
+        partial(late_grad_kernel, len(args)),
+        [shaped((width, cols), BF)],
+        [order, *args],
+        4 * half * width * cols,
         smem=1,
-    )
-
-
-def attention_grad_kernel(first, last, order, g_own, g_oth, o_ref, h_own, h_oth, p_ref, *out_refs):
+    )[0]
+
+
+def attention_grad_body(first, last, col, order, g_own, g_oth, o_ref, h_own, h_oth, p_ref, out_refs):
     heads = o_ref.shape[0]
     local = heads * HD
-    col = 0
     if first == 0:
         g = jnp.concatenate([g_own[...], g_oth[...]], axis=0).T
         o = jnp.concatenate([o_ref[j] for j in range(heads)], axis=0)
-        grads_out(order, out_refs, dot(g, o, NT), 0)
-        col = local
+        grads_out(order, out_refs, dot(g, o, NT), col)
+        col += local
+        first = 1
     h = jnp.concatenate([h_own[...], h_oth[...]], axis=0).T
-    grads_out(order, out_refs, dot(h, p_ref[:, (max(first, 1) - 1) * local : (last - 1) * local]), col)
+    grads_out(order, out_refs, dot(h, p_ref[:, (first - 1) * local : (last - 1) * local]), col)
+
+
+def attention_grad_kernel(first, last, order, *refs):
+    attention_grad_body(first, last, 0, order, *refs[:6], refs[6:])
 
 
 def attention_grad(first, last, order, g_own, g_oth, o_rows, h_own, h_oth, g_proj, nf):
@@ -313,23 +324,27 @@
     )
 
 
-def part_sum_kernel(order, own_ref, *refs):
+def part_sum_kernel(order, own_ref, small_ref, *refs):
     came, out_ref = refs[:-1], refs[-1]
-    slots, depth, _ = out_ref.shape
+    slots = out_ref.shape[0]
+    depth = own_ref.shape[0] // slots
     for number in range(slots):
         rows = slice(number * depth, (number + 1) * depth)
         total = own_ref[rows, :].astype(F32)
         for ref in came:
             total = total + ref[rows, :].astype(F32)
-        out_ref[lax.rem(order[number], slots)] = total.astype(BF)
-
-
-def part_sum(order, own, came, depth):
+        slot = lax.rem(order[number], slots)
+        out_ref[slot, :depth, :] = total.astype(BF)
+        out_ref[slot, depth:, :] = small_ref[number].astype(BF)
+
+
+def part_sum(order, own, small, came):
     rows, cols = own.shape
+    slots, extra, _ = small.shape
     return call(
         part_sum_kernel,
-        shaped((rows // depth, depth, cols), BF),
-        [order, own, *came],
+        shaped((slots, rows // slots + extra, cols), BF),
+        [order, own, small, *came],
         rows * cols * 2,
         smem=1,
     )
@@ -342,11 +357,12 @@
         for index, which, col in plan:
             ref = refs[which]
             if len(ref.shape) == 2:
-                out_ref[index] = ref[:, col : col + cols].astype(F32)
+                out_ref[index] = ref[: out_ref.shape[-2], col : col + cols].astype(F32)
                 continue
-            total = ref[0, :, col : col + cols].astype(F32)
+            rows = slice(0, out_ref.shape[-2])
+            total = ref[0, rows, col : col + cols].astype(F32)
             for slot in range(1, ref.shape[0]):
-                total = total + ref[slot, :, col : col + cols].astype(F32)
+                total = total + ref[slot, rows, col : col + cols].astype(F32)
             out_ref[index] = total
 
 
@@ -574,6 +590,28 @@
     )(source, slope, segments, qkv, grads, lse)
 
 
+def to_relative_kernel(place_ref, value_ref, own_ref, oth_ref):
+    half = own_ref.shape[0]
+    for ref, side in ((own_ref, place_ref[0]), (oth_ref, 1 - place_ref[0])):
+        rows = pl.ds(pl.multiple_of(side * half, half), half)
+        for number in range(place_ref.shape[0] - 1):
+            depth = value_ref.shape[1] // (place_ref.shape[0] - 1)
+            start = pl.multiple_of(place_ref[number + 1] * depth, depth)
+            ref[:, number * depth : (number + 1) * depth] = value_ref[rows, pl.ds(start, depth)]
+
+
+def from_relative_kernel(place_ref, own_ref, oth_ref, value_ref):
+    half = own_ref.shape[0]
+    for ref, side in ((own_ref, place_ref[0]), (oth_ref, 1 - place_ref[0])):
+        rows = pl.ds(pl.multiple_of(side * half, half), half)
+        for number in range(place_ref.shape[0] - 1):
+            depth = value_ref.shape[1] // (place_ref.shape[0] - 1)
+            start = pl.multiple_of(place_ref[number + 1] * depth, depth)
+            value_ref[rows, pl.ds(start, depth)] = ref[:, number * depth : (number + 1) * depth].astype(
+                value_ref.dtype
+            )
+
+
 def on_device(
     nf,
     nc,
@@ -628,8 +666,9 @@
         pack = [shard, *came]
         for bit in range(1, nf):
             if apart:
-                pack.append(swap(shard, "fsdp", nf, bit))
-                pack.append(swap(jnp.concatenate(came, axis=0), "fsdp", nf, bit))
+                own = swap(shard, "fsdp", nf, bit)
+                pack.append(own)
+                pack.append(swap(tie(jnp.concatenate(came, axis=0), own), "fsdp", nf, bit))
             else:
                 pack.append(swap(jnp.concatenate([shard, *came], axis=0), "fsdp", nf, bit))
         return pack
@@ -642,9 +681,6 @@
 
     def send_y(parts):
         return [swap(parts[bit], "fsdp", nf, bit) for bit in range(1, nf)]
-
-    def reduce_z(parts, came, *others):
-        return across(part_sum(order, tie(parts[0], *others), came, depth))
 
     def tensor_sum(other, own):
         term = (own + sibling(other).astype(F32)).astype(BF)
@@ -654,41 +690,52 @@
             bit *= 2
         return term, swap(term, "tp", nt, bit)
 
-    def columns_relative(value):
+    order = jnp.stack(
+        [(y_index ^ a) * nc + (z_index ^ b) for a in range(nf) for b in range(nc)]
+    ).astype(jnp.int32)
+    place = jnp.concatenate([side.reshape(1).astype(jnp.int32), order])
+
+    def columns_moved(value):
         return jnp.concatenate(
             [
-                lax.dynamic_slice_in_dim(
-                    value, ((y_index ^ a) * nc + (z_index ^ b)) * depth, depth, axis=1
-                )
-                for a in range(nf)
-                for b in range(nc)
+                lax.dynamic_slice_in_dim(value, order[number] * depth, depth, axis=1)
+                for number in range(nf * nc)
             ],
             axis=1,
         )
 
-    def take_half(value, which):
-        return lax.dynamic_slice_in_dim(value, which * half, half)
-
-    def columns_canonical(own, oth):
-        rows_all = jnp.where(
-            side == 0, jnp.concatenate([own, oth], axis=0), jnp.concatenate([oth, own], axis=0)
+    def to_relative(value):
+        if depth % 128 == 0:
+            return call(
+                to_relative_kernel,
+                [shaped((half, width), value.dtype)] * 2,
+                [place, value],
+                value.size,
+                smem=1,
+            )
+        moved = columns_moved(value)
+        return [lax.dynamic_slice_in_dim(moved, which * half, half) for which in (side, 1 - side)]
+
+    def from_relative(own, oth):
+        if depth % 128 == 0:
+            return call(
+                from_relative_kernel, shaped((rows, width), own.dtype), [place, own, oth], 2 * own.size, smem=1
+            )
+        return columns_moved(
+            jnp.where(side == 0, jnp.concatenate([own, oth], axis=0), jnp.concatenate([oth, own], axis=0))
         )
-        return columns_relative(rows_all)
 
     per_device = rows // BLK
     count = nc * per_device
-    place = block_place[0]
+    stored_place = block_place[0]
     stored = jnp.arange(count, dtype=jnp.int32)
     relative = (stored // per_device) * per_device + (stored % per_device + side * (per_device // 2)) % per_device
     source = jnp.sum(
-        jnp.where(place[None, :] == jnp.arange(count, dtype=jnp.int32)[:, None], relative[None, :], 0), axis=1
+        jnp.where(stored_place[None, :] == jnp.arange(count, dtype=jnp.int32)[:, None], relative[None, :], 0), axis=1
     ).astype(jnp.int32)
     head = (t_index * heads + z_index).astype(F32)
     slope = jnp.exp2(-8.0 * (head + 1.0) / HEADS).reshape(1)
     segments = segment_ids
-    order = jnp.stack(
-        [(y_index ^ a) * nc + (z_index ^ b) for a in range(nf) for b in range(nc)]
-    ).astype(jnp.int32)
 
     def qkv_shard(layer):
         return [qkv_weight[layer, :, i, :] for i in range(3)]
@@ -717,22 +764,23 @@
     ]
     up_biases = [up_bias[l].astype(F32).reshape(1, hidden) for l in range(LAYERS)]
 
-    x_all = columns_relative(tokens)
-    x_half = take_half(x_all, side)
+    x_half, x_oth = to_relative(tokens)
     n_own = norm_stats(x_half.astype(F32))[0]
-    n_oth = norm_stats(take_half(x_all, 1 - side).astype(F32))[0]
+    n_oth = norm_stats(x_oth.astype(F32))[0]
     h_own, h_oth, qkv_sent = first_qkv(order, n_own, n_oth, table, 0, biases[0], first_pack, depth, extra)
 
     out_up_shard = tie(jnp.concatenate([out_weight[0], up_weight[0]], axis=1), *first_z)
     out_up_z = gather_z(out_up_shard)
     out_up = gather_y(out_up_shard, out_up_z)
     out_packs, qkv_packs, up_packs = [(out_up, 0)], [(first_pack, 0, extra)], [(out_up, local)]
-    shared = whole_gather(
-        tie(jnp.concatenate([down_weight[0], out_weight[1], *qkv_shard(1)], axis=1), *first_z)
-    )
-    down_packs = [([shared], 0)]
-    out_packs.append(([shared], hidden))
-    qkv_packs.append(([shared], hidden + local, 0))
+    next_out_qkv = whole_gather(
+        tie(jnp.concatenate([out_weight[1], *qkv_shard(1)], axis=1), *first_z)
+    )
+    down_shard = tie(down_weight[0], *out_up_z)
+    down_z = gather_z(down_shard, True)
+    down_packs = [(gather_y(down_shard, down_z), 0)]
+    out_packs.append(([next_out_qkv], 0))
+    qkv_packs.append(([next_out_qkv], local, 0))
 
     records = []
     last_other = last_own = None
@@ -741,14 +789,14 @@
         qkv = across(qkv_sent)
         if l == 0:
             next_mlp = whole_gather(
-                tie(jnp.concatenate([up_weight[1], down_weight[1]], axis=1), shared)
+                tie(jnp.concatenate([up_weight[1], down_weight[1]], axis=1), next_out_qkv)
             )
             up_packs.append(([next_mlp], 0))
             down_packs.append(([next_mlp], hidden))
         o_stream, lse = attend(qkv, source, slope, segments)
         o_rows = across(o_stream)
         if l == 0:
-            pass
+            o_rows = tie(o_rows, *down_z)
         other = out_project(order, o_rows, *out_packs[l], depth, width, half, BF)
         own = out_project(order, tie(o_rows, other), *out_packs[l], depth, width, 0, F32)
         a, b = tensor_sum(other, own)
@@ -765,20 +813,19 @@
         else:
             last_other, last_own = other, own
 
-    g_all = columns_relative(cotangent)
-    gz_own, gz_oth = take_half(g_all, side), take_half(g_all, 1 - side)
+    gz_own, gz_oth = to_relative(cotangent)
     gx_half = gz_own.astype(F32)
     sums = [None] * LAYERS
-    mlp_pieces = [None] * LAYERS
-    above = None
+    late = [None] * LAYERS
+    above = ()
     for l in reversed(range(LAYERS)):
         row = l * NORM_ROWS
         x_half, h_own, h_oth, qkv, lse, o_rows, y_half, h2_own, h2_oth, u = records[l]
         act, gu, up_sum, other, own = mlp_backward(order, gz_own, gz_oth, u, up_packs[l], down_packs[l], depth)
         a, b = tensor_sum(other, own)
-        parts = mlp_grad(order, gz_own, gz_oth, h2_own, h2_oth, tie(act, a), gu, 1)
-        b = tie(b, *parts)
-        mlp_pieces[l] = whole_scatter(parts[0])
+        total = late_grad(order, (gz_own, gz_oth, h2_own, h2_oth, tie(act, a), gu), above)
+        b = tie(b, total)
+        late[l] = whole_scatter(tie(total, *late[l + 1 :]))
         gy_half, ga_own, sums_two = norm_backward(gx_half, a, b, y_half, table, row + 1)
         ga_oth = sibling(ga_own)
         g_stream = across(out_backward(order, ga_own, ga_oth, *out_packs[l], depth, local))
@@ -786,76 +833,86 @@
             a, b = tensor_sum(tie(last_other, g_stream), last_own)
             final_half = y_half + (a.astype(F32) + b.astype(F32) + table[row + 5])
             final_low = final_half.astype(BF)
-            block_output = columns_canonical(final_low, sibling(final_low))
+            block_output = from_relative(final_low, sibling(final_low))
         g_sent = attend_backward(qkv, g_stream, lse, source, slope, segments)
         g_rows = across(g_sent)
-        if l < LAYERS - 1:
-            above = reduce_z(*above, g_rows)
         g_proj, qkv_sum, other, own = qkv_backward(
             order, g_rows, qkv_packs[l][0], qkv_packs[l][1], depth, qkv_packs[l][2], width
         )
         a, b = tensor_sum(other, own)
         sources = (order, ga_own, ga_oth, o_rows, h_own, h_oth)
-        if l == LAYERS - 1:
-            attn = attention_grad(0, 4, *sources, tie(g_proj, a), nf)
-            above = (attn, send_y(attn))
-            b = tie(b, *attn)
+        if l > 0:
+            above = (*sources[1:], g_proj)
         else:
-            out_q = attention_grad(0, 2, *sources, g_proj, nf)
+            out_q = attention_grad(0, 2, *sources, tie(g_proj, a), nf)
             out_q_came = send_y(out_q)
-            kv = attention_grad(2, 4, *sources, tie(g_proj, *out_q), nf)
-            kv_came = send_y(kv)
-            b = tie(b, *kv)
+            last_parts = attention_grad(2, 4, *sources, tie(g_proj, *out_q), nf)
+            last_came = send_y(last_parts)
+            b = tie(b, *last_parts)
         gx_half, gz_own, sums_one = norm_backward(gy_half, a, b, x_half, table, row)
         if l > 0:
             gz_oth = sibling(gz_own)
         sums[l] = (sums_one, sums_two, qkv_sum, up_sum)
-    out_q_pieces = reduce_z(out_q, out_q_came, above)
-    kv_pieces = reduce_z(kv, kv_came, out_q_pieces)
-
-    grad_tokens = columns_canonical(gx_half, sibling(gx_half))
-
+    grad_tokens = from_relative(gx_half, sibling(gx_half))
+
+    norm_all = jnp.concatenate([sums[l][which] for l in range(LAYERS) for which in (0, 1)], axis=0)
+    bias_all = jnp.concatenate(
+        [sums[l][2][:, :local] for l in range(LAYERS)]
+        + [sums[l][2][:, 2 * local :] for l in range(LAYERS)]
+        + [sums[l][3] for l in range(LAYERS)],
+        axis=1,
+    ).reshape(-1, depth)
+    count = norm_all.shape[0]
+    norm_total = norm_all[:, :span]
+    bias_total = bias_all
+    for bit in range(1, nf):
+        sent = jnp.concatenate(
+            [norm_all[:, bit * span + b * depth : bit * span + (b + 1) * depth] for b in range(nc)] + [bias_all],
+            axis=0,
+        )
+        came = swap(sent, "fsdp", nf, bit)
+        norm_total = norm_total + jnp.concatenate(
+            [came[b * count : (b + 1) * count] for b in range(nc)], axis=1
+        )
+        bias_total = bias_total + came[nc * count :]
+    cols = last_parts[0].shape[1]
+    held = count * depth + bias_total.size
+    extra_rows = -(-held // (16 * cols)) * 16
+    small = jnp.concatenate(
+        [
+            norm_total.reshape(count, nc, depth).transpose(1, 0, 2).reshape(nc, -1),
+            jnp.broadcast_to(bias_total.reshape(1, -1), (nc, bias_total.size)),
+            jnp.zeros((nc, extra_rows * cols - held), F32),
+        ],
+        axis=1,
+    ).reshape(nc, extra_rows, cols)
+    nothing = jnp.zeros((nc, 16, cols), F32)
+    out_q_sums = part_sum(order, out_q[0], nothing, out_q_came)
+    out_q_pieces = across(out_q_sums)
+    last_sums = part_sum(order, tie(last_parts[0], out_q_pieces), small, last_came)
+    last_pieces = across(last_sums)
+    small = jnp.sum(last_pieces[:, depth:, :].astype(F32), axis=0).reshape(-1)
+    norm_mine = small[: count * depth].reshape(count, depth)
+    bias_sum = small[count * depth : held]
     grad_up, grad_down = final_sums(
         [[(l, l, col) for l in range(LAYERS)] for col in (0, hidden)],
         [shaped((LAYERS, depth, hidden), F32)] * 2,
-        mlp_pieces,
-    )
-    qkv_plan = [((1, i), 2, (i + 1) * local) for i in range(3)]
-    qkv_plan += [((0, 0), 0, local), ((0, 1), 1, 0), ((0, 2), 1, local)]
+        late,
+    )
+    qkv_plan = [((1, i), 1, 2 * hidden + (i + 1) * local) for i in range(3)]
+    qkv_plan += [((0, 0), 2, local), ((0, 1), 0, 0), ((0, 2), 0, local)]
     grad_out, grad_qkv = final_sums(
-        [[(0, 0, 0), (1, 2, 0)], qkv_plan],
+        [[(0, 2, 0), (1, 1, 2 * hidden)], qkv_plan],
         [shaped((LAYERS, depth, local), F32), shaped((LAYERS, 3, depth, local), F32)],
-        [out_q_pieces, kv_pieces, above],
+        [last_pieces, late[0], out_q_pieces],
     )
     grad_qkv = grad_qkv.transpose(0, 2, 1, 3)
 
-    norm_parts = []
-    for l in range(LAYERS):
-        one, two = sums[l][0], sums[l][1]
-        norm_parts += [one[0], two[0], one[1], two[2], two[1], two[3]]
-    norm_all = jnp.stack(norm_parts)
-    bias_all = jnp.concatenate(
-        [sums[l][2][0, :local] for l in range(LAYERS)]
-        + [sums[l][2][0, 2 * local :] for l in range(LAYERS)]
-        + [sums[l][3][0] for l in range(LAYERS)]
-    )
-    count_norm = norm_all.shape[0]
-    by_part = norm_all.reshape(count_norm, nf, nc, depth).transpose(1, 2, 3, 0).reshape(nf, nc, -1)
-    norm_total = by_part[0]
-    bias_total = bias_all
-    size = nc * depth * count_norm
-    for bit in range(1, nf):
-        came = swap(jnp.concatenate([by_part[bit].reshape(-1), bias_all]), "fsdp", nf, bit)
-        norm_total = norm_total + came[:size].reshape(norm_total.shape)
-        bias_total = bias_total + came[size:]
-    norm_mine = norm_total[0]
-    bias_sum = bias_total
-    for bit in range(1, nc):
-        came = swap(jnp.concatenate([norm_total[bit], bias_total]), "ctx", nc, bit)
-        norm_mine = norm_mine + came[: depth * count_norm]
-        bias_sum = bias_sum + came[depth * count_norm :]
-    norm_mine = (norm_mine + sibling(norm_mine)).reshape(depth, LAYERS, count_norm // LAYERS)
-    norm_mine = norm_mine.transpose(1, 0, 2)
+    norm_mine = (norm_mine + sibling(norm_mine)).reshape(LAYERS, 2, 8, depth)
+    grad_gains = norm_mine[:, :, 0].transpose(0, 2, 1)
+    grad_shifts = jnp.stack(
+        [norm_mine[:, 0, 1], norm_mine[:, 1, 2], norm_mine[:, 1, 1], norm_mine[:, 1, 3]], axis=1
+    ).transpose(0, 2, 1)
     queries, values = bias_sum[: LAYERS * local], bias_sum[LAYERS * local : 2 * LAYERS * local]
     grad_bias = jnp.stack([queries.reshape(LAYERS, local), values.reshape(LAYERS, local)], axis=1)
     grad_up_bias = bias_sum[2 * LAYERS * local :].reshape(LAYERS, hidden)
@@ -869,8 +926,8 @@
         grad_down,
         grad_bias,
         grad_up_bias,
-        norm_mine[:, :, :2],
-        norm_mine[:, :, 2:],
+        grad_gains,
+        grad_shifts,
     )
 
 

time: 596 us -> 590 us (0.990)
  local copies, waits for them, and re-layouts: 96.5 us -> 49.5 us
  waiting for transfers between devices: 222 us -> 237 us
  starting transfers between devices: 64.1 us -> 77.9 us
  blocking collectives: 95.6 us -> 103 us
    unnamed x266 -> x261, local copies, waits for them, and re-layouts: 78 us -> 40.2 us
    all_to_all x7 -> x5, waiting for transfers between devices: 52.9 us -> 85.9 us  [across(): return lax.all_to_all(value, 'ctx', 0, 0)]
    ppermute x41 -> x40, starting transfers between devices: 34.6 us -> 58 us  [swap(): return lax.ppermute(value, axis, [(i, i ^ bit) for i in range(size)])]
    ppermute x41 -> x40, waiting for transfers between devices: 167 us -> 151 us  [swap(): return lax.ppermute(value, axis, [(i, i ^ bit) for i in range(size)])]
    all_to_all x7 -> x5, starting transfers between devices: 29.1 us -> 19.2 us  [across(): return lax.all_to_all(value, 'ctx', 0, 0)]
    all_to_all x4 -> x5, blocking collectives: 95.6 us -> 103 us  [across(): return lax.all_to_all(value, 'ctx', 0, 0)]
    pallas_call x31 -> x33, Pallas kernels: 53.4 us -> 58.2 us  [call(): pl.pallas_call(kernel, in_specs=specs, out_specs=[whole()] * len(outs) if...]
  transfers between devices with their start and end apart: 52 -> 49, of which waited for: 30 -> 27; matrix products, arithmetic and copies ran while one was open for 12% -> 4% of each run, Pallas kernels for 11% -> 12%
where the time goes in v4:
time: 590 us; the launch traced here: 582 us
  waiting for transfers between devices  237 us (40%)
  blocking collectives  103 us (17%)
  Pallas kernels  81.1 us (14%)
  starting transfers between devices  77.9 us (13%)
  local copies, waits for them, and re-layouts  49.5 us (8%)
  other arithmetic  18 us (3%)
  between operations  15.5 us (3%)
    ppermute x40, waiting for transfers between devices, swap(): return lax.ppermute(value, axis, [(i, i ^ bit) for i in range(size)])  151 us
    all_to_all x5, blocking collectives, across(): return lax.all_to_all(value, 'ctx', 0, 0)  103 us
    all_to_all x5, waiting for transfers between devices, across(): return lax.all_to_all(value, 'ctx', 0, 0)  85.9 us
    pallas_call x33, Pallas kernels, call(): pl.pallas_call(kernel, in_specs=specs, out_specs=[whole()] * len(outs) if...  58.2 us
    ppermute x40, starting transfers between devices, swap(): return lax.ppermute(value, axis, [(i, i ^ bit) for i in range(size)])  58 us
    unnamed x261, local copies, waits for them, and re-layouts  40.2 us
    all_to_all x5, starting transfers between devices, across(): return lax.all_to_all(value, 'ctx', 0, 0)  19.2 us
    pallas_call x2, Pallas kernels, attend_backward(): pl.pallas_call(partial(attend_back_kernel, rows // BLK), in_specs=[smem,...  13.6 us
  transfers between devices with their start and end apart: 49, of which 27 were waited for; matrix products, arithmetic and copies ran while one was open for 4% of the time, Pallas kernels for 12%

profile of v4, /device:TPU:0, one launch (start us, length us, event | category | flops | bytes accessed | tf_op | source)
XLA Modules:
  0.0 582.0 jit_solution(12955566339109915448)
XLA Ops:
  25.3 7.9 %collective-permute-done.1.refs_2_ = bf16[144,768]{1,0:T(8,128)(2,1)S(1)} collective-permute-done((bf16[144,768]{1,0:T(8,128)(2,1)}, bf16[144,768]{1,0:T(8,128)(2,1)S(1)}, u32[]{:S(2)}, u32[]{:S(2)}) %collective-permute-start.1) | collective-permute-done | bytes 221216 | tf_op jit(solution)/shard_map/ppermute | solution.py:645
  44.8 14.2 %collective-permute-done.4.refs_5_ = bf16[432,768]{1,0:T(8,128)(2,1)S(1)} collective-permute-done((bf16[432,768]{1,0:T(8,128)(2,1)S(1)}, bf16[432,768]{1,0:T(8,128)(2,1)S(1)}, u32[]{:S(2)}, u32[]{:S(2)}) %collective-permute-start.4) | collective-permute-done | bytes 663584 | tf_op jit(solution)/shard_map/ppermute | solution.py:645
  74.3 22.6 %collective-permute-start.8 = (bf16[128,1024]{1,0:T(8,128)(2,1)S(1)}, bf16[128,1024]{1,0:T(8,128)(2,1)S(1)}, u32[]{:S(2)}, u32[]{:S(2)}) collective-permute-start(bf16[128,1024]{1,0:T(8,128)(2,1)S(1)} %get-tuple-element.94.refs_5_), channel_id=1, source_target_pairs={{0,4},{4,0},{8,12},{12,8},{1,5},{5,1},{9,13},{13,9},{2,6},{6,2},{1... | collective-permute-start | bytes 786440 | tf_op jit(solution)/shard_map/ppermute | solution.py:645
  96.9 11.4 %collective-permute-done.8.refs_6_ = bf16[128,1024]{1,0:T(8,128)(2,1)S(1)} collective-permute-done((bf16[128,1024]{1,0:T(8,128)(2,1)S(1)}, bf16[128,1024]{1,0:T(8,128)(2,1)S(1)}, u32[]{:S(2)}, u32[]{:S(2)}) %collective-permute-start.8) | collective-permute-done | bytes 262176 | tf_op jit(solution)/shard_map/ppermute | solution.py:645
  110.3 14.4 %all-to-all-done.qkv_ref = bf16[4,192,512]{2,1,0:T(8,128)(2,1)} async-done(((bf16[4,192,512]{2,1,0:T(8,128)(2,1)}), bf16[4,192,512]{2,1,0:T(8,128)(2,1)}, u32[]{:S(2)}, u32[]{:S(2)}) %all-to-all-start) | async-done | bytes 786464 | tf_op jit(solution)/shard_map/all_to_all | solution.py:651
  134.8 6.7 %all-to-all-done.1.o_ref.refs_2_ = bf16[4,64,512]{2,1,0:T(8,128)(2,1)S(1)} async-done(((bf16[4,64,512]{2,1,0:T(8,128)(2,1)}), bf16[4,64,512]{2,1,0:T(8,128)(2,1)S(1)}, u32[]{:S(2)}, u32[]{:S(2)}) %all-to-all-start.1) | async-done | bytes 262176 | tf_op jit(solution)/shard_map/all_to_all | solution.py:651
  152.9 10.1 %collective-permute-done.12.b_ref = bf16[256,1024]{1,0:T(8,128)(2,1)S(1)} collective-permute-done((bf16[256,1024]{1,0:T(8,128)(2,1)S(1)}, bf16[256,1024]{1,0:T(8,128)(2,1)S(1)}, u32[]{:S(2)}, u32[]{:S(2)}) %collective-permute-start.12) | collective-permute-done | bytes 524320 | tf_op jit(solution)/shard_map/ppermute | solution.py:645
  163.7 18.6 %collective-permute-done.14.refs_8_ = bf16[512,1024]{1,0:T(8,128)(2,1)S(1)} collective-permute-done((bf16[512,1024]{1,0:T(8,128)(2,1)S(1)}, bf16[512,1024]{1,0:T(8,128)(2,1)S(1)}, u32[]{:S(2)}, u32[]{:S(2)}) %collective-permute-start.14) | collective-permute-done | bytes 1048608 | tf_op jit(solution)/shard_map/ppermute | solution.py:645
  190.2 13.4 %collective-permute-done.16.b_ref = bf16[256,1024]{1,0:T(8,128)(2,1)S(1)} collective-permute-done((bf16[256,1024]{1,0:T(8,128)(2,1)S(1)}, bf16[256,1024]{1,0:T(8,128)(2,1)S(1)}, u32[]{:S(2)}, u32[]{:S(2)}) %collective-permute-start.16) | collective-permute-done | bytes 524320 | tf_op jit(solution)/shard_map/ppermute | solution.py:645
  208.5 29.7 %all_to_all.50.qkv_ref = bf16[4,192,512]{2,1,0:T(8,128)(2,1)S(1)} all-to-all(bf16[4,192,512]{2,1,0:T(8,128)(2,1)S(1)} %shard_map.203), channel_id=1, replica_groups=mesh['fsdp'=2,'ctx'=4,'tp'=4] {'ctx'}, dimensions={0} | all-to-all | bytes 1572864 | tf_op jit(solution)/shard_map/all_to_all | solution.py:651
  243.2 11.8 %all_to_all.51.o_ref.refs_8_ = bf16[4,64,512]{2,1,0:T(8,128)(2,1)S(1)} all-to-all(bf16[4,64,512]{2,1,0:T(8,128)(2,1)S(1)} %get-tuple-element.104), channel_id=1, replica_groups=mesh['fsdp'=2,'ctx'=4,'tp'=4] {'ctx'}, dimensions={0} | all-to-all | bytes 524288 | tf_op jit(solution)/shard_map/all_to_all | solution.py:651
  259.6 12.4 %collective-permute-done.19.b_ref = bf16[256,1024]{1,0:T(8,128)(2,1)S(1)} collective-permute-done((bf16[256,1024]{1,0:T(8,128)(2,1)S(1)}, bf16[256,1024]{1,0:T(8,128)(2,1)S(1)}, u32[]{:S(2)}, u32[]{:S(2)}) %collective-permute-start.19) | collective-permute-done | bytes 524320 | tf_op jit(solution)/shard_map/ppermute | solution.py:645
  300.8 11.7 %collective-permute-done.22.b_ref = bf16[256,1024]{1,0:T(8,128)(2,1)S(1)} collective-permute-done((bf16[256,1024]{1,0:T(8,128)(2,1)}, bf16[256,1024]{1,0:T(8,128)(2,1)S(1)}, u32[]{:S(2)}, u32[]{:S(2)}) %collective-permute-start.22) | collective-permute-done | bytes 524320 | tf_op jit(solution)/shard_map/ppermute | solution.py:645
  317.7 20.0 %all_to_all.52.g_ref = bf16[4,64,512]{2,1,0:T(8,128)(2,1)S(1)} all-to-all(bf16[4,64,512]{2,1,0:T(8,128)(2,1)S(1)} %shard_map.213), channel_id=1, replica_groups=mesh['fsdp'=2,'ctx'=4,'tp'=4] {'ctx'}, dimensions={0} | all-to-all | bytes 524288 | tf_op jit(solution)/shard_map/all_to_all | solution.py:651
  337.7 6.0 %shard_map.215 = bf16[4,192,512]{2,1,0:T(8,128)(2,1)S(1)} custom-call(s32[16]{0:T(128)S(1)} %copy-done.99, f32[1]{0:T(128)} %bitcast.10.slope_ref, s32[1,2048]{1,0:T(1,128)S(1)} %copy-done.95, bf16[4,192,512]{2,1,0:T(8,128)(2,1)S(1)} %copy-done.72, bf16[4,64,512]{2,1,0:T(8,128)(2,1)S(1)} %all_to_all.52.g_ref, f32[1,2048]{1,0:T(1,128)S(1)} %copy-done.106), custom_call_target="tpu_custom_call" | custom-call | flops 939524096 | bytes 2097152 | tf_op jit(solution)/shard_map/pallas_call | solution.py:577
  343.7 22.1 %all_to_all.53.g_ref = bf16[4,192,512]{2,1,0:T(8,128)(2,1)S(1)} all-to-all(bf16[4,192,512]{2,1,0:T(8,128)(2,1)S(1)} %shard_map.215), channel_id=1, replica_groups=mesh['fsdp'=2,'ctx'=4,'tp'=4] {'ctx'}, dimensions={0} | all-to-all | bytes 1572864 | tf_op jit(solution)/shard_map/all_to_all | solution.py:651
  371.2 12.4 %collective-permute-done.28.b_ref = bf16[256,1024]{1,0:T(8,128)(2,1)S(1)} collective-permute-done((bf16[256,1024]{1,0:T(8,128)(2,1)S(1)}, bf16[256,1024]{1,0:T(8,128)(2,1)S(1)}, u32[]{:S(2)}, u32[]{:S(2)}) %collective-permute-start.28) | collective-permute-done | bytes 524320 | tf_op jit(solution)/shard_map/ppermute | solution.py:645
  403.6 12.6 %collective-permute-done.31.b_ref = bf16[256,1024]{1,0:T(8,128)(2,1)S(1)} collective-permute-done((bf16[256,1024]{1,0:T(8,128)(2,1)}, bf16[256,1024]{1,0:T(8,128)(2,1)S(1)}, u32[]{:S(2)}, u32[]{:S(2)}) %collective-permute-start.31) | collective-permute-done | bytes 524320 | tf_op jit(solution)/shard_map/ppermute | solution.py:645
  423.9 19.5 %all_to_all.54.g_ref = bf16[4,64,512]{2,1,0:T(8,128)(2,1)S(1)} all-to-all(bf16[4,64,512]{2,1,0:T(8,128)(2,1)S(1)} %shard_map.221), channel_id=1, replica_groups=mesh['fsdp'=2,'ctx'=4,'tp'=4] {'ctx'}, dimensions={0} | all-to-all | bytes 524288 | tf_op jit(solution)/shard_map/all_to_all | solution.py:651
  443.6 7.6 %shard_map.222 = bf16[4,192,512]{2,1,0:T(8,128)(2,1)} custom-call(s32[16]{0:T(128)S(1)} %copy-done.100, f32[1]{0:T(128)} %bitcast.10.slope_ref, s32[1,2048]{1,0:T(1,128)S(1)} %copy-done.96, bf16[4,192,512]{2,1,0:T(8,128)(2,1)} %all-to-all-done.qkv_ref, bf16[4,64,512]{2,1,0:T(8,128)(2,1)S(1)} %all_to_all.54.g_ref, f32[1,2048]{1,0:T(1,128)S(1)} %copy-done.104), custom_call_target="tpu_custom_call" | custom-call | flops 939524096 | bytes 2097152 | tf_op jit(solution)/shard_map/pallas_call | solution.py:577
  456.2 27.6 %all-to-all-done.7.g_ref = bf16[4,192,512]{2,1,0:T(8,128)(2,1)} async-done(((bf16[4,192,512]{2,1,0:T(8,128)(2,1)}), bf16[4,192,512]{2,1,0:T(8,128)(2,1)}, u32[]{:S(2)}, u32[]{:S(2)}) %all-to-all-start.7) | async-done | bytes 786464 | tf_op jit(solution)/shard_map/all_to_all | solution.py:651
  497.8 6.6 %collective-permute-done.34.b_ref = bf16[256,1024]{1,0:T(8,128)(2,1)S(1)} collective-permute-done((bf16[256,1024]{1,0:T(8,128)(2,1)S(1)}, bf16[256,1024]{1,0:T(8,128)(2,1)S(1)}, u32[]{:S(2)}, u32[]{:S(2)}) %collective-permute-start.34) | collective-permute-done | bytes 524320 | tf_op jit(solution)/shard_map/ppermute | solution.py:645
  518.2 31.5 %all-to-all-done.8.refs_2_ = bf16[4,144,512]{2,1,0:T(8,128)(2,1)S(1)} async-done(((bf16[4,144,512]{2,1,0:T(8,128)(2,1)}), bf16[4,144,512]{2,1,0:T(8,128)(2,1)S(1)}, u32[]{:S(2)}, u32[]{:S(2)}) %all-to-all-start.8) | async-done | bytes 589856 | tf_op jit(solution)/shard_map/all_to_all | solution.py:651
  563.6 5.6 all-to-all-done.9.refs_0_
  (450 shorter events, 209.9 us)
Async XLA Ops:
  7.2 137.8 %all-gather.3.cloned.1.call-start = ((), (), s32[]{:S(2)}) async-start(), calls=%async_computation.12 | async-start | bytes 2359296 | tf_op jit(solution)/shard_map/all_gather | solution.py:677
  14.2 18.9 %collective-permute-start.1 = (bf16[144,768]{1,0:T(8,128)(2,1)}, bf16[144,768]{1,0:T(8,128)(2,1)S(1)}, u32[]{:S(2)}, u32[]{:S(2)}) collective-permute-start(bf16[144,768]{1,0:T(8,128)(2,1)} %fusion.7.refs_0_), channel_id=1, source_target_pairs={{0,8},{4,12},{8,0},{12,4},{1,9},{5,13},{9,1},{13,5},{2,10},{6,14},... | collective-permute-start | bytes 663560 | tf_op jit(solution)/shard_map/ppermute | solution.py:645
  16.8 24.4 %collective-permute-start.3 = (bf16[144,768]{1,0:T(8,128)(2,1)}, bf16[144,768]{1,0:T(8,128)(2,1)}, u32[]{:S(2)}, u32[]{:S(2)}) collective-permute-start(bf16[144,768]{1,0:T(8,128)(2,1)} %fusion.7.refs_0_), channel_id=1, source_target_pairs={{0,16},{16,0},{1,17},{17,1},{2,18},{18,2},{3,19},{19,3},{4,20},{20... | collective-permute-start | bytes 663560 | tf_op jit(solution)/shard_map/ppermute | solution.py:645
  33.8 36.3 %collective-permute-start.5 = (bf16[128,1280]{1,0:T(8,128)(2,1)S(1)}, bf16[128,1280]{1,0:T(8,128)(2,1)S(1)}, u32[]{:S(2)}, u32[]{:S(2)}) collective-permute-start(bf16[128,1280]{1,0:T(8,128)(2,1)S(1)} %pad_maximum_fusion.5.refs_0_), channel_id=1, source_target_pairs={{0,4},{4,0},{8,12},{12,8},{1,5},{5,1},{9,13},{13,9},{2,6},{6,2},{1... | collective-permute-start | bytes 983048 | tf_op jit(solution)/shard_map/ppermute | solution.py:645
  37.2 32.9 %collective-permute-start.6 = (bf16[128,1280]{1,0:T(8,128)(2,1)S(1)}, bf16[128,1280]{1,0:T(8,128)(2,1)S(1)}, u32[]{:S(2)}, u32[]{:S(2)}) collective-permute-start(bf16[128,1280]{1,0:T(8,128)(2,1)S(1)} %pad_maximum_fusion.5.refs_0_), channel_id=1, source_target_pairs={{0,8},{4,12},{8,0},{12,4},{1,9},{5,13},{9,1},{13,5},{2,10},{6,14},... | collective-permute-start | bytes 983048 | tf_op jit(solution)/shard_map/ppermute | solution.py:645
  38.7 31.4 %collective-permute-start.7 = (bf16[128,1280]{1,0:T(8,128)(2,1)S(1)}, bf16[128,1280]{1,0:T(8,128)(2,1)S(1)}, u32[]{:S(2)}, u32[]{:S(2)}) collective-permute-start(bf16[128,1280]{1,0:T(8,128)(2,1)S(1)} %pad_maximum_fusion.5.refs_0_), channel_id=1, source_target_pairs={{0,12},{4,8},{8,4},{12,0},{1,13},{5,9},{9,5},{13,1},{2,14},{6,10},... | collective-permute-start | bytes 983048 | tf_op jit(solution)/shard_map/ppermute | solution.py:645
  41.2 17.8 %collective-permute-start.4 = (bf16[432,768]{1,0:T(8,128)(2,1)S(1)}, bf16[432,768]{1,0:T(8,128)(2,1)S(1)}, u32[]{:S(2)}, u32[]{:S(2)}) collective-permute-start(bf16[432,768]{1,0:T(8,128)(2,1)S(1)} %pad_maximum_fusion.2), channel_id=1, source_target_pairs={{0,16},{16,0},{1,17},{17,1},{2,18},{18,2},{3,19},{19,3},{4,20},{20... | collective-permute-start | bytes 1990664 | tf_op jit(solution)/shard_map/ppermute | solution.py:645
  65.8 58.9 %all-to-all-start = ((bf16[4,192,512]{2,1,0:T(8,128)(2,1)}), bf16[4,192,512]{2,1,0:T(8,128)(2,1)}, u32[]{:S(2)}, u32[]{:S(2)}) async-start(bf16[4,192,512]{2,1,0:T(8,128)(2,1)} %copy-done.73), calls=%async_computation | async-start | bytes 1572864 | tf_op jit(solution)/shard_map/all_to_all | solution.py:651
  72.0 69.5 %collective-permute-start.10 = (bf16[512,1280]{1,0:T(8,128)(2,1)}, bf16[512,1280]{1,0:T(8,128)(2,1)S(1)}, u32[]{:S(2)}, u32[]{:S(2)}) collective-permute-start(bf16[512,1280]{1,0:T(8,128)(2,1)} %pad_maximum_fusion), channel_id=1, source_target_pairs={{0,16},{16,0},{1,17},{17,1},{2,18},{18,2},{3,19},{19,3},{4,20},{20... | collective-permute-start | bytes 3932168 | tf_op jit(solution)/shard_map/ppermute | solution.py:645
  74.3 34.0 %collective-permute-start.8 = (bf16[128,1024]{1,0:T(8,128)(2,1)S(1)}, bf16[128,1024]{1,0:T(8,128)(2,1)S(1)}, u32[]{:S(2)}, u32[]{:S(2)}) collective-permute-start(bf16[128,1024]{1,0:T(8,128)(2,1)S(1)} %get-tuple-element.94.refs_5_), channel_id=1, source_target_pairs={{0,4},{4,0},{8,12},{12,8},{1,5},{5,1},{9,13},{13,9},{2,6},{6,2},{1... | collective-permute-start | bytes 786440 | tf_op jit(solution)/shard_map/ppermute | solution.py:645
  109.8 25.0 %collective-permute-start.9 = (bf16[256,1024]{1,0:T(8,128)(2,1)}, bf16[256,1024]{1,0:T(8,128)(2,1)}, u32[]{:S(2)}, u32[]{:S(2)}) collective-permute-start(bf16[256,1024]{1,0:T(8,128)(2,1)} %pad_maximum_fusion.3), channel_id=1, source_target_pairs={{0,8},{4,12},{8,0},{12,4},{1,9},{5,13},{9,1},{13,5},{2,10},{6,14},... | collective-permute-start | bytes 1572872 | tf_op jit(solution)/shard_map/ppermute | solution.py:645
  134.8 142.1 %all-gather.5.cloned.1.call-start = ((), (), s32[]{:S(2)}) async-start(), calls=%async_computation.13 | async-start | bytes 4718592 | tf_op jit(solution)/shard_map/all_gather | solution.py:677
  145.1 257.0 %reduce-scatter.3.cloned.1.call-start = ((), (), s32[]{:S(2)}) async-start(), calls=%async_computation.14 | async-start | bytes 4718592 | tf_op jit(solution)/shard_map/reduce_scatter | solution.py:680
  151.3 31.0 %collective-permute-start.14 = (bf16[512,1024]{1,0:T(8,128)(2,1)S(1)}, bf16[512,1024]{1,0:T(8,128)(2,1)S(1)}, u32[]{:S(2)}, u32[]{:S(2)}) collective-permute-start(bf16[512,1024]{1,0:T(8,128)(2,1)S(1)} %pad_maximum_fusion.1), channel_id=1, source_target_pairs={{0,16},{16,0},{1,17},{17,1},{2,18},{18,2},{3,19},{19,3},{4,20},{20... | collective-permute-start | bytes 3145736 | tf_op jit(solution)/shard_map/ppermute | solution.py:645
  163.6 18.7 %collective-permute-start.13 = (bf16[256,1024]{1,0:T(8,128)(2,1)S(1)}, bf16[256,1024]{1,0:T(8,128)(2,1)S(1)}, u32[]{:S(2)}, u32[]{:S(2)}) collective-permute-start(bf16[256,1024]{1,0:T(8,128)(2,1)S(1)} %get-tuple-element.98.h_own.refs_2_), channel_id=1, source_target_pairs={{0,1},{1,0},{2,3},{3,2},{4,5},{5,4},{6,7},{7,6},{8,9},{9,8},{10,11... | collective-permute-start | bytes 1572872 | tf_op jit(solution)/shard_map/ppermute | solution.py:645
  298.0 273.7 %reduce-scatter.5.cloned.1.call-start = ((), (), s32[]{:S(2)}) async-start(), calls=%async_computation.15 | async-start | bytes 7077888 | tf_op jit(solution)/shard_map/reduce_scatter | solution.py:680
  451.1 32.7 %all-to-all-start.7 = ((bf16[4,192,512]{2,1,0:T(8,128)(2,1)}), bf16[4,192,512]{2,1,0:T(8,128)(2,1)}, u32[]{:S(2)}, u32[]{:S(2)}) async-start(bf16[4,192,512]{2,1,0:T(8,128)(2,1)} %shard_map.222), calls=%async_computation.7 | async-start | bytes 1572864 | tf_op jit(solution)/shard_map/all_to_all | solution.py:651
  456.1 52.8 %collective-permute-start.24 = (bf16[256,1024]{1,0:T(8,128)(2,1)}, bf16[256,1024]{1,0:T(8,128)(2,1)}, u32[]{:S(2)}, u32[]{:S(2)}) collective-permute-start(bf16[256,1024]{1,0:T(8,128)(2,1)} %copy-done.92), channel_id=1, source_target_pairs={{0,1},{1,0},{2,3},{3,2},{4,5},{5,4},{6,7},{7,6},{8,9},{9,8},{10,11... | collective-permute-start | bytes 1572872 | tf_op jit(solution)/shard_map/ppermute | solution.py:645
  493.3 19.6 %collective-permute-start.36 = (bf16[512,512]{1,0:T(8,128)(2,1)S(1)}, bf16[512,512]{1,0:T(8,128)(2,1)S(1)}, u32[]{:S(2)}, u32[]{:S(2)}) collective-permute-start(bf16[512,512]{1,0:T(8,128)(2,1)S(1)} %get-tuple-element.146), channel_id=1, source_target_pairs={{0,16},{16,0},{1,17},{17,1},{2,18},{18,2},{3,19},{19,3},{4,20},{20... | collective-permute-start | bytes 1572872 | tf_op jit(solution)/shard_map/ppermute | solution.py:645
  510.9 44.5 %collective-permute-start.25 = (bf16[256,1024]{1,0:T(8,128)(2,1)}, bf16[256,1024]{1,0:T(8,128)(2,1)}, u32[]{:S(2)}, u32[]{:S(2)}) collective-permute-start(bf16[256,1024]{1,0:T(8,128)(2,1)} %add_convert_fusion.4), channel_id=1, source_target_pairs={{0,2},{1,3},{2,0},{3,1},{4,6},{5,7},{6,4},{7,5},{8,10},{9,11},{10,... | collective-permute-start | bytes 1572872 | tf_op jit(solution)/shard_map/ppermute | solution.py:645
  512.3 37.3 %collective-permute-start.38 = (bf16[512,512]{1,0:T(8,128)(2,1)}, bf16[512,512]{1,0:T(8,128)(2,1)S(1)}, u32[]{:S(2)}, u32[]{:S(2)}) collective-permute-start(bf16[512,512]{1,0:T(8,128)(2,1)} %get-tuple-element.149), channel_id=1, source_target_pairs={{0,16},{16,0},{1,17},{17,1},{2,18},{18,2},{3,19},{19,3},{4,20},{20... | collective-permute-start | bytes 1572872 | tf_op jit(solution)/shard_map/ppermute | solution.py:645
  514.4 35.3 %all-to-all-start.8 = ((bf16[4,144,512]{2,1,0:T(8,128)(2,1)}), bf16[4,144,512]{2,1,0:T(8,128)(2,1)S(1)}, u32[]{:S(2)}, u32[]{:S(2)}) async-start(bf16[4,144,512]{2,1,0:T(8,128)(2,1)} %shard_map.228), calls=%async_computation.8 | async-start | bytes 1179648 | tf_op jit(solution)/shard_map/all_to_all | solution.py:651
  517.9 42.8 %collective-permute-start.35 = (f32[256,1024]{1,0:T(8,128)}, f32[256,1024]{1,0:T(8,128)}, u32[]{:S(2)}, u32[]{:S(2)}) collective-permute-start(f32[256,1024]{1,0:T(8,128)} %copy-done.50), channel_id=1, source_target_pairs={{0,1},{1,0},{2,3},{3,2},{4,5},{5,4},{6,7},{7,6},{8,9},{9,8},{10,11... | collective-permute-start | bytes 3145736 | tf_op jit(solution)/shard_map/ppermute | solution.py:645
  551.2 18.0 %all-to-all-start.9 = ((bf16[4,144,512]{2,1,0:T(8,128)(2,1)}), bf16[4,144,512]{2,1,0:T(8,128)(2,1)S(1)}, u32[]{:S(2)}, u32[]{:S(2)}) async-start(bf16[4,144,512]{2,1,0:T(8,128)(2,1)} %shard_map.229), calls=%async_computation.9 | async-start | bytes 1179648 | tf_op jit(solution)/shard_map/all_to_all | solution.py:651
  (145 other events, 2105.5 us)
Sparse Core Ops, SparseCore 0:
  33.3 83.0 all-gather.2
  145.2 85.0 all-gather.4
  298.1 91.2 reduce-scatter.2
  402.2 151.2 reduce-scatter.4

commit v5 on v4

--- a/solution.py
+++ b/solution.py
@@ -817,13 +817,12 @@
     gx_half = gz_own.astype(F32)
     sums = [None] * LAYERS
     late = [None] * LAYERS
-    above = ()
     for l in reversed(range(LAYERS)):
         row = l * NORM_ROWS
         x_half, h_own, h_oth, qkv, lse, o_rows, y_half, h2_own, h2_oth, u = records[l]
         act, gu, up_sum, other, own = mlp_backward(order, gz_own, gz_oth, u, up_packs[l], down_packs[l], depth)
         a, b = tensor_sum(other, own)
-        total = late_grad(order, (gz_own, gz_oth, h2_own, h2_oth, tie(act, a), gu), above)
+        total = late_grad(order, (gz_own, gz_oth, h2_own, h2_oth, tie(act, a), gu), ())
         b = tie(b, total)
         late[l] = whole_scatter(tie(total, *late[l + 1 :]))
         gy_half, ga_own, sums_two = norm_backward(gx_half, a, b, y_half, table, row + 1)
@@ -834,16 +833,26 @@
             final_half = y_half + (a.astype(F32) + b.astype(F32) + table[row + 5])
             final_low = final_half.astype(BF)
             block_output = from_relative(final_low, sibling(final_low))
+        if l < LAYERS - 1:
+            g_stream = tie(g_stream, *above_came)
         g_sent = attend_backward(qkv, g_stream, lse, source, slope, segments)
         g_rows = across(g_sent)
+        if l < LAYERS - 1:
+            above_sums = part_sum(
+                order, tie(above[0], g_sent), jnp.zeros((nc, 16, 4 * local), F32), above_came
+            )
+            g_rows = tie(g_rows, above_sums)
         g_proj, qkv_sum, other, own = qkv_backward(
             order, g_rows, qkv_packs[l][0], qkv_packs[l][1], depth, qkv_packs[l][2], width
         )
         a, b = tensor_sum(other, own)
         sources = (order, ga_own, ga_oth, o_rows, h_own, h_oth)
         if l > 0:
-            above = (*sources[1:], g_proj)
+            above = attention_grad(0, 4, *sources, tie(g_proj, a), nf)
+            above_came = send_y(above)
+            b = tie(b, *above)
         else:
+            above = across(tie(above_sums, g_proj))
             out_q = attention_grad(0, 2, *sources, tie(g_proj, a), nf)
             out_q_came = send_y(out_q)
             last_parts = attention_grad(2, 4, *sources, tie(g_proj, *out_q), nf)
@@ -887,9 +896,9 @@
         axis=1,
     ).reshape(nc, extra_rows, cols)
     nothing = jnp.zeros((nc, 16, cols), F32)
-    out_q_sums = part_sum(order, out_q[0], nothing, out_q_came)
+    out_q_sums = part_sum(order, tie(out_q[0], above), nothing, out_q_came)
     out_q_pieces = across(out_q_sums)
-    last_sums = part_sum(order, tie(last_parts[0], out_q_pieces), small, last_came)
+    last_sums = part_sum(order, tie(last_parts[0], out_q_pieces, late[0]), small, last_came)
     last_pieces = across(last_sums)
     small = jnp.sum(last_pieces[:, depth:, :].astype(F32), axis=0).reshape(-1)
     norm_mine = small[: count * depth].reshape(count, depth)
@@ -899,12 +908,12 @@
         [shaped((LAYERS, depth, hidden), F32)] * 2,
         late,
     )
-    qkv_plan = [((1, i), 1, 2 * hidden + (i + 1) * local) for i in range(3)]
+    qkv_plan = [((1, i), 1, (i + 1) * local) for i in range(3)]
     qkv_plan += [((0, 0), 2, local), ((0, 1), 0, 0), ((0, 2), 0, local)]
     grad_out, grad_qkv = final_sums(
-        [[(0, 2, 0), (1, 1, 2 * hidden)], qkv_plan],
+        [[(0, 2, 0), (1, 1, 0)], qkv_plan],
         [shaped((LAYERS, depth, local), F32), shaped((LAYERS, 3, depth, local), F32)],
-        [last_pieces, late[0], out_q_pieces],
+        [last_pieces, above, out_q_pieces],
     )
     grad_qkv = grad_qkv.transpose(0, 2, 1, 3)
 

time: 590 us -> 582 us (0.986)
  blocking collectives: 103 us -> 84 us
  starting transfers between devices: 77.9 us -> 85 us
  waiting for transfers between devices: 237 us -> 230 us
  Pallas kernels: 81.1 us -> 87.5 us
    all_to_all x5 -> x4, blocking collectives: 103 us -> 84 us  [across(): return lax.all_to_all(value, 'ctx', 0, 0)]
    all_to_all x5 -> x7, waiting for transfers between devices: 85.9 us -> 75 us  [across(): return lax.all_to_all(value, 'ctx', 0, 0)]
    all_to_all x5 -> x7, starting transfers between devices: 19.2 us -> 27 us  [across(): return lax.all_to_all(value, 'ctx', 0, 0)]
    pallas_call x33 -> x35, Pallas kernels: 58.2 us -> 64.6 us  [call(): pl.pallas_call(kernel, in_specs=specs, out_specs=[whole()] * len(outs) if...]
    unnamed x261 -> x289, local copies, waits for them, and re-layouts: 40.2 us -> 43.8 us
    ppermute x40 -> x41, waiting for transfers between devices: 151 us -> 154 us  [swap(): return lax.ppermute(value, axis, [(i, i ^ bit) for i in range(size)])]
    ppermute x40 -> x41, starting transfers between devices: 58 us -> 57.6 us  [swap(): return lax.ppermute(value, axis, [(i, i ^ bit) for i in range(size)])]
  transfers between devices with their start and end apart: 49 -> 52, of which waited for: 27 -> 30; matrix products, arithmetic and copies ran while one was open for 4% -> 4% of each run, Pallas kernels for 12% -> 13%
where the time goes in v5:
time: 582 us; the launch traced here: 574 us
  waiting for transfers between devices  230 us (40%)
  Pallas kernels  87.5 us (15%)
  starting transfers between devices  85 us (15%)
  blocking collectives  84 us (14%)
  local copies, waits for them, and re-layouts  53.2 us (9%)
  other arithmetic  19.4 us (3%)
  between operations  15.8 us (3%)
    ppermute x41, waiting for transfers between devices, swap(): return lax.ppermute(value, axis, [(i, i ^ bit) for i in range(size)])  154 us
    all_to_all x4, blocking collectives, across(): return lax.all_to_all(value, 'ctx', 0, 0)  84 us
    all_to_all x7, waiting for transfers between devices, across(): return lax.all_to_all(value, 'ctx', 0, 0)  75 us
    pallas_call x35, Pallas kernels, call(): pl.pallas_call(kernel, in_specs=specs, out_specs=[whole()] * len(outs) if...  64.6 us
    ppermute x41, starting transfers between devices, swap(): return lax.ppermute(value, axis, [(i, i ^ bit) for i in range(size)])  57.6 us
    unnamed x289, local copies, waits for them, and re-layouts  43.8 us
    all_to_all x7, starting transfers between devices, across(): return lax.all_to_all(value, 'ctx', 0, 0)  27 us
    pallas_call x2, Pallas kernels, attend_backward(): pl.pallas_call(partial(attend_back_kernel, rows // BLK), in_specs=[smem,...  13.5 us
  transfers between devices with their start and end apart: 52, of which 30 were waited for; matrix products, arithmetic and copies ran while one was open for 4% of the time, Pallas kernels for 13%

profile of v5, /device:TPU:0, one launch (start us, length us, event | category | flops | bytes accessed | tf_op | source)
XLA Modules:
  0.0 574.3 jit_solution(14447438432221949632)
XLA Ops:
  25.2 7.9 %collective-permute-done.1.refs_2_ = bf16[144,768]{1,0:T(8,128)(2,1)S(1)} collective-permute-done((bf16[144,768]{1,0:T(8,128)(2,1)}, bf16[144,768]{1,0:T(8,128)(2,1)S(1)}, u32[]{:S(2)}, u32[]{:S(2)}) %collective-permute-start.1) | collective-permute-done | bytes 221216 | tf_op jit(solution)/shard_map/ppermute | solution.py:645
  44.8 14.2 %collective-permute-done.4.refs_5_ = bf16[432,768]{1,0:T(8,128)(2,1)S(1)} collective-permute-done((bf16[432,768]{1,0:T(8,128)(2,1)S(1)}, bf16[432,768]{1,0:T(8,128)(2,1)S(1)}, u32[]{:S(2)}, u32[]{:S(2)}) %collective-permute-start.4) | collective-permute-done | bytes 663584 | tf_op jit(solution)/shard_map/ppermute | solution.py:645
  74.2 22.7 %collective-permute-start.8 = (bf16[128,1024]{1,0:T(8,128)(2,1)S(1)}, bf16[128,1024]{1,0:T(8,128)(2,1)S(1)}, u32[]{:S(2)}, u32[]{:S(2)}) collective-permute-start(bf16[128,1024]{1,0:T(8,128)(2,1)S(1)} %get-tuple-element.103.refs_5_), channel_id=1, source_target_pairs={{0,4},{4,0},{8,12},{12,8},{1,5},{5,1},{9,13},{13,9},{2,6},{6,2},{1... | collective-permute-start | bytes 786440 | tf_op jit(solution)/shard_map/ppermute | solution.py:645
  97.0 11.3 %collective-permute-done.8.refs_6_ = bf16[128,1024]{1,0:T(8,128)(2,1)S(1)} collective-permute-done((bf16[128,1024]{1,0:T(8,128)(2,1)S(1)}, bf16[128,1024]{1,0:T(8,128)(2,1)S(1)}, u32[]{:S(2)}, u32[]{:S(2)}) %collective-permute-start.8) | collective-permute-done | bytes 262176 | tf_op jit(solution)/shard_map/ppermute | solution.py:645
  110.4 14.3 %all-to-all-done.qkv_ref = bf16[4,192,512]{2,1,0:T(8,128)(2,1)} async-done(((bf16[4,192,512]{2,1,0:T(8,128)(2,1)}), bf16[4,192,512]{2,1,0:T(8,128)(2,1)}, u32[]{:S(2)}, u32[]{:S(2)}) %all-to-all-start) | async-done | bytes 786464 | tf_op jit(solution)/shard_map/all_to_all | solution.py:651
  134.8 6.1 %all-to-all-done.1.o_ref.refs_2_ = bf16[4,64,512]{2,1,0:T(8,128)(2,1)S(1)} async-done(((bf16[4,64,512]{2,1,0:T(8,128)(2,1)}), bf16[4,64,512]{2,1,0:T(8,128)(2,1)S(1)}, u32[]{:S(2)}, u32[]{:S(2)}) %all-to-all-start.1) | async-done | bytes 262176 | tf_op jit(solution)/shard_map/all_to_all | solution.py:651
  152.0 10.1 %collective-permute-done.12.b_ref = bf16[256,1024]{1,0:T(8,128)(2,1)S(1)} collective-permute-done((bf16[256,1024]{1,0:T(8,128)(2,1)S(1)}, bf16[256,1024]{1,0:T(8,128)(2,1)S(1)}, u32[]{:S(2)}, u32[]{:S(2)}) %collective-permute-start.12) | collective-permute-done | bytes 524320 | tf_op jit(solution)/shard_map/ppermute | solution.py:645
  162.8 18.6 %collective-permute-done.14.refs_8_ = bf16[512,1024]{1,0:T(8,128)(2,1)S(1)} collective-permute-done((bf16[512,1024]{1,0:T(8,128)(2,1)S(1)}, bf16[512,1024]{1,0:T(8,128)(2,1)S(1)}, u32[]{:S(2)}, u32[]{:S(2)}) %collective-permute-start.14) | collective-permute-done | bytes 1048608 | tf_op jit(solution)/shard_map/ppermute | solution.py:645
  189.3 13.5 %collective-permute-done.16.b_ref = bf16[256,1024]{1,0:T(8,128)(2,1)S(1)} collective-permute-done((bf16[256,1024]{1,0:T(8,128)(2,1)S(1)}, bf16[256,1024]{1,0:T(8,128)(2,1)S(1)}, u32[]{:S(2)}, u32[]{:S(2)}) %collective-permute-start.16) | collective-permute-done | bytes 524320 | tf_op jit(solution)/shard_map/ppermute | solution.py:645
  207.7 30.0 %all_to_all.55.qkv_ref = bf16[4,192,512]{2,1,0:T(8,128)(2,1)S(1)} all-to-all(bf16[4,192,512]{2,1,0:T(8,128)(2,1)S(1)} %shard_map.203), channel_id=1, replica_groups=mesh['fsdp'=2,'ctx'=4,'tp'=4] {'ctx'}, dimensions={0} | all-to-all | bytes 1572864 | tf_op jit(solution)/shard_map/all_to_all | solution.py:651
  242.6 12.0 %all_to_all.56.o_ref.refs_2_ = bf16[4,64,512]{2,1,0:T(8,128)(2,1)S(1)} all-to-all(bf16[4,64,512]{2,1,0:T(8,128)(2,1)S(1)} %get-tuple-element.113), channel_id=1, replica_groups=mesh['fsdp'=2,'ctx'=4,'tp'=4] {'ctx'}, dimensions={0} | all-to-all | bytes 524288 | tf_op jit(solution)/shard_map/all_to_all | solution.py:651
  259.2 12.5 %collective-permute-done.19.b_ref = bf16[256,1024]{1,0:T(8,128)(2,1)S(1)} collective-permute-done((bf16[256,1024]{1,0:T(8,128)(2,1)S(1)}, bf16[256,1024]{1,0:T(8,128)(2,1)S(1)}, u32[]{:S(2)}, u32[]{:S(2)}) %collective-permute-start.19) | collective-permute-done | bytes 524320 | tf_op jit(solution)/shard_map/ppermute | solution.py:645
  300.4 11.7 %collective-permute-done.22.b_ref = bf16[256,1024]{1,0:T(8,128)(2,1)S(1)} collective-permute-done((bf16[256,1024]{1,0:T(8,128)(2,1)}, bf16[256,1024]{1,0:T(8,128)(2,1)S(1)}, u32[]{:S(2)}, u32[]{:S(2)}) %collective-permute-start.22) | collective-permute-done | bytes 524320 | tf_op jit(solution)/shard_map/ppermute | solution.py:645
  317.3 19.7 %all_to_all.57.g_ref = bf16[4,64,512]{2,1,0:T(8,128)(2,1)S(1)} all-to-all(bf16[4,64,512]{2,1,0:T(8,128)(2,1)S(1)} %shard_map.213), channel_id=1, replica_groups=mesh['fsdp'=2,'ctx'=4,'tp'=4] {'ctx'}, dimensions={0} | all-to-all | bytes 524288 | tf_op jit(solution)/shard_map/all_to_all | solution.py:651
  337.0 6.0 %shard_map.215 = bf16[4,192,512]{2,1,0:T(8,128)(2,1)S(1)} custom-call(s32[16]{0:T(128)S(1)} %select_reduce_fusion.src_ref, f32[1]{0:T(128)} %bitcast.10.slope_ref, s32[1,2048]{1,0:T(1,128)S(1)} %copy-done.114, bf16[4,192,512]{2,1,0:T(8,128)(2,1)S(1)} %copy-done.73, bf16[4,64,512]{2,1,0:T(8,128)(2,1)S(1)} %all_to_all.57.g_ref, f32[1,2048]{1,0:T(1,128)S(1)} %copy-done.120), custom_call_target="tpu_custom_call" | custom-call | flops 939524096 | bytes 2097152 | tf_op jit(solution)/shard_map/pallas_call | solution.py:577
  343.0 22.4 %all_to_all.58.g_ref = bf16[4,192,512]{2,1,0:T(8,128)(2,1)S(1)} all-to-all(bf16[4,192,512]{2,1,0:T(8,128)(2,1)S(1)} %shard_map.215), channel_id=1, replica_groups=mesh['fsdp'=2,'ctx'=4,'tp'=4] {'ctx'}, dimensions={0} | all-to-all | bytes 1572864 | tf_op jit(solution)/shard_map/all_to_all | solution.py:651
  374.6 8.6 %collective-permute-done.28.b_ref = bf16[256,1024]{1,0:T(8,128)(2,1)S(1)} collective-permute-done((bf16[256,1024]{1,0:T(8,128)(2,1)S(1)}, bf16[256,1024]{1,0:T(8,128)(2,1)S(1)}, u32[]{:S(2)}, u32[]{:S(2)}) %collective-permute-start.28) | collective-permute-done | bytes 524320 | tf_op jit(solution)/shard_map/ppermute | solution.py:645
  401.8 7.1 %collective-permute-done.31.b_ref = bf16[256,1024]{1,0:T(8,128)(2,1)} collective-permute-done((bf16[256,1024]{1,0:T(8,128)(2,1)}, bf16[256,1024]{1,0:T(8,128)(2,1)}, u32[]{:S(2)}, u32[]{:S(2)}) %collective-permute-start.31) | collective-permute-done | bytes 524320 | tf_op jit(solution)/shard_map/ppermute | solution.py:645
  423.5 13.8 %collective-permute-done.33.refs_0_ = bf16[512,1024]{1,0:T(8,128)(2,1)} collective-permute-done((bf16[512,1024]{1,0:T(8,128)(2,1)}, bf16[512,1024]{1,0:T(8,128)(2,1)}, u32[]{:S(2)}, u32[]{:S(2)}) %collective-permute-start.33) | collective-permute-done | bytes 1048608 | tf_op jit(solution)/shard_map/ppermute | solution.py:645
  440.3 7.5 %shard_map.223 = bf16[4,192,512]{2,1,0:T(8,128)(2,1)} custom-call(s32[16]{0:T(128)S(1)} %select_reduce_fusion.src_ref, f32[1]{0:T(128)} %bitcast.10.slope_ref, s32[1,2048]{1,0:T(1,128)S(1)} %copy-done.114, bf16[4,192,512]{2,1,0:T(8,128)(2,1)} %all-to-all-done.qkv_ref, bf16[4,64,512]{2,1,0:T(8,128)(2,1)S(1)} %all-to-all-done.6.g_ref, f32[1,2048]{1,0:T(1,128)S(1)} %copy-done.118), custom_call_target="tpu_custom_call" | custom-call | flops 939524096 | bytes 2097152 | tf_op jit(solution)/shard_map/pallas_call | solution.py:577
  455.5 17.4 %all-to-all-done.7.g_ref = bf16[4,192,512]{2,1,0:T(8,128)(2,1)} async-done(((bf16[4,192,512]{2,1,0:T(8,128)(2,1)}), bf16[4,192,512]{2,1,0:T(8,128)(2,1)}, u32[]{:S(2)}, u32[]{:S(2)}) %all-to-all-start.7) | async-done | bytes 786464 | tf_op jit(solution)/shard_map/all_to_all | solution.py:651
  490.7 6.9 %collective-permute-done.35.b_ref = bf16[256,1024]{1,0:T(8,128)(2,1)S(1)} collective-permute-done((bf16[256,1024]{1,0:T(8,128)(2,1)S(1)}, bf16[256,1024]{1,0:T(8,128)(2,1)S(1)}, u32[]{:S(2)}, u32[]{:S(2)}) %collective-permute-start.35) | collective-permute-done | bytes 524320 | tf_op jit(solution)/shard_map/ppermute | solution.py:645
  506.2 13.7 %all-to-all-done.8.refs_1_ = bf16[4,144,1024]{2,1,0:T(8,128)(2,1)S(1)} async-done(((bf16[4,144,1024]{2,1,0:T(8,128)(2,1)}), bf16[4,144,1024]{2,1,0:T(8,128)(2,1)S(1)}, u32[]{:S(2)}, u32[]{:S(2)}) %all-to-all-start.8) | async-done | bytes 1179680 | tf_op jit(solution)/shard_map/all_to_all | solution.py:651
  525.7 15.8 %all-to-all-done.9.refs_2_ = bf16[4,144,512]{2,1,0:T(8,128)(2,1)S(1)} async-done(((bf16[4,144,512]{2,1,0:T(8,128)(2,1)}), bf16[4,144,512]{2,1,0:T(8,128)(2,1)S(1)}, u32[]{:S(2)}, u32[]{:S(2)}) %all-to-all-start.9) | async-done | bytes 589856 | tf_op jit(solution)/shard_map/all_to_all | solution.py:651
  (486 shorter events, 234.8 us)
Async XLA Ops:
  7.2 137.2 %all-gather.3.cloned.1.call-start = ((), (), s32[]{:S(2)}) async-start(), calls=%async_computation.13 | async-start | bytes 2359296 | tf_op jit(solution)/shard_map/all_gather | solution.py:677
  14.2 18.9 %collective-permute-start.1 = (bf16[144,768]{1,0:T(8,128)(2,1)}, bf16[144,768]{1,0:T(8,128)(2,1)S(1)}, u32[]{:S(2)}, u32[]{:S(2)}) collective-permute-start(bf16[144,768]{1,0:T(8,128)(2,1)} %fusion.7.refs_0_), channel_id=1, source_target_pairs={{0,8},{4,12},{8,0},{12,4},{1,9},{5,13},{9,1},{13,5},{2,10},{6,14},... | collective-permute-start | bytes 663560 | tf_op jit(solution)/shard_map/ppermute | solution.py:645
  16.8 24.4 %collective-permute-start.3 = (bf16[144,768]{1,0:T(8,128)(2,1)}, bf16[144,768]{1,0:T(8,128)(2,1)}, u32[]{:S(2)}, u32[]{:S(2)}) collective-permute-start(bf16[144,768]{1,0:T(8,128)(2,1)} %fusion.7.refs_0_), channel_id=1, source_target_pairs={{0,16},{16,0},{1,17},{17,1},{2,18},{18,2},{3,19},{19,3},{4,20},{20... | collective-permute-start | bytes 663560 | tf_op jit(solution)/shard_map/ppermute | solution.py:645
  33.8 36.2 %collective-permute-start.5 = (bf16[128,1280]{1,0:T(8,128)(2,1)S(1)}, bf16[128,1280]{1,0:T(8,128)(2,1)S(1)}, u32[]{:S(2)}, u32[]{:S(2)}) collective-permute-start(bf16[128,1280]{1,0:T(8,128)(2,1)S(1)} %pad_maximum_fusion.5.refs_0_), channel_id=1, source_target_pairs={{0,4},{4,0},{8,12},{12,8},{1,5},{5,1},{9,13},{13,9},{2,6},{6,2},{1... | collective-permute-start | bytes 983048 | tf_op jit(solution)/shard_map/ppermute | solution.py:645
  37.2 32.8 %collective-permute-start.6 = (bf16[128,1280]{1,0:T(8,128)(2,1)S(1)}, bf16[128,1280]{1,0:T(8,128)(2,1)S(1)}, u32[]{:S(2)}, u32[]{:S(2)}) collective-permute-start(bf16[128,1280]{1,0:T(8,128)(2,1)S(1)} %pad_maximum_fusion.5.refs_0_), channel_id=1, source_target_pairs={{0,8},{4,12},{8,0},{12,4},{1,9},{5,13},{9,1},{13,5},{2,10},{6,14},... | collective-permute-start | bytes 983048 | tf_op jit(solution)/shard_map/ppermute | solution.py:645
  38.7 31.4 %collective-permute-start.7 = (bf16[128,1280]{1,0:T(8,128)(2,1)S(1)}, bf16[128,1280]{1,0:T(8,128)(2,1)S(1)}, u32[]{:S(2)}, u32[]{:S(2)}) collective-permute-start(bf16[128,1280]{1,0:T(8,128)(2,1)S(1)} %pad_maximum_fusion.5.refs_0_), channel_id=1, source_target_pairs={{0,12},{4,8},{8,4},{12,0},{1,13},{5,9},{9,5},{13,1},{2,14},{6,10},... | collective-permute-start | bytes 983048 | tf_op jit(solution)/shard_map/ppermute | solution.py:645
  65.8 58.9 %all-to-all-start = ((bf16[4,192,512]{2,1,0:T(8,128)(2,1)}), bf16[4,192,512]{2,1,0:T(8,128)(2,1)}, u32[]{:S(2)}, u32[]{:S(2)}) async-start(bf16[4,192,512]{2,1,0:T(8,128)(2,1)} %copy-done.74), calls=%async_computation | async-start | bytes 1572864 | tf_op jit(solution)/shard_map/all_to_all | solution.py:651
  72.0 69.0 %collective-permute-start.10 = (bf16[512,1280]{1,0:T(8,128)(2,1)}, bf16[512,1280]{1,0:T(8,128)(2,1)S(1)}, u32[]{:S(2)}, u32[]{:S(2)}) collective-permute-start(bf16[512,1280]{1,0:T(8,128)(2,1)} %pad_maximum_fusion), channel_id=1, source_target_pairs={{0,16},{16,0},{1,17},{17,1},{2,18},{18,2},{3,19},{19,3},{4,20},{20... | collective-permute-start | bytes 3932168 | tf_op jit(solution)/shard_map/ppermute | solution.py:645
  74.2 34.1 %collective-permute-start.8 = (bf16[128,1024]{1,0:T(8,128)(2,1)S(1)}, bf16[128,1024]{1,0:T(8,128)(2,1)S(1)}, u32[]{:S(2)}, u32[]{:S(2)}) collective-permute-start(bf16[128,1024]{1,0:T(8,128)(2,1)S(1)} %get-tuple-element.103.refs_5_), channel_id=1, source_target_pairs={{0,4},{4,0},{8,12},{12,8},{1,5},{5,1},{9,13},{13,9},{2,6},{6,2},{1... | collective-permute-start | bytes 786440 | tf_op jit(solution)/shard_map/ppermute | solution.py:645
  109.9 24.9 %collective-permute-start.9 = (bf16[256,1024]{1,0:T(8,128)(2,1)}, bf16[256,1024]{1,0:T(8,128)(2,1)}, u32[]{:S(2)}, u32[]{:S(2)}) collective-permute-start(bf16[256,1024]{1,0:T(8,128)(2,1)} %pad_maximum_fusion.3), channel_id=1, source_target_pairs={{0,8},{4,12},{8,0},{12,4},{1,9},{5,13},{9,1},{13,5},{2,10},{6,14},... | collective-permute-start | bytes 1572872 | tf_op jit(solution)/shard_map/ppermute | solution.py:645
  134.1 142.3 %all-gather.5.cloned.1.call-start = ((), (), s32[]{:S(2)}) async-start(), calls=%async_computation.14 | async-start | bytes 4718592 | tf_op jit(solution)/shard_map/all_gather | solution.py:677
  144.5 256.7 %reduce-scatter.3.cloned.1.call-start = ((), (), s32[]{:S(2)}) async-start(), calls=%async_computation.15 | async-start | bytes 4718592 | tf_op jit(solution)/shard_map/reduce_scatter | solution.py:680
  150.5 31.0 %collective-permute-start.14 = (bf16[512,1024]{1,0:T(8,128)(2,1)S(1)}, bf16[512,1024]{1,0:T(8,128)(2,1)S(1)}, u32[]{:S(2)}, u32[]{:S(2)}) collective-permute-start(bf16[512,1024]{1,0:T(8,128)(2,1)S(1)} %pad_maximum_fusion.1), channel_id=1, source_target_pairs={{0,16},{16,0},{1,17},{17,1},{2,18},{18,2},{3,19},{19,3},{4,20},{20... | collective-permute-start | bytes 3145736 | tf_op jit(solution)/shard_map/ppermute | solution.py:645
  297.6 243.9 %reduce-scatter.5.cloned.1.call-start = ((), (), s32[]{:S(2)}) async-start(), calls=%async_computation.16 | async-start | bytes 4718592 | tf_op jit(solution)/shard_map/reduce_scatter | solution.py:680
  401.2 36.2 %collective-permute-start.33 = (bf16[512,1024]{1,0:T(8,128)(2,1)}, bf16[512,1024]{1,0:T(8,128)(2,1)}, u32[]{:S(2)}, u32[]{:S(2)}) collective-permute-start(bf16[512,1024]{1,0:T(8,128)(2,1)} %copy-done.111), channel_id=1, source_target_pairs={{0,16},{16,0},{1,17},{17,1},{2,18},{18,2},{3,19},{19,3},{4,20},{20... | collective-permute-start | bytes 3145736 | tf_op jit(solution)/shard_map/ppermute | solution.py:645
  419.9 20.4 %all-to-all-start.6 = ((bf16[4,64,512]{2,1,0:T(8,128)(2,1)}), bf16[4,64,512]{2,1,0:T(8,128)(2,1)S(1)}, u32[]{:S(2)}, u32[]{:S(2)}) async-start(bf16[4,64,512]{2,1,0:T(8,128)(2,1)} %shard_map.222), calls=%async_computation.6 | async-start | bytes 524288 | tf_op jit(solution)/shard_map/all_to_all | solution.py:651
  447.8 25.0 %all-to-all-start.7 = ((bf16[4,192,512]{2,1,0:T(8,128)(2,1)}), bf16[4,192,512]{2,1,0:T(8,128)(2,1)}, u32[]{:S(2)}, u32[]{:S(2)}) async-start(bf16[4,192,512]{2,1,0:T(8,128)(2,1)} %shard_map.223), calls=%async_computation.7 | async-start | bytes 1572864 | tf_op jit(solution)/shard_map/all_to_all | solution.py:651
  452.7 48.6 %collective-permute-start.24 = (bf16[256,1024]{1,0:T(8,128)(2,1)}, bf16[256,1024]{1,0:T(8,128)(2,1)}, u32[]{:S(2)}, u32[]{:S(2)}) collective-permute-start(bf16[256,1024]{1,0:T(8,128)(2,1)} %copy-done.112), channel_id=1, source_target_pairs={{0,1},{1,0},{2,3},{3,2},{4,5},{5,4},{6,7},{7,6},{8,9},{9,8},{10,11... | collective-permute-start | bytes 1572872 | tf_op jit(solution)/shard_map/ppermute | solution.py:645
  477.9 42.1 %all-to-all-start.8 = ((bf16[4,144,1024]{2,1,0:T(8,128)(2,1)}), bf16[4,144,1024]{2,1,0:T(8,128)(2,1)S(1)}, u32[]{:S(2)}, u32[]{:S(2)}) async-start(bf16[4,144,1024]{2,1,0:T(8,128)(2,1)} %shard_map.224), calls=%async_computation.8 | async-start | bytes 2359296 | tf_op jit(solution)/shard_map/all_to_all | solution.py:651
  503.3 45.8 %collective-permute-start.25 = (bf16[256,1024]{1,0:T(8,128)(2,1)}, bf16[256,1024]{1,0:T(8,128)(2,1)}, u32[]{:S(2)}, u32[]{:S(2)}) collective-permute-start(bf16[256,1024]{1,0:T(8,128)(2,1)} %add_convert_fusion.4), channel_id=1, source_target_pairs={{0,2},{1,3},{2,0},{3,1},{4,6},{5,7},{6,4},{7,5},{8,10},{9,11},{10,... | collective-permute-start | bytes 1572872 | tf_op jit(solution)/shard_map/ppermute | solution.py:645
  505.6 36.0 %collective-permute-start.39 = (bf16[512,512]{1,0:T(8,128)(2,1)}, bf16[512,512]{1,0:T(8,128)(2,1)}, u32[]{:S(2)}, u32[]{:S(2)}) collective-permute-start(bf16[512,512]{1,0:T(8,128)(2,1)} %get-tuple-element.165), channel_id=1, source_target_pairs={{0,16},{16,0},{1,17},{17,1},{2,18},{18,2},{3,19},{19,3},{4,20},{20... | collective-permute-start | bytes 1572872 | tf_op jit(solution)/shard_map/ppermute | solution.py:645
  506.2 48.1 %collective-permute-start.36 = (f32[256,1024]{1,0:T(8,128)}, f32[256,1024]{1,0:T(8,128)}, u32[]{:S(2)}, u32[]{:S(2)}) collective-permute-start(f32[256,1024]{1,0:T(8,128)} %get-tuple-element.167.own_ref), channel_id=1, source_target_pairs={{0,1},{1,0},{2,3},{3,2},{4,5},{5,4},{6,7},{7,6},{8,9},{9,8},{10,11... | collective-permute-start | bytes 3145736 | tf_op jit(solution)/shard_map/ppermute | solution.py:645
  521.5 20.0 %all-to-all-start.9 = ((bf16[4,144,512]{2,1,0:T(8,128)(2,1)}), bf16[4,144,512]{2,1,0:T(8,128)(2,1)S(1)}, u32[]{:S(2)}, u32[]{:S(2)}) async-start(bf16[4,144,512]{2,1,0:T(8,128)(2,1)} %copy-done.36), calls=%async_computation.9 | async-start | bytes 1179648 | tf_op jit(solution)/shard_map/all_to_all | solution.py:651
  544.8 18.9 %all-to-all-start.10 = ((bf16[4,144,512]{2,1,0:T(8,128)(2,1)}), bf16[4,144,512]{2,1,0:T(8,128)(2,1)S(1)}, u32[]{:S(2)}, u32[]{:S(2)}) async-start(bf16[4,144,512]{2,1,0:T(8,128)(2,1)} %copy-done.35), calls=%async_computation.12 | async-start | bytes 1179648 | tf_op jit(solution)/shard_map/all_to_all | solution.py:651
  (162 other events, 2457.3 us)
Sparse Core Ops, SparseCore 0:
  33.3 83.0 all-gather.2
  144.6 85.3 all-gather.4
  297.7 91.2 reduce-scatter.2
  401.3 104.9 reduce-scatter.4

commit v6 on v5

--- a/solution.py
+++ b/solution.py
@@ -350,11 +350,42 @@
     )
 
 
+def part_pieces_kernel(own_ref, small_ref, *refs):
+    slots, extra, _ = small_ref.shape
+    came, outs = refs[:-slots], refs[-slots:]
+    depth = own_ref.shape[0] // slots
+    for number, out_ref in enumerate(outs):
+        rows = slice(number * depth, (number + 1) * depth)
+        total = own_ref[rows, :].astype(F32)
+        for ref in came:
+            total = total + ref[rows, :].astype(F32)
+        out_ref[:depth, :] = total.astype(BF)
+        out_ref[depth:, :] = small_ref[number].astype(BF)
+
+
+def part_pieces(own, small, came):
+    rows, cols = own.shape
+    slots, extra, _ = small.shape
+    return call(
+        part_pieces_kernel,
+        [shaped((rows // slots + extra, cols), BF)] * slots,
+        [own, small, *came],
+        rows * cols * 2,
+    )
+
+
 def final_kernel(plans, *refs):
     outs = refs[-len(plans) :]
     for out_ref, plan in zip(outs, plans):
         cols = out_ref.shape[-1]
         for index, which, col in plan:
+            if isinstance(which, tuple):
+                rows = slice(0, out_ref.shape[-2])
+                total = refs[which[0]][rows, col : col + cols].astype(F32)
+                for other in which[1:]:
+                    total = total + refs[other][rows, col : col + cols].astype(F32)
+                out_ref[index] = total
+                continue
             ref = refs[which]
             if len(ref.shape) == 2:
                 out_ref[index] = ref[: out_ref.shape[-2], col : col + cols].astype(F32)
@@ -898,9 +929,9 @@
     nothing = jnp.zeros((nc, 16, cols), F32)
     out_q_sums = part_sum(order, tie(out_q[0], above), nothing, out_q_came)
     out_q_pieces = across(out_q_sums)
-    last_sums = part_sum(order, tie(last_parts[0], out_q_pieces, late[0]), small, last_came)
-    last_pieces = across(last_sums)
-    small = jnp.sum(last_pieces[:, depth:, :].astype(F32), axis=0).reshape(-1)
+    last_sums = part_pieces(tie(last_parts[0], out_q_sums, late[0]), small, last_came)
+    last_pieces = [last_sums[0]] + [swap(last_sums[bit], "ctx", nc, bit) for bit in range(1, nc)]
+    small = sum(piece[depth:, :].astype(F32) for piece in last_pieces).reshape(-1)
     norm_mine = small[: count * depth].reshape(count, depth)
     bias_sum = small[count * depth : held]
     grad_up, grad_down = final_sums(
@@ -908,12 +939,13 @@
         [shaped((LAYERS, depth, hidden), F32)] * 2,
         late,
     )
-    qkv_plan = [((1, i), 1, (i + 1) * local) for i in range(3)]
-    qkv_plan += [((0, 0), 2, local), ((0, 1), 0, 0), ((0, 2), 0, local)]
+    summed = tuple(range(nc))
+    qkv_plan = [((1, i), nc, (i + 1) * local) for i in range(3)]
+    qkv_plan += [((0, 0), nc + 1, local), ((0, 1), summed, 0), ((0, 2), summed, local)]
     grad_out, grad_qkv = final_sums(
-        [[(0, 2, 0), (1, 1, 0)], qkv_plan],
+        [[(0, nc + 1, 0), (1, nc, 0)], qkv_plan],
         [shaped((LAYERS, depth, local), F32), shaped((LAYERS, 3, depth, local), F32)],
-        [last_pieces, above, out_q_pieces],
+        [*last_pieces, above, out_q_pieces],
     )
     grad_qkv = grad_qkv.transpose(0, 2, 1, 3)
 

time: 582 us -> 574 us (0.986)
  waiting for transfers between devices: 230 us -> 220 us
    all_to_all x7 -> x6, waiting for transfers between devices: 75 us -> 51.1 us  [across(): return lax.all_to_all(value, 'ctx', 0, 0)]
    ppermute x41 -> x44, waiting for transfers between devices: 154 us -> 169 us  [swap(): return lax.ppermute(value, axis, [(i, i ^ bit) for i in range(size)])]
    ppermute x41 -> x44, starting transfers between devices: 57.6 us -> 64.4 us  [swap(): return lax.ppermute(value, axis, [(i, i ^ bit) for i in range(size)])]
    all_to_all x7 -> x6, starting transfers between devices: 27 us -> 23.1 us  [across(): return lax.all_to_all(value, 'ctx', 0, 0)]
    unnamed x289 -> x259, local copies, waits for them, and re-layouts: 43.8 us -> 44.3 us
  transfers between devices with their start and end apart: 52 -> 54, of which waited for: 30 -> 31; matrix products, arithmetic and copies ran while one was open for 4% -> 4% of each run, Pallas kernels for 13% -> 14%
where the time goes in v6:
time: 574 us; the launch traced here: 566 us
  waiting for transfers between devices  220 us (38%)
  Pallas kernels  88 us (15%)
  starting transfers between devices  87.8 us (15%)
  blocking collectives  84 us (15%)
  local copies, waits for them, and re-layouts  52.4 us (9%)
  other arithmetic  18.4 us (3%)
  between operations  15.6 us (3%)
    ppermute x44, waiting for transfers between devices, swap(): return lax.ppermute(value, axis, [(i, i ^ bit) for i in range(size)])  169 us
    all_to_all x4, blocking collectives, across(): return lax.all_to_all(value, 'ctx', 0, 0)  84 us
    pallas_call x35, Pallas kernels, call(): pl.pallas_call(kernel, in_specs=specs, out_specs=[whole()] * len(outs) if...  66 us
    ppermute x44, starting transfers between devices, swap(): return lax.ppermute(value, axis, [(i, i ^ bit) for i in range(size)])  64.4 us
    all_to_all x6, waiting for transfers between devices, across(): return lax.all_to_all(value, 'ctx', 0, 0)  51.1 us
    unnamed x259, local copies, waits for them, and re-layouts  44.3 us
    all_to_all x6, starting transfers between devices, across(): return lax.all_to_all(value, 'ctx', 0, 0)  23.1 us
    pallas_call x2, Pallas kernels, attend_backward(): pl.pallas_call(partial(attend_back_kernel, rows // BLK), in_specs=[smem,...  12.7 us
  transfers between devices with their start and end apart: 54, of which 31 were waited for; matrix products, arithmetic and copies ran while one was open for 4% of the time, Pallas kernels for 14%

profile of v6, /device:TPU:0, one launch (start us, length us, event | category | flops | bytes accessed | tf_op | source)
XLA Modules:
  0.0 565.9 jit_solution(6070545731597701182)
XLA Ops:
  23.9 8.5 %collective-permute-done.1.refs_2_ = bf16[144,768]{1,0:T(8,128)(2,1)S(1)} collective-permute-done((bf16[144,768]{1,0:T(8,128)(2,1)}, bf16[144,768]{1,0:T(8,128)(2,1)S(1)}, u32[]{:S(2)}, u32[]{:S(2)}) %collective-permute-start.1) | collective-permute-done | bytes 221216 | tf_op jit(solution)/shard_map/ppermute | solution.py:676
  43.9 14.2 %collective-permute-done.4.refs_5_ = bf16[432,768]{1,0:T(8,128)(2,1)S(1)} collective-permute-done((bf16[432,768]{1,0:T(8,128)(2,1)S(1)}, bf16[432,768]{1,0:T(8,128)(2,1)S(1)}, u32[]{:S(2)}, u32[]{:S(2)}) %collective-permute-start.4) | collective-permute-done | bytes 663584 | tf_op jit(solution)/shard_map/ppermute | solution.py:676
  72.4 24.1 %collective-permute-start.8 = (bf16[128,1024]{1,0:T(8,128)(2,1)S(1)}, bf16[128,1024]{1,0:T(8,128)(2,1)S(1)}, u32[]{:S(2)}, u32[]{:S(2)}) collective-permute-start(bf16[128,1024]{1,0:T(8,128)(2,1)S(1)} %get-tuple-element.107.refs_5_), channel_id=1, source_target_pairs={{0,4},{4,0},{8,12},{12,8},{1,5},{5,1},{9,13},{13,9},{2,6},{6,2},{1... | collective-permute-start | bytes 786440 | tf_op jit(solution)/shard_map/ppermute | solution.py:676
  96.6 11.1 %collective-permute-done.8.refs_6_ = bf16[128,1024]{1,0:T(8,128)(2,1)S(1)} collective-permute-done((bf16[128,1024]{1,0:T(8,128)(2,1)S(1)}, bf16[128,1024]{1,0:T(8,128)(2,1)S(1)}, u32[]{:S(2)}, u32[]{:S(2)}) %collective-permute-start.8) | collective-permute-done | bytes 262176 | tf_op jit(solution)/shard_map/ppermute | solution.py:676
  110.5 13.6 %all-to-all-done.qkv_ref = bf16[4,192,512]{2,1,0:T(8,128)(2,1)} async-done(((bf16[4,192,512]{2,1,0:T(8,128)(2,1)}), bf16[4,192,512]{2,1,0:T(8,128)(2,1)}, u32[]{:S(2)}, u32[]{:S(2)}) %all-to-all-start) | async-done | bytes 786464 | tf_op jit(solution)/shard_map/all_to_all | solution.py:682
  134.2 6.2 %all-to-all-done.1.o_ref.refs_2_ = bf16[4,64,512]{2,1,0:T(8,128)(2,1)S(1)} async-done(((bf16[4,64,512]{2,1,0:T(8,128)(2,1)}), bf16[4,64,512]{2,1,0:T(8,128)(2,1)S(1)}, u32[]{:S(2)}, u32[]{:S(2)}) %all-to-all-start.1) | async-done | bytes 262176 | tf_op jit(solution)/shard_map/all_to_all | solution.py:682
  151.5 10.2 %collective-permute-done.12.b_ref = bf16[256,1024]{1,0:T(8,128)(2,1)S(1)} collective-permute-done((bf16[256,1024]{1,0:T(8,128)(2,1)S(1)}, bf16[256,1024]{1,0:T(8,128)(2,1)S(1)}, u32[]{:S(2)}, u32[]{:S(2)}) %collective-permute-start.12) | collective-permute-done | bytes 524320 | tf_op jit(solution)/shard_map/ppermute | solution.py:676
  162.3 18.6 %collective-permute-done.14.refs_8_ = bf16[512,1024]{1,0:T(8,128)(2,1)S(1)} collective-permute-done((bf16[512,1024]{1,0:T(8,128)(2,1)S(1)}, bf16[512,1024]{1,0:T(8,128)(2,1)S(1)}, u32[]{:S(2)}, u32[]{:S(2)}) %collective-permute-start.14) | collective-permute-done | bytes 1048608 | tf_op jit(solution)/shard_map/ppermute | solution.py:676
  188.8 13.4 %collective-permute-done.16.b_ref = bf16[256,1024]{1,0:T(8,128)(2,1)S(1)} collective-permute-done((bf16[256,1024]{1,0:T(8,128)(2,1)S(1)}, bf16[256,1024]{1,0:T(8,128)(2,1)S(1)}, u32[]{:S(2)}, u32[]{:S(2)}) %collective-permute-start.16) | collective-permute-done | bytes 524320 | tf_op jit(solution)/shard_map/ppermute | solution.py:676
  207.1 29.9 %all_to_all.50.qkv_ref = bf16[4,192,512]{2,1,0:T(8,128)(2,1)S(1)} all-to-all(bf16[4,192,512]{2,1,0:T(8,128)(2,1)S(1)} %shard_map.203), channel_id=1, replica_groups=mesh['fsdp'=2,'ctx'=4,'tp'=4] {'ctx'}, dimensions={0} | all-to-all | bytes 1572864 | tf_op jit(solution)/shard_map/all_to_all | solution.py:682
  242.1 12.0 %all_to_all.51.o_ref.refs_2_ = bf16[4,64,512]{2,1,0:T(8,128)(2,1)S(1)} all-to-all(bf16[4,64,512]{2,1,0:T(8,128)(2,1)S(1)} %get-tuple-element.117), channel_id=1, replica_groups=mesh['fsdp'=2,'ctx'=4,'tp'=4] {'ctx'}, dimensions={0} | all-to-all | bytes 524288 | tf_op jit(solution)/shard_map/all_to_all | solution.py:682
  258.7 12.5 %collective-permute-done.19.b_ref = bf16[256,1024]{1,0:T(8,128)(2,1)S(1)} collective-permute-done((bf16[256,1024]{1,0:T(8,128)(2,1)S(1)}, bf16[256,1024]{1,0:T(8,128)(2,1)S(1)}, u32[]{:S(2)}, u32[]{:S(2)}) %collective-permute-start.19) | collective-permute-done | bytes 524320 | tf_op jit(solution)/shard_map/ppermute | solution.py:676
  299.7 11.8 %collective-permute-done.22.b_ref = bf16[256,1024]{1,0:T(8,128)(2,1)S(1)} collective-permute-done((bf16[256,1024]{1,0:T(8,128)(2,1)}, bf16[256,1024]{1,0:T(8,128)(2,1)S(1)}, u32[]{:S(2)}, u32[]{:S(2)}) %collective-permute-start.22) | collective-permute-done | bytes 524320 | tf_op jit(solution)/shard_map/ppermute | solution.py:676
  316.7 19.7 %all_to_all.52.g_ref = bf16[4,64,512]{2,1,0:T(8,128)(2,1)S(1)} all-to-all(bf16[4,64,512]{2,1,0:T(8,128)(2,1)S(1)} %shard_map.213), channel_id=1, replica_groups=mesh['fsdp'=2,'ctx'=4,'tp'=4] {'ctx'}, dimensions={0} | all-to-all | bytes 524288 | tf_op jit(solution)/shard_map/all_to_all | solution.py:682
  336.4 6.0 %shard_map.215 = bf16[4,192,512]{2,1,0:T(8,128)(2,1)S(1)} custom-call(s32[16]{0:T(128)S(1)} %select_reduce_fusion.src_ref, f32[1]{0:T(128)} %bitcast.10.slope_ref, s32[1,2048]{1,0:T(1,128)S(1)} %copy-done.101, bf16[4,192,512]{2,1,0:T(8,128)(2,1)S(1)} %copy-done.66, bf16[4,64,512]{2,1,0:T(8,128)(2,1)S(1)} %all_to_all.52.g_ref, f32[1,2048]{1,0:T(1,128)S(1)} %copy-done.108), custom_call_target="tpu_custom_call" | custom-call | flops 939524096 | bytes 2097152 | tf_op jit(solution)/shard_map/pallas_call | solution.py:608
  342.3 22.3 %all_to_all.53.g_ref = bf16[4,192,512]{2,1,0:T(8,128)(2,1)S(1)} all-to-all(bf16[4,192,512]{2,1,0:T(8,128)(2,1)S(1)} %shard_map.215), channel_id=1, replica_groups=mesh['fsdp'=2,'ctx'=4,'tp'=4] {'ctx'}, dimensions={0} | all-to-all | bytes 1572864 | tf_op jit(solution)/shard_map/all_to_all | solution.py:682
  373.8 8.6 %collective-permute-done.28.b_ref = bf16[256,1024]{1,0:T(8,128)(2,1)S(1)} collective-permute-done((bf16[256,1024]{1,0:T(8,128)(2,1)S(1)}, bf16[256,1024]{1,0:T(8,128)(2,1)S(1)}, u32[]{:S(2)}, u32[]{:S(2)}) %collective-permute-start.28) | collective-permute-done | bytes 524320 | tf_op jit(solution)/shard_map/ppermute | solution.py:676
  401.1 7.1 %collective-permute-done.31.b_ref = bf16[256,1024]{1,0:T(8,128)(2,1)} collective-permute-done((bf16[256,1024]{1,0:T(8,128)(2,1)}, bf16[256,1024]{1,0:T(8,128)(2,1)}, u32[]{:S(2)}, u32[]{:S(2)}) %collective-permute-start.31) | collective-permute-done | bytes 524320 | tf_op jit(solution)/shard_map/ppermute | solution.py:676
  422.8 13.7 %collective-permute-done.33.refs_0_ = bf16[512,1024]{1,0:T(8,128)(2,1)} collective-permute-done((bf16[512,1024]{1,0:T(8,128)(2,1)}, bf16[512,1024]{1,0:T(8,128)(2,1)}, u32[]{:S(2)}, u32[]{:S(2)}) %collective-permute-start.33) | collective-permute-done | bytes 1048608 | tf_op jit(solution)/shard_map/ppermute | solution.py:676
  440.1 6.7 %shard_map.223 = bf16[4,192,512]{2,1,0:T(8,128)(2,1)S(1)} custom-call(s32[16]{0:T(128)S(1)} %select_reduce_fusion.src_ref, f32[1]{0:T(128)} %bitcast.10.slope_ref, s32[1,2048]{1,0:T(1,128)S(1)} %copy-done.102, bf16[4,192,512]{2,1,0:T(8,128)(2,1)} %all-to-all-done.qkv_ref, bf16[4,64,512]{2,1,0:T(8,128)(2,1)S(1)} %all-to-all-done.6.g_ref, ...), custom_call_target="tpu_custom_call" | custom-call | flops 939524096 | bytes 2097152 | tf_op jit(solution)/shard_map/pallas_call | solution.py:608
  459.2 13.6 %all-to-all-done.7.g_ref = bf16[4,192,512]{2,1,0:T(8,128)(2,1)} async-done(((bf16[4,192,512]{2,1,0:T(8,128)(2,1)}), bf16[4,192,512]{2,1,0:T(8,128)(2,1)}, u32[]{:S(2)}, u32[]{:S(2)}) %all-to-all-start.7) | async-done | bytes 786464 | tf_op jit(solution)/shard_map/all_to_all | solution.py:682
  489.9 7.8 %collective-permute-done.35.b_ref = bf16[256,1024]{1,0:T(8,128)(2,1)S(1)} collective-permute-done((bf16[256,1024]{1,0:T(8,128)(2,1)S(1)}, bf16[256,1024]{1,0:T(8,128)(2,1)S(1)}, u32[]{:S(2)}, u32[]{:S(2)}) %collective-permute-start.35) | collective-permute-done | bytes 524320 | tf_op jit(solution)/shard_map/ppermute | solution.py:676
  504.9 14.2 %all-to-all-done.8.refs_4_ = bf16[4,144,1024]{2,1,0:T(8,128)(2,1)S(1)} async-done(((bf16[4,144,1024]{2,1,0:T(8,128)(2,1)}), bf16[4,144,1024]{2,1,0:T(8,128)(2,1)S(1)}, u32[]{:S(2)}, u32[]{:S(2)}) %all-to-all-start.8) | async-done | bytes 1179680 | tf_op jit(solution)/shard_map/all_to_all | solution.py:682
  541.1 10.2 %collective-permute-done.41.refs_2_ = bf16[144,512]{1,0:T(8,128)(2,1)S(1)} collective-permute-done((bf16[144,512]{1,0:T(8,128)(2,1)S(1)}, bf16[144,512]{1,0:T(8,128)(2,1)S(1)}, u32[]{:S(2)}, u32[]{:S(2)}) %collective-permute-start.41) | collective-permute-done | bytes 147488 | tf_op jit(solution)/shard_map/ppermute | solution.py:676
  (460 shorter events, 234.3 us)
Async XLA Ops:
  7.2 136.7 %all-gather.3.cloned.1.call-start = ((), (), s32[]{:S(2)}) async-start(), calls=%async_computation.12 | async-start | bytes 2359296 | tf_op jit(solution)/shard_map/all_gather | solution.py:708
  13.5 18.9 %collective-permute-start.1 = (bf16[144,768]{1,0:T(8,128)(2,1)}, bf16[144,768]{1,0:T(8,128)(2,1)S(1)}, u32[]{:S(2)}, u32[]{:S(2)}) collective-permute-start(bf16[144,768]{1,0:T(8,128)(2,1)} %fusion.7.refs_0_), channel_id=1, source_target_pairs={{0,8},{4,12},{8,0},{12,4},{1,9},{5,13},{9,1},{13,5},{2,10},{6,14},... | collective-permute-start | bytes 663560 | tf_op jit(solution)/shard_map/ppermute | solution.py:676
  16.1 24.1 %collective-permute-start.3 = (bf16[144,768]{1,0:T(8,128)(2,1)}, bf16[144,768]{1,0:T(8,128)(2,1)}, u32[]{:S(2)}, u32[]{:S(2)}) collective-permute-start(bf16[144,768]{1,0:T(8,128)(2,1)} %fusion.7.refs_0_), channel_id=1, source_target_pairs={{0,16},{16,0},{1,17},{17,1},{2,18},{18,2},{3,19},{19,3},{4,20},{20... | collective-permute-start | bytes 663560 | tf_op jit(solution)/shard_map/ppermute | solution.py:676
  32.6 35.6 %collective-permute-start.5 = (bf16[128,1280]{1,0:T(8,128)(2,1)S(1)}, bf16[128,1280]{1,0:T(8,128)(2,1)S(1)}, u32[]{:S(2)}, u32[]{:S(2)}) collective-permute-start(bf16[128,1280]{1,0:T(8,128)(2,1)S(1)} %pad_maximum_fusion.5.refs_0_), channel_id=1, source_target_pairs={{0,4},{4,0},{8,12},{12,8},{1,5},{5,1},{9,13},{13,9},{2,6},{6,2},{1... | collective-permute-start | bytes 983048 | tf_op jit(solution)/shard_map/ppermute | solution.py:676
  36.7 31.6 %collective-permute-start.6 = (bf16[128,1280]{1,0:T(8,128)(2,1)S(1)}, bf16[128,1280]{1,0:T(8,128)(2,1)S(1)}, u32[]{:S(2)}, u32[]{:S(2)}) collective-permute-start(bf16[128,1280]{1,0:T(8,128)(2,1)S(1)} %pad_maximum_fusion.5.refs_0_), channel_id=1, source_target_pairs={{0,8},{4,12},{8,0},{12,4},{1,9},{5,13},{9,1},{13,5},{2,10},{6,14},... | collective-permute-start | bytes 983048 | tf_op jit(solution)/shard_map/ppermute | solution.py:676
  37.7 30.5 %collective-permute-start.7 = (bf16[128,1280]{1,0:T(8,128)(2,1)S(1)}, bf16[128,1280]{1,0:T(8,128)(2,1)S(1)}, u32[]{:S(2)}, u32[]{:S(2)}) collective-permute-start(bf16[128,1280]{1,0:T(8,128)(2,1)S(1)} %pad_maximum_fusion.5.refs_0_), channel_id=1, source_target_pairs={{0,12},{4,8},{8,4},{12,0},{1,13},{5,9},{9,5},{13,1},{2,14},{6,10},... | collective-permute-start | bytes 983048 | tf_op jit(solution)/shard_map/ppermute | solution.py:676
  64.0 60.1 %all-to-all-start = ((bf16[4,192,512]{2,1,0:T(8,128)(2,1)}), bf16[4,192,512]{2,1,0:T(8,128)(2,1)}, u32[]{:S(2)}, u32[]{:S(2)}) async-start(bf16[4,192,512]{2,1,0:T(8,128)(2,1)} %copy-done.67), calls=%async_computation | async-start | bytes 1572864 | tf_op jit(solution)/shard_map/all_to_all | solution.py:682
  70.2 70.2 %collective-permute-start.10 = (bf16[512,1280]{1,0:T(8,128)(2,1)}, bf16[512,1280]{1,0:T(8,128)(2,1)S(1)}, u32[]{:S(2)}, u32[]{:S(2)}) collective-permute-start(bf16[512,1280]{1,0:T(8,128)(2,1)} %pad_maximum_fusion), channel_id=1, source_target_pairs={{0,16},{16,0},{1,17},{17,1},{2,18},{18,2},{3,19},{19,3},{4,20},{20... | collective-permute-start | bytes 3932168 | tf_op jit(solution)/shard_map/ppermute | solution.py:676
  72.4 35.2 %collective-permute-start.8 = (bf16[128,1024]{1,0:T(8,128)(2,1)S(1)}, bf16[128,1024]{1,0:T(8,128)(2,1)S(1)}, u32[]{:S(2)}, u32[]{:S(2)}) collective-permute-start(bf16[128,1024]{1,0:T(8,128)(2,1)S(1)} %get-tuple-element.107.refs_5_), channel_id=1, source_target_pairs={{0,4},{4,0},{8,12},{12,8},{1,5},{5,1},{9,13},{13,9},{2,6},{6,2},{1... | collective-permute-start | bytes 786440 | tf_op jit(solution)/shard_map/ppermute | solution.py:676
  109.2 25.0 %collective-permute-start.9 = (bf16[256,1024]{1,0:T(8,128)(2,1)}, bf16[256,1024]{1,0:T(8,128)(2,1)}, u32[]{:S(2)}, u32[]{:S(2)}) collective-permute-start(bf16[256,1024]{1,0:T(8,128)(2,1)} %pad_maximum_fusion.3), channel_id=1, source_target_pairs={{0,8},{4,12},{8,0},{12,4},{1,9},{5,13},{9,1},{13,5},{2,10},{6,14},... | collective-permute-start | bytes 1572872 | tf_op jit(solution)/shard_map/ppermute | solution.py:676
  133.6 142.2 %all-gather.5.cloned.1.call-start = ((), (), s32[]{:S(2)}) async-start(), calls=%async_computation.13 | async-start | bytes 4718592 | tf_op jit(solution)/shard_map/all_gather | solution.py:708
  143.9 256.4 %reduce-scatter.3.cloned.1.call-start = ((), (), s32[]{:S(2)}) async-start(), calls=%async_computation.14 | async-start | bytes 4718592 | tf_op jit(solution)/shard_map/reduce_scatter | solution.py:711
  149.9 31.0 %collective-permute-start.14 = (bf16[512,1024]{1,0:T(8,128)(2,1)S(1)}, bf16[512,1024]{1,0:T(8,128)(2,1)S(1)}, u32[]{:S(2)}, u32[]{:S(2)}) collective-permute-start(bf16[512,1024]{1,0:T(8,128)(2,1)S(1)} %pad_maximum_fusion.1), channel_id=1, source_target_pairs={{0,16},{16,0},{1,17},{17,1},{2,18},{18,2},{3,19},{19,3},{4,20},{20... | collective-permute-start | bytes 3145736 | tf_op jit(solution)/shard_map/ppermute | solution.py:676
  297.0 227.8 %reduce-scatter.5.cloned.1.call-start = ((), (), s32[]{:S(2)}) async-start(), calls=%async_computation.15 | async-start | bytes 4718592 | tf_op jit(solution)/shard_map/reduce_scatter | solution.py:711
  400.4 36.1 %collective-permute-start.33 = (bf16[512,1024]{1,0:T(8,128)(2,1)}, bf16[512,1024]{1,0:T(8,128)(2,1)}, u32[]{:S(2)}, u32[]{:S(2)}) collective-permute-start(bf16[512,1024]{1,0:T(8,128)(2,1)} %copy-done.98), channel_id=1, source_target_pairs={{0,16},{16,0},{1,17},{17,1},{2,18},{18,2},{3,19},{19,3},{4,20},{20... | collective-permute-start | bytes 3145736 | tf_op jit(solution)/shard_map/ppermute | solution.py:676
  419.2 20.9 %all-to-all-start.6 = ((bf16[4,64,512]{2,1,0:T(8,128)(2,1)}), bf16[4,64,512]{2,1,0:T(8,128)(2,1)S(1)}, u32[]{:S(2)}, u32[]{:S(2)}) async-start(bf16[4,64,512]{2,1,0:T(8,128)(2,1)} %shard_map.222), calls=%async_computation.6 | async-start | bytes 524288 | tf_op jit(solution)/shard_map/all_to_all | solution.py:682
  447.6 25.1 %all-to-all-start.7 = ((bf16[4,192,512]{2,1,0:T(8,128)(2,1)}), bf16[4,192,512]{2,1,0:T(8,128)(2,1)}, u32[]{:S(2)}, u32[]{:S(2)}) async-start(bf16[4,192,512]{2,1,0:T(8,128)(2,1)} %copy-done.68), calls=%async_computation.7 | async-start | bytes 1572864 | tf_op jit(solution)/shard_map/all_to_all | solution.py:682
  455.1 45.2 %collective-permute-start.25 = (bf16[256,1024]{1,0:T(8,128)(2,1)}, bf16[256,1024]{1,0:T(8,128)(2,1)}, u32[]{:S(2)}, u32[]{:S(2)}) collective-permute-start(bf16[256,1024]{1,0:T(8,128)(2,1)} %add_convert_fusion.4), channel_id=1, source_target_pairs={{0,2},{1,3},{2,0},{3,1},{4,6},{5,7},{6,4},{7,5},{8,10},{9,11},{10,... | collective-permute-start | bytes 1572872 | tf_op jit(solution)/shard_map/ppermute | solution.py:676
  478.0 41.1 %all-to-all-start.8 = ((bf16[4,144,1024]{2,1,0:T(8,128)(2,1)}), bf16[4,144,1024]{2,1,0:T(8,128)(2,1)S(1)}, u32[]{:S(2)}, u32[]{:S(2)}) async-start(bf16[4,144,1024]{2,1,0:T(8,128)(2,1)} %shard_map.224), calls=%async_computation.8 | async-start | bytes 2359296 | tf_op jit(solution)/shard_map/all_to_all | solution.py:682
  501.8 32.6 %collective-permute-start.26 = (bf16[256,1024]{1,0:T(8,128)(2,1)S(1)}, bf16[256,1024]{1,0:T(8,128)(2,1)}, u32[]{:S(2)}, u32[]{:S(2)}) collective-permute-start(bf16[256,1024]{1,0:T(8,128)(2,1)S(1)} %add_convert_fusion.3.own_ref), channel_id=1, source_target_pairs={{0,1},{1,0},{2,3},{3,2},{4,5},{5,4},{6,7},{7,6},{8,9},{9,8},{10,11... | collective-permute-start | bytes 1572872 | tf_op jit(solution)/shard_map/ppermute | solution.py:676
  503.4 24.3 %collective-permute-start.39 = (bf16[512,512]{1,0:T(8,128)(2,1)}, bf16[512,512]{1,0:T(8,128)(2,1)}, u32[]{:S(2)}, u32[]{:S(2)}) collective-permute-start(bf16[512,512]{1,0:T(8,128)(2,1)} %get-tuple-element.169), channel_id=1, source_target_pairs={{0,16},{16,0},{1,17},{17,1},{2,18},{18,2},{3,19},{19,3},{4,20},{20... | collective-permute-start | bytes 1572872 | tf_op jit(solution)/shard_map/ppermute | solution.py:676
  504.0 32.8 %collective-permute-start.36 = (f32[256,1024]{1,0:T(8,128)S(1)}, f32[256,1024]{1,0:T(8,128)}, u32[]{:S(2)}, u32[]{:S(2)}) collective-permute-start(f32[256,1024]{1,0:T(8,128)S(1)} %get-tuple-element.171.own_ref), channel_id=1, source_target_pairs={{0,1},{1,0},{2,3},{3,2},{4,5},{5,4},{6,7},{7,6},{8,9},{9,8},{10,11... | collective-permute-start | bytes 3145736 | tf_op jit(solution)/shard_map/ppermute | solution.py:676
  521.1 32.8 %all-to-all-start.9 = ((bf16[4,144,512]{2,1,0:T(8,128)(2,1)}), bf16[4,144,512]{2,1,0:T(8,128)(2,1)S(1)}, u32[]{:S(2)}, u32[]{:S(2)}) async-start(bf16[4,144,512]{2,1,0:T(8,128)(2,1)} %shard_map.230), calls=%async_computation.11 | async-start | bytes 1179648 | tf_op jit(solution)/shard_map/all_to_all | solution.py:682
  531.7 19.6 %collective-permute-start.41 = (bf16[144,512]{1,0:T(8,128)(2,1)S(1)}, bf16[144,512]{1,0:T(8,128)(2,1)S(1)}, u32[]{:S(2)}, u32[]{:S(2)}) collective-permute-start(bf16[144,512]{1,0:T(8,128)(2,1)S(1)} %get-tuple-element.186), channel_id=1, source_target_pairs={{0,8},{4,12},{8,0},{12,4},{1,9},{5,13},{9,1},{13,5},{2,10},{6,14},... | collective-permute-start | bytes 442376 | tf_op jit(solution)/shard_map/ppermute | solution.py:676
  (149 other events, 1989.3 us)
Sparse Core Ops, SparseCore 0:
  32.6 83.0 all-gather.2
  144.1 85.3 all-gather.4
  297.1 91.2 reduce-scatter.2
  400.5 104.3 reduce-scatter.4

commit v7 on v6

--- a/solution.py
+++ b/solution.py
@@ -883,11 +883,11 @@
             above_came = send_y(above)
             b = tie(b, *above)
         else:
-            above = across(tie(above_sums, g_proj))
             out_q = attention_grad(0, 2, *sources, tie(g_proj, a), nf)
             out_q_came = send_y(out_q)
             last_parts = attention_grad(2, 4, *sources, tie(g_proj, *out_q), nf)
             last_came = send_y(last_parts)
+            above = across(tie(above_sums, *last_parts))
             b = tie(b, *last_parts)
         gx_half, gz_own, sums_one = norm_backward(gy_half, a, b, x_half, table, row)
         if l > 0:

time: 574 us -> 574 us (level)
    unnamed x259 -> x257, local copies, waits for them, and re-layouts: 44.3 us -> 45.6 us
where the time goes in v7:
time: 574 us; the launch traced here: 566 us
  waiting for transfers between devices  218 us (38%)
  starting transfers between devices  88.6 us (15%)
  Pallas kernels  88.4 us (15%)
  blocking collectives  84 us (15%)
  local copies, waits for them, and re-layouts  53.6 us (9%)
  other arithmetic  17.7 us (3%)
  between operations  15.6 us (3%)
    ppermute x44, waiting for transfers between devices, swap(): return lax.ppermute(value, axis, [(i, i ^ bit) for i in range(size)])  164 us
    all_to_all x4, blocking collectives, across(): return lax.all_to_all(value, 'ctx', 0, 0)  84 us
    pallas_call x35, Pallas kernels, call(): pl.pallas_call(kernel, in_specs=specs, out_specs=[whole()] * len(outs) if...  66.4 us
    ppermute x44, starting transfers between devices, swap(): return lax.ppermute(value, axis, [(i, i ^ bit) for i in range(size)])  65.2 us
    all_to_all x6, waiting for transfers between devices, across(): return lax.all_to_all(value, 'ctx', 0, 0)  53.4 us
    unnamed x257, local copies, waits for them, and re-layouts  45.6 us
    all_to_all x6, starting transfers between devices, across(): return lax.all_to_all(value, 'ctx', 0, 0)  23.1 us
    pallas_call x2, Pallas kernels, attend_backward(): pl.pallas_call(partial(attend_back_kernel, rows // BLK), in_specs=[smem,...  12.7 us
  transfers between devices with their start and end apart: 54, of which 31 were waited for; matrix products, arithmetic and copies ran while one was open for 4% of the time, Pallas kernels for 14%

profile of v7, /device:TPU:0, one launch (start us, length us, event | category | flops | bytes accessed | tf_op | source)
XLA Modules:
  0.0 565.6 jit_solution(9121118171975400570)
XLA Ops:
  23.9 8.5 %collective-permute-done.1.refs_2_ = bf16[144,768]{1,0:T(8,128)(2,1)S(1)} collective-permute-done((bf16[144,768]{1,0:T(8,128)(2,1)}, bf16[144,768]{1,0:T(8,128)(2,1)S(1)}, u32[]{:S(2)}, u32[]{:S(2)}) %collective-permute-start.1) | collective-permute-done | bytes 221216 | tf_op jit(solution)/shard_map/ppermute | solution.py:676
  43.9 14.2 %collective-permute-done.4.refs_5_ = bf16[432,768]{1,0:T(8,128)(2,1)S(1)} collective-permute-done((bf16[432,768]{1,0:T(8,128)(2,1)S(1)}, bf16[432,768]{1,0:T(8,128)(2,1)S(1)}, u32[]{:S(2)}, u32[]{:S(2)}) %collective-permute-start.4) | collective-permute-done | bytes 663584 | tf_op jit(solution)/shard_map/ppermute | solution.py:676
  72.4 24.1 %collective-permute-start.8 = (bf16[128,1024]{1,0:T(8,128)(2,1)S(1)}, bf16[128,1024]{1,0:T(8,128)(2,1)S(1)}, u32[]{:S(2)}, u32[]{:S(2)}) collective-permute-start(bf16[128,1024]{1,0:T(8,128)(2,1)S(1)} %get-tuple-element.107.refs_5_), channel_id=1, source_target_pairs={{0,4},{4,0},{8,12},{12,8},{1,5},{5,1},{9,13},{13,9},{2,6},{6,2},{1... | collective-permute-start | bytes 786440 | tf_op jit(solution)/shard_map/ppermute | solution.py:676
  96.6 11.0 %collective-permute-done.8.refs_6_ = bf16[128,1024]{1,0:T(8,128)(2,1)S(1)} collective-permute-done((bf16[128,1024]{1,0:T(8,128)(2,1)S(1)}, bf16[128,1024]{1,0:T(8,128)(2,1)S(1)}, u32[]{:S(2)}, u32[]{:S(2)}) %collective-permute-start.8) | collective-permute-done | bytes 262176 | tf_op jit(solution)/shard_map/ppermute | solution.py:676
  110.5 13.6 %all-to-all-done.qkv_ref = bf16[4,192,512]{2,1,0:T(8,128)(2,1)} async-done(((bf16[4,192,512]{2,1,0:T(8,128)(2,1)}), bf16[4,192,512]{2,1,0:T(8,128)(2,1)}, u32[]{:S(2)}, u32[]{:S(2)}) %all-to-all-start) | async-done | bytes 786464 | tf_op jit(solution)/shard_map/all_to_all | solution.py:682
  124.2 5.0 shard_map.197
  134.2 6.2 %all-to-all-done.1.o_ref.refs_2_ = bf16[4,64,512]{2,1,0:T(8,128)(2,1)S(1)} async-done(((bf16[4,64,512]{2,1,0:T(8,128)(2,1)}), bf16[4,64,512]{2,1,0:T(8,128)(2,1)S(1)}, u32[]{:S(2)}, u32[]{:S(2)}) %all-to-all-start.1) | async-done | bytes 262176 | tf_op jit(solution)/shard_map/all_to_all | solution.py:682
  151.5 10.2 %collective-permute-done.12.b_ref = bf16[256,1024]{1,0:T(8,128)(2,1)S(1)} collective-permute-done((bf16[256,1024]{1,0:T(8,128)(2,1)S(1)}, bf16[256,1024]{1,0:T(8,128)(2,1)S(1)}, u32[]{:S(2)}, u32[]{:S(2)}) %collective-permute-start.12) | collective-permute-done | bytes 524320 | tf_op jit(solution)/shard_map/ppermute | solution.py:676
  162.3 18.6 %collective-permute-done.14.refs_8_ = bf16[512,1024]{1,0:T(8,128)(2,1)S(1)} collective-permute-done((bf16[512,1024]{1,0:T(8,128)(2,1)S(1)}, bf16[512,1024]{1,0:T(8,128)(2,1)S(1)}, u32[]{:S(2)}, u32[]{:S(2)}) %collective-permute-start.14) | collective-permute-done | bytes 1048608 | tf_op jit(solution)/shard_map/ppermute | solution.py:676
  188.8 13.5 %collective-permute-done.16.b_ref = bf16[256,1024]{1,0:T(8,128)(2,1)S(1)} collective-permute-done((bf16[256,1024]{1,0:T(8,128)(2,1)S(1)}, bf16[256,1024]{1,0:T(8,128)(2,1)S(1)}, u32[]{:S(2)}, u32[]{:S(2)}) %collective-permute-start.16) | collective-permute-done | bytes 524320 | tf_op jit(solution)/shard_map/ppermute | solution.py:676
  207.2 29.9 %all_to_all.50.qkv_ref = bf16[4,192,512]{2,1,0:T(8,128)(2,1)S(1)} all-to-all(bf16[4,192,512]{2,1,0:T(8,128)(2,1)S(1)} %shard_map.203), channel_id=1, replica_groups=mesh['fsdp'=2,'ctx'=4,'tp'=4] {'ctx'}, dimensions={0} | all-to-all | bytes 1572864 | tf_op jit(solution)/shard_map/all_to_all | solution.py:682
  242.1 12.0 %all_to_all.51.o_ref.refs_2_ = bf16[4,64,512]{2,1,0:T(8,128)(2,1)S(1)} all-to-all(bf16[4,64,512]{2,1,0:T(8,128)(2,1)S(1)} %get-tuple-element.117), channel_id=1, replica_groups=mesh['fsdp'=2,'ctx'=4,'tp'=4] {'ctx'}, dimensions={0} | all-to-all | bytes 524288 | tf_op jit(solution)/shard_map/all_to_all | solution.py:682
  258.7 12.5 %collective-permute-done.19.b_ref = bf16[256,1024]{1,0:T(8,128)(2,1)S(1)} collective-permute-done((bf16[256,1024]{1,0:T(8,128)(2,1)S(1)}, bf16[256,1024]{1,0:T(8,128)(2,1)S(1)}, u32[]{:S(2)}, u32[]{:S(2)}) %collective-permute-start.19) | collective-permute-done | bytes 524320 | tf_op jit(solution)/shard_map/ppermute | solution.py:676
  299.8 11.8 %collective-permute-done.22.b_ref = bf16[256,1024]{1,0:T(8,128)(2,1)S(1)} collective-permute-done((bf16[256,1024]{1,0:T(8,128)(2,1)}, bf16[256,1024]{1,0:T(8,128)(2,1)S(1)}, u32[]{:S(2)}, u32[]{:S(2)}) %collective-permute-start.22) | collective-permute-done | bytes 524320 | tf_op jit(solution)/shard_map/ppermute | solution.py:676
  316.7 19.7 %all_to_all.52.g_ref = bf16[4,64,512]{2,1,0:T(8,128)(2,1)S(1)} all-to-all(bf16[4,64,512]{2,1,0:T(8,128)(2,1)S(1)} %shard_map.213), channel_id=1, replica_groups=mesh['fsdp'=2,'ctx'=4,'tp'=4] {'ctx'}, dimensions={0} | all-to-all | bytes 524288 | tf_op jit(solution)/shard_map/all_to_all | solution.py:682
  336.4 6.0 %shard_map.215 = bf16[4,192,512]{2,1,0:T(8,128)(2,1)S(1)} custom-call(s32[16]{0:T(128)S(1)} %select_reduce_fusion.src_ref, f32[1]{0:T(128)} %bitcast.10.slope_ref, s32[1,2048]{1,0:T(1,128)S(1)} %copy-done.100, bf16[4,192,512]{2,1,0:T(8,128)(2,1)S(1)} %copy-done.63, bf16[4,64,512]{2,1,0:T(8,128)(2,1)S(1)} %all_to_all.52.g_ref, f32[1,2048]{1,0:T(1,128)S(1)} %copy-done.107), custom_call_target="tpu_custom_call" | custom-call | flops 939524096 | bytes 2097152 | tf_op jit(solution)/shard_map/pallas_call | solution.py:608
  342.4 22.3 %all_to_all.53.g_ref = bf16[4,192,512]{2,1,0:T(8,128)(2,1)S(1)} all-to-all(bf16[4,192,512]{2,1,0:T(8,128)(2,1)S(1)} %shard_map.215), channel_id=1, replica_groups=mesh['fsdp'=2,'ctx'=4,'tp'=4] {'ctx'}, dimensions={0} | all-to-all | bytes 1572864 | tf_op jit(solution)/shard_map/all_to_all | solution.py:682
  373.8 8.6 %collective-permute-done.28.b_ref = bf16[256,1024]{1,0:T(8,128)(2,1)S(1)} collective-permute-done((bf16[256,1024]{1,0:T(8,128)(2,1)S(1)}, bf16[256,1024]{1,0:T(8,128)(2,1)S(1)}, u32[]{:S(2)}, u32[]{:S(2)}) %collective-permute-start.28) | collective-permute-done | bytes 524320 | tf_op jit(solution)/shard_map/ppermute | solution.py:676
  401.1 7.1 %collective-permute-done.31.b_ref = bf16[256,1024]{1,0:T(8,128)(2,1)} collective-permute-done((bf16[256,1024]{1,0:T(8,128)(2,1)}, bf16[256,1024]{1,0:T(8,128)(2,1)}, u32[]{:S(2)}, u32[]{:S(2)}) %collective-permute-start.31) | collective-permute-done | bytes 524320 | tf_op jit(solution)/shard_map/ppermute | solution.py:676
  422.8 13.6 %collective-permute-done.33.refs_0_ = bf16[512,1024]{1,0:T(8,128)(2,1)} collective-permute-done((bf16[512,1024]{1,0:T(8,128)(2,1)}, bf16[512,1024]{1,0:T(8,128)(2,1)}, u32[]{:S(2)}, u32[]{:S(2)}) %collective-permute-start.33) | collective-permute-done | bytes 1048608 | tf_op jit(solution)/shard_map/ppermute | solution.py:676
  440.1 6.7 %shard_map.223 = bf16[4,192,512]{2,1,0:T(8,128)(2,1)S(1)} custom-call(s32[16]{0:T(128)S(1)} %select_reduce_fusion.src_ref, f32[1]{0:T(128)} %bitcast.10.slope_ref, s32[1,2048]{1,0:T(1,128)S(1)} %copy-done.101, bf16[4,192,512]{2,1,0:T(8,128)(2,1)} %all-to-all-done.qkv_ref, bf16[4,64,512]{2,1,0:T(8,128)(2,1)S(1)} %all-to-all-done.6.g_ref, ...), custom_call_target="tpu_custom_call" | custom-call | flops 939524096 | bytes 2097152 | tf_op jit(solution)/shard_map/pallas_call | solution.py:608
  459.2 13.0 %all-to-all-done.7.g_ref = bf16[4,192,512]{2,1,0:T(8,128)(2,1)} async-done(((bf16[4,192,512]{2,1,0:T(8,128)(2,1)}), bf16[4,192,512]{2,1,0:T(8,128)(2,1)}, u32[]{:S(2)}, u32[]{:S(2)}) %all-to-all-start.7) | async-done | bytes 786464 | tf_op jit(solution)/shard_map/all_to_all | solution.py:682
  502.4 16.9 %all-to-all-done.8.refs_4_ = bf16[4,144,1024]{2,1,0:T(8,128)(2,1)S(1)} async-done(((bf16[4,144,1024]{2,1,0:T(8,128)(2,1)}), bf16[4,144,1024]{2,1,0:T(8,128)(2,1)S(1)}, u32[]{:S(2)}, u32[]{:S(2)}) %all-to-all-start.8) | async-done | bytes 1179680 | tf_op jit(solution)/shard_map/all_to_all | solution.py:682
  539.4 11.5 %collective-permute-done.41.refs_2_ = bf16[144,512]{1,0:T(8,128)(2,1)S(1)} collective-permute-done((bf16[144,512]{1,0:T(8,128)(2,1)S(1)}, bf16[144,512]{1,0:T(8,128)(2,1)S(1)}, u32[]{:S(2)}, u32[]{:S(2)}) %collective-permute-start.41) | collective-permute-done | bytes 147488 | tf_op jit(solution)/shard_map/ppermute | solution.py:676
  (458 shorter events, 233.3 us)
Async XLA Ops:
  7.2 136.7 %all-gather.3.cloned.1.call-start = ((), (), s32[]{:S(2)}) async-start(), calls=%async_computation.12 | async-start | bytes 2359296 | tf_op jit(solution)/shard_map/all_gather | solution.py:708
  16.1 24.1 %collective-permute-start.3 = (bf16[144,768]{1,0:T(8,128)(2,1)}, bf16[144,768]{1,0:T(8,128)(2,1)}, u32[]{:S(2)}, u32[]{:S(2)}) collective-permute-start(bf16[144,768]{1,0:T(8,128)(2,1)} %fusion.7.refs_0_), channel_id=1, source_target_pairs={{0,16},{16,0},{1,17},{17,1},{2,18},{18,2},{3,19},{19,3},{4,20},{20... | collective-permute-start | bytes 663560 | tf_op jit(solution)/shard_map/ppermute | solution.py:676
  32.6 35.6 %collective-permute-start.5 = (bf16[128,1280]{1,0:T(8,128)(2,1)S(1)}, bf16[128,1280]{1,0:T(8,128)(2,1)S(1)}, u32[]{:S(2)}, u32[]{:S(2)}) collective-permute-start(bf16[128,1280]{1,0:T(8,128)(2,1)S(1)} %pad_maximum_fusion.5.refs_0_), channel_id=1, source_target_pairs={{0,4},{4,0},{8,12},{12,8},{1,5},{5,1},{9,13},{13,9},{2,6},{6,2},{1... | collective-permute-start | bytes 983048 | tf_op jit(solution)/shard_map/ppermute | solution.py:676
  36.7 31.6 %collective-permute-start.6 = (bf16[128,1280]{1,0:T(8,128)(2,1)S(1)}, bf16[128,1280]{1,0:T(8,128)(2,1)S(1)}, u32[]{:S(2)}, u32[]{:S(2)}) collective-permute-start(bf16[128,1280]{1,0:T(8,128)(2,1)S(1)} %pad_maximum_fusion.5.refs_0_), channel_id=1, source_target_pairs={{0,8},{4,12},{8,0},{12,4},{1,9},{5,13},{9,1},{13,5},{2,10},{6,14},... | collective-permute-start | bytes 983048 | tf_op jit(solution)/shard_map/ppermute | solution.py:676
  37.7 30.5 %collective-permute-start.7 = (bf16[128,1280]{1,0:T(8,128)(2,1)S(1)}, bf16[128,1280]{1,0:T(8,128)(2,1)S(1)}, u32[]{:S(2)}, u32[]{:S(2)}) collective-permute-start(bf16[128,1280]{1,0:T(8,128)(2,1)S(1)} %pad_maximum_fusion.5.refs_0_), channel_id=1, source_target_pairs={{0,12},{4,8},{8,4},{12,0},{1,13},{5,9},{9,5},{13,1},{2,14},{6,10},... | collective-permute-start | bytes 983048 | tf_op jit(solution)/shard_map/ppermute | solution.py:676
  64.0 60.2 %all-to-all-start = ((bf16[4,192,512]{2,1,0:T(8,128)(2,1)}), bf16[4,192,512]{2,1,0:T(8,128)(2,1)}, u32[]{:S(2)}, u32[]{:S(2)}) async-start(bf16[4,192,512]{2,1,0:T(8,128)(2,1)} %copy-done.64), calls=%async_computation | async-start | bytes 1572864 | tf_op jit(solution)/shard_map/all_to_all | solution.py:682
  70.1 70.3 %collective-permute-start.10 = (bf16[512,1280]{1,0:T(8,128)(2,1)}, bf16[512,1280]{1,0:T(8,128)(2,1)S(1)}, u32[]{:S(2)}, u32[]{:S(2)}) collective-permute-start(bf16[512,1280]{1,0:T(8,128)(2,1)} %pad_maximum_fusion), channel_id=1, source_target_pairs={{0,16},{16,0},{1,17},{17,1},{2,18},{18,2},{3,19},{19,3},{4,20},{20... | collective-permute-start | bytes 3932168 | tf_op jit(solution)/shard_map/ppermute | solution.py:676
  72.4 35.2 %collective-permute-start.8 = (bf16[128,1024]{1,0:T(8,128)(2,1)S(1)}, bf16[128,1024]{1,0:T(8,128)(2,1)S(1)}, u32[]{:S(2)}, u32[]{:S(2)}) collective-permute-start(bf16[128,1024]{1,0:T(8,128)(2,1)S(1)} %get-tuple-element.107.refs_5_), channel_id=1, source_target_pairs={{0,4},{4,0},{8,12},{12,8},{1,5},{5,1},{9,13},{13,9},{2,6},{6,2},{1... | collective-permute-start | bytes 786440 | tf_op jit(solution)/shard_map/ppermute | solution.py:676
  109.1 25.1 %collective-permute-start.9 = (bf16[256,1024]{1,0:T(8,128)(2,1)}, bf16[256,1024]{1,0:T(8,128)(2,1)}, u32[]{:S(2)}, u32[]{:S(2)}) collective-permute-start(bf16[256,1024]{1,0:T(8,128)(2,1)} %pad_maximum_fusion.3), channel_id=1, source_target_pairs={{0,8},{4,12},{8,0},{12,4},{1,9},{5,13},{9,1},{13,5},{2,10},{6,14},... | collective-permute-start | bytes 1572872 | tf_op jit(solution)/shard_map/ppermute | solution.py:676
  133.6 142.2 %all-gather.5.cloned.1.call-start = ((), (), s32[]{:S(2)}) async-start(), calls=%async_computation.13 | async-start | bytes 4718592 | tf_op jit(solution)/shard_map/all_gather | solution.py:708
  144.0 256.4 %reduce-scatter.3.cloned.1.call-start = ((), (), s32[]{:S(2)}) async-start(), calls=%async_computation.14 | async-start | bytes 4718592 | tf_op jit(solution)/shard_map/reduce_scatter | solution.py:711
  150.0 31.0 %collective-permute-start.14 = (bf16[512,1024]{1,0:T(8,128)(2,1)S(1)}, bf16[512,1024]{1,0:T(8,128)(2,1)S(1)}, u32[]{:S(2)}, u32[]{:S(2)}) collective-permute-start(bf16[512,1024]{1,0:T(8,128)(2,1)S(1)} %pad_maximum_fusion.1), channel_id=1, source_target_pairs={{0,16},{16,0},{1,17},{17,1},{2,18},{18,2},{3,19},{19,3},{4,20},{20... | collective-permute-start | bytes 3145736 | tf_op jit(solution)/shard_map/ppermute | solution.py:676
  297.0 228.0 %reduce-scatter.5.cloned.1.call-start = ((), (), s32[]{:S(2)}) async-start(), calls=%async_computation.15 | async-start | bytes 4718592 | tf_op jit(solution)/shard_map/reduce_scatter | solution.py:711
  400.4 36.1 %collective-permute-start.33 = (bf16[512,1024]{1,0:T(8,128)(2,1)}, bf16[512,1024]{1,0:T(8,128)(2,1)}, u32[]{:S(2)}, u32[]{:S(2)}) collective-permute-start(bf16[512,1024]{1,0:T(8,128)(2,1)} %copy-done.97), channel_id=1, source_target_pairs={{0,16},{16,0},{1,17},{17,1},{2,18},{18,2},{3,19},{19,3},{4,20},{20... | collective-permute-start | bytes 3145736 | tf_op jit(solution)/shard_map/ppermute | solution.py:676
  419.2 20.9 %all-to-all-start.6 = ((bf16[4,64,512]{2,1,0:T(8,128)(2,1)}), bf16[4,64,512]{2,1,0:T(8,128)(2,1)S(1)}, u32[]{:S(2)}, u32[]{:S(2)}) async-start(bf16[4,64,512]{2,1,0:T(8,128)(2,1)} %shard_map.222), calls=%async_computation.6 | async-start | bytes 524288 | tf_op jit(solution)/shard_map/all_to_all | solution.py:682
  447.7 24.6 %all-to-all-start.7 = ((bf16[4,192,512]{2,1,0:T(8,128)(2,1)}), bf16[4,192,512]{2,1,0:T(8,128)(2,1)}, u32[]{:S(2)}, u32[]{:S(2)}) async-start(bf16[4,192,512]{2,1,0:T(8,128)(2,1)} %copy-done.65), calls=%async_computation.7 | async-start | bytes 1572864 | tf_op jit(solution)/shard_map/all_to_all | solution.py:682
  455.1 43.6 %collective-permute-start.25 = (bf16[256,1024]{1,0:T(8,128)(2,1)}, bf16[256,1024]{1,0:T(8,128)(2,1)}, u32[]{:S(2)}, u32[]{:S(2)}) collective-permute-start(bf16[256,1024]{1,0:T(8,128)(2,1)} %add_convert_fusion.4), channel_id=1, source_target_pairs={{0,2},{1,3},{2,0},{3,1},{4,6},{5,7},{6,4},{7,5},{8,10},{9,11},{10,... | collective-permute-start | bytes 1572872 | tf_op jit(solution)/shard_map/ppermute | solution.py:676
  486.7 32.7 %all-to-all-start.8 = ((bf16[4,144,1024]{2,1,0:T(8,128)(2,1)}), bf16[4,144,1024]{2,1,0:T(8,128)(2,1)S(1)}, u32[]{:S(2)}, u32[]{:S(2)}) async-start(bf16[4,144,1024]{2,1,0:T(8,128)(2,1)} %shard_map.224), calls=%async_computation.8 | async-start | bytes 2359296 | tf_op jit(solution)/shard_map/all_to_all | solution.py:682
  500.2 32.6 %collective-permute-start.26 = (bf16[256,1024]{1,0:T(8,128)(2,1)S(1)}, bf16[256,1024]{1,0:T(8,128)(2,1)}, u32[]{:S(2)}, u32[]{:S(2)}) collective-permute-start(bf16[256,1024]{1,0:T(8,128)(2,1)S(1)} %add_convert_fusion.3.own_ref), channel_id=1, source_target_pairs={{0,1},{1,0},{2,3},{3,2},{4,5},{5,4},{6,7},{7,6},{8,9},{9,8},{10,11... | collective-permute-start | bytes 1572872 | tf_op jit(solution)/shard_map/ppermute | solution.py:676
  501.5 24.7 %collective-permute-start.39 = (bf16[512,512]{1,0:T(8,128)(2,1)}, bf16[512,512]{1,0:T(8,128)(2,1)}, u32[]{:S(2)}, u32[]{:S(2)}) collective-permute-start(bf16[512,512]{1,0:T(8,128)(2,1)} %get-tuple-element.169), channel_id=1, source_target_pairs={{0,16},{16,0},{1,17},{17,1},{2,18},{18,2},{3,19},{19,3},{4,20},{20... | collective-permute-start | bytes 1572872 | tf_op jit(solution)/shard_map/ppermute | solution.py:676
  502.3 32.8 %collective-permute-start.36 = (f32[256,1024]{1,0:T(8,128)S(1)}, f32[256,1024]{1,0:T(8,128)}, u32[]{:S(2)}, u32[]{:S(2)}) collective-permute-start(f32[256,1024]{1,0:T(8,128)S(1)} %get-tuple-element.171.own_ref), channel_id=1, source_target_pairs={{0,1},{1,0},{2,3},{3,2},{4,5},{5,4},{6,7},{7,6},{8,9},{9,8},{10,11... | collective-permute-start | bytes 3145736 | tf_op jit(solution)/shard_map/ppermute | solution.py:676
  521.4 32.2 %all-to-all-start.9 = ((bf16[4,144,512]{2,1,0:T(8,128)(2,1)}), bf16[4,144,512]{2,1,0:T(8,128)(2,1)S(1)}, u32[]{:S(2)}, u32[]{:S(2)}) async-start(bf16[4,144,512]{2,1,0:T(8,128)(2,1)} %shard_map.230), calls=%async_computation.11 | async-start | bytes 1179648 | tf_op jit(solution)/shard_map/all_to_all | solution.py:682
  529.3 21.7 %collective-permute-start.41 = (bf16[144,512]{1,0:T(8,128)(2,1)S(1)}, bf16[144,512]{1,0:T(8,128)(2,1)S(1)}, u32[]{:S(2)}, u32[]{:S(2)}) collective-permute-start(bf16[144,512]{1,0:T(8,128)(2,1)S(1)} %get-tuple-element.186), channel_id=1, source_target_pairs={{0,8},{4,12},{8,0},{12,4},{1,9},{5,13},{9,1},{13,5},{2,10},{6,14},... | collective-permute-start | bytes 442376 | tf_op jit(solution)/shard_map/ppermute | solution.py:676
  531.6 19.4 %collective-permute-start.42 = (bf16[144,512]{1,0:T(8,128)(2,1)S(1)}, bf16[144,512]{1,0:T(8,128)(2,1)S(1)}, u32[]{:S(2)}, u32[]{:S(2)}) collective-permute-start(bf16[144,512]{1,0:T(8,128)(2,1)S(1)} %get-tuple-element.187), channel_id=1, source_target_pairs={{0,12},{4,8},{8,4},{12,0},{1,13},{5,9},{9,5},{13,1},{2,14},{6,10},... | collective-permute-start | bytes 442376 | tf_op jit(solution)/shard_map/ppermute | solution.py:676
  (148 other events, 2037.6 us)
Sparse Core Ops, SparseCore 0:
  32.6 83.0 all-gather.2
  144.1 85.3 all-gather.4
  297.1 91.2 reduce-scatter.2
  400.5 93.6 reduce-scatter.4
